TPU v7x, 32 devices: a whole 2x2x4 slice. The times are simulated.
32 devices in a mesh: energy: 16 (over z, y, x), slab: 2 (over core).
Axes of the slice: x: 2, y: 2, z: 4, core: 2. Of those that a mesh axis runs over, the one named last changes fastest.
Arguments:
- green_local: bfloat16 [16, 768, 768], P('energy', 'slab'), may hold values from -6 to 6
- coupling: bfloat16 [768, 384], P('slab'), may hold values from -0.3125 to 0.3125
- phonon_coupling: bfloat16 [3, 384, 384], replicated, may hold values from -0.3125 to 0.3125
- offsets: int32 [3], replicated, may hold values from 1 to 4, as said below
- bose_factors: float32 [3], replicated, may hold values from 0.2 to 3
Outputs:
- phonon_sigma: bfloat16 [16, 768, 768], P('energy', 'slab')
- cumulative: float32 [16, 768], P('energy', 'slab')
Inputs may be any that keep to these rules, and one draw needn't show every extreme that they name: The offsets are distinct, and one of them equals 4.
All inputs are finite; a program needn't handle non-finite values.
Results may differ from a plain program's by a relative error of at most 0.018.
Values may be sent and summed in bfloat16 or wider, within the bound.
No kernel may reach another device: no remote copies, remote signals or barrier semaphores. Data moves between devices by JAX's collectives and lax.ppermute only.
A program may use at most 64 MiB of HBM per device.

v0:
```python
import jax
import jax.numpy as jnp
from jax import lax
from jax.sharding import PartitionSpec as P

M = 384
MODES = 3
OMAX = 4


def from_behind(value, axis, steps):
    count = lax.axis_size(axis)
    leading, last = (max(0, -steps), min(count, count - steps))
    return lax.ppermute(value, axis, [(source, source + steps) for source in range(leading, last)])


def entering(part, axis, combine, identity):
    place = lax.axis_index(axis)
    gathered = lax.all_gather(part, axis)
    state = jnp.zeros_like(part) + jnp.asarray(identity, part.dtype)

    def one(hop, state):
        return combine(state, lax.dynamic_index_in_dim(gathered, hop, 0, False))

    return lax.fori_loop(0, place, one, state)


def left_real(matrices, blocks):
    return jnp.einsum("eab,ebc->eac", matrices, blocks, preferred_element_type=jnp.float32)


def right_real(blocks, matrices):
    batch_size, row_count, double = blocks.shape
    halves = blocks.reshape(batch_size, row_count, 2, double // 2)
    product = jnp.einsum("eatm,emb->eatb", halves, matrices, preferred_element_type=jnp.float32)
    return product.reshape(batch_size, row_count, double)


def complex_matrix(blocks):
    half_width = blocks.shape[-1] // 2
    real_part = blocks[..., :half_width]
    imag_part = blocks[..., half_width:]
    top_rows = jnp.concatenate([real_part, imag_part], axis=-1)
    bottom_rows = jnp.concatenate([-imag_part, real_part], axis=-1)
    return jnp.concatenate([top_rows, bottom_rows], axis=-2)


def complex_product(first, second):
    return jnp.einsum(
        "eam,emn->ean", first, complex_matrix(second), preferred_element_type=jnp.float32
    )


def add_vectors(earlier, later):
    return earlier + later


def body(green_local, coupling, phonon_coupling, offsets, bose_factors):
    local_count, row_count, double = green_local.shape
    links = coupling[None]
    links_transposed = jnp.swapaxes(links, 1, 2)
    upper_blocks = from_behind(green_local, "slab", -1)
    down_left = left_real(links_transposed, green_local).astype(jnp.bfloat16)
    own_sandwich = right_real(down_left, links).astype(jnp.bfloat16)
    lower_term = from_behind(own_sandwich, "slab", 1)
    up_left = left_real(links, upper_blocks).astype(jnp.bfloat16)
    upper_term = right_real(up_left, links_transposed).astype(jnp.bfloat16)
    couple = (upper_term.astype(jnp.float32) + lower_term.astype(jnp.float32)).astype(jnp.bfloat16)
    dressed = complex_product(green_local, couple).astype(jnp.bfloat16)
    greens = (green_local.astype(jnp.float32) + complex_product(dressed, green_local) / M).astype(
        jnp.bfloat16
    )
    hop_count = (OMAX + local_count - 1) // local_count
    lower_list = [from_behind(greens, "energy", distance) for distance in range(hop_count, 0, -1)]
    upper_list = [from_behind(greens, "energy", -distance) for distance in range(1, hop_count + 1)]
    window_low = jnp.concatenate(lower_list + [greens], axis=0)
    window_high = jnp.concatenate([greens] + upper_list, axis=0)
    accumulated = jnp.zeros((local_count, row_count, double), jnp.float32)
    for mode_index in range(MODES):
        shift_size = offsets[mode_index]
        lower_block = lax.dynamic_slice_in_dim(
            window_low, hop_count * local_count - shift_size, local_count, 0
        )
        upper_block = lax.dynamic_slice_in_dim(window_high, shift_size, local_count, 0)
        factor = bose_factors[mode_index]
        mixture = (
            (factor + 1.0) * lower_block.astype(jnp.float32)
            + factor * upper_block.astype(jnp.float32)
        ).astype(jnp.bfloat16)
        matrices = phonon_coupling[mode_index][None]
        phonon_left = left_real(matrices, mixture).astype(jnp.bfloat16)
        accumulated = accumulated + right_real(phonon_left, jnp.swapaxes(matrices, 1, 2))
    phonon_sigma = accumulated.astype(jnp.bfloat16)
    energies = local_count * lax.axis_size("energy")
    positions = (
        lax.axis_index("energy") * local_count + jnp.arange(local_count, dtype=jnp.int32)
    ).astype(jnp.float32)
    holes = jax.nn.sigmoid((positions + 0.5 - energies / 2) * 4.0 / energies)
    imag_diag = jnp.diagonal(greens[..., row_count:], axis1=1, axis2=2).astype(jnp.float32)
    dos_terms = -holes[:, None] * imag_diag
    block_total = jnp.sum(dos_terms, axis=0)
    prefix = entering(block_total, "energy", add_vectors, jnp.zeros((row_count,), jnp.float32))
    cumulative = prefix[None] + jnp.cumsum(dos_terms, axis=0)
    return (phonon_sigma, cumulative)


def solution(mesh):
    in_specs = (P("energy", "slab", None), P("slab", None), P(), P(), P())
    out_specs = (P("energy", "slab", None), P("energy", "slab"))
    return jax.shard_map(body, mesh=mesh, in_specs=in_specs, out_specs=out_specs, check_vma=False)
```

profile of v0, /device:TPU:10, one launch (start us, length us, event | category | flops | bytes accessed | tf_op | source)
XLA Modules:
  0.0 150.8 jit_solution(1254850396683676293)
XLA Ops:
  0.7 1.4 collective-permute-start
  2.1 1.6 %convolution_convert_fusion.5 = bf16[384,768]{1,0:T(8,128)(2,1)S(1)} fusion(bf16[384,384]{1,0:T(8,128)(2,1)S(1)} %copy-done, bf16[1,384,768]{2,1,0:T(8,128)(2,1)} %param.7), kind=kOutput, calls=%fused_computation.14 | convolution fusion | flops 226787328 | bytes 1474560 | tf_op jit(solution)/shard_map/eab,ebc->eac/dot_general | solution.py:29
  3.7 0.5 convolution_convert_fusion.4
  4.2 3.1 %collective-permute-start.1 = (bf16[1,384,768]{1,2,0:T(8,128)(2,1)S(1)}, bf16[1,384,768]{1,2,0:T(8,128)(2,1)S(1)}, u32[]{:S(2)}, u32[]{:S(2)}) collective-permute-start(bf16[1,384,768]{1,2,0:T(8,128)(2,1)S(1)} %bitcast.97), channel_id=1, source_target_pairs={{0,1},{2,3},{4,5},{6,7},{8,9},{10,11},{12,13},{14,15},{16,17},{18,... | collective-permute-start | bytes 1769480 | tf_op jit(solution)/shard_map/ppermute | solution.py:14
  7.3 0.6 fusion.61
  15.2 0.8 slice_negate_fusion.1
  16.0 0.6 fusion.60
  20.5 0.5 convolution_convert_fusion.7
  21.0 0.5 convolution_convert_fusion.6
  21.8 0.7 copy-done.3
  22.5 1.6 %fusion.2 = bf16[1,384,768]{2,1,0:T(8,128)(2,1)S(1)} fusion(bf16[1,384,384]{2,1,0:T(8,128)(2,1)S(1)} %copy-done.3, bf16[1,384,384]{2,1,0:T(8,128)(2,1)S(1)} %get-tuple-element.44, bf16[1,384,768]{2,1,0:T(8,128)(2,1)S(1)} %copy-done.1, bf16[1,384,384]{1,2,0:T(8,128)(2,1)S(1)} %get-tuple-element.43, bf16[1,384,384]{1,2,0:T(8,128)(2,1)S(1)} %get-tuple-element.42, ...), kind=kOutput, calls=%fused_computation.7 | convolution fusion | flops 914522112 | bytes 2949120 | tf_op jit(solution)/shard_map/eam,emn->ean/dot_general | solution.py:49
  24.1 3.5 %collective-permute-start.2 = (bf16[1,384,768]{2,1,0:T(8,128)(2,1)S(1)}, bf16[1,384,768]{2,1,0:T(8,128)(2,1)}, u32[]{:S(2)}, u32[]{:S(2)}) collective-permute-start(bf16[1,384,768]{2,1,0:T(8,128)(2,1)S(1)} %fusion.2), channel_id=1, source_target_pairs={{0,8},{2,10},{4,12},{6,14},{8,16},{10,18},{12,20},{14,22},{16,24},... | collective-permute-start | bytes 1769480 | tf_op jit(solution)/shard_map/ppermute | solution.py:14
  27.6 3.5 %collective-permute-start.3 = (bf16[1,384,768]{2,1,0:T(8,128)(2,1)S(1)}, bf16[1,384,768]{2,1,0:T(8,128)(2,1)}, u32[]{:S(2)}, u32[]{:S(2)}) collective-permute-start(bf16[1,384,768]{2,1,0:T(8,128)(2,1)S(1)} %fusion.2), channel_id=1, source_target_pairs={{0,6},{2,8},{4,10},{6,12},{8,14},{10,16},{12,18},{14,20},{16,22},{... | collective-permute-start | bytes 1769480 | tf_op jit(solution)/shard_map/ppermute | solution.py:14
  31.0 3.4 %collective-permute-start.4 = (bf16[1,384,768]{2,1,0:T(8,128)(2,1)S(1)}, bf16[1,384,768]{2,1,0:T(8,128)(2,1)S(1)}, u32[]{:S(2)}, u32[]{:S(2)}) collective-permute-start(bf16[1,384,768]{2,1,0:T(8,128)(2,1)S(1)} %fusion.2), channel_id=1, source_target_pairs={{0,4},{2,6},{4,8},{6,10},{8,12},{10,14},{12,16},{14,18},{16,20},{1... | collective-permute-start | bytes 1769480 | tf_op jit(solution)/shard_map/ppermute | solution.py:14
  34.5 4.3 %collective-permute-start.5 = (bf16[1,384,768]{2,1,0:T(8,128)(2,1)S(1)}, bf16[1,384,768]{2,1,0:T(8,128)(2,1)S(1)}, u32[]{:S(2)}, u32[]{:S(2)}) collective-permute-start(bf16[1,384,768]{2,1,0:T(8,128)(2,1)S(1)} %fusion.2), channel_id=1, source_target_pairs={{0,2},{2,4},{4,6},{6,8},{8,10},{10,12},{12,14},{14,16},{16,18},{18... | collective-permute-start | bytes 1769480 | tf_op jit(solution)/shard_map/ppermute | solution.py:14
  38.8 1.9 %collective-permute-start.6 = (bf16[1,384,768]{2,1,0:T(8,128)(2,1)S(1)}, bf16[1,384,768]{2,1,0:T(8,128)(2,1)S(1)}, u32[]{:S(2)}, u32[]{:S(2)}) collective-permute-start(bf16[1,384,768]{2,1,0:T(8,128)(2,1)S(1)} %fusion.2), channel_id=1, source_target_pairs={{2,0},{4,2},{6,4},{8,6},{10,8},{12,10},{14,12},{16,14},{18,16},{20... | collective-permute-start | bytes 1769480 | tf_op jit(solution)/shard_map/ppermute | solution.py:14
  40.7 3.7 %gather_fusion = bf16[384]{0:T(512)(128)(2,1)S(1)} fusion(bf16[384,384]{1,0:T(8,128)(2,1)S(1)} %slice_bitcast_fusion, s32[384]{0:T(512)S(1)} %or_reduce_fusion), kind=kCustom, calls=%fused_computation | custom fusion | bytes 4608 | tf_op jit(solution)/shard_map/jit(diagonal)/gather | solution.py:99
  44.5 61.2 %all-gather.1 = f32[16,1,384]{2,1,0:T(1,128)S(1)} all-gather(f32[1,1,384]{2,1,0:T(1,128)S(1)} %reshape.244), channel_id=2, replica_groups=mesh['energy'=16,'slab'=2] {'energy'}, dimensions={0}, use_global_device_ids=true | all-gather | bytes 26112 | tf_op jit(solution)/shard_map/all_gather | solution.py:19
  105.9 0.6 add.118
  106.5 6.6 %collective-permute-start.7 = (bf16[1,384,768]{2,1,0:T(8,128)(2,1)S(1)}, bf16[1,384,768]{2,1,0:T(8,128)(2,1)S(1)}, u32[]{:S(2)}, u32[]{:S(2)}) collective-permute-start(bf16[1,384,768]{2,1,0:T(8,128)(2,1)S(1)} %fusion.2), channel_id=1, source_target_pairs={{4,0},{6,2},{8,4},{10,6},{12,8},{14,10},{16,12},{18,14},{20,16},{2... | collective-permute-start | bytes 1769480 | tf_op jit(solution)/shard_map/ppermute | solution.py:14
  113.1 1.1 constant_dynamic-update-slice_fusion.4
  114.2 5.2 %collective-permute-start.8 = (bf16[1,384,768]{2,1,0:T(8,128)(2,1)S(1)}, bf16[1,384,768]{2,1,0:T(8,128)(2,1)S(1)}, u32[]{:S(2)}, u32[]{:S(2)}) collective-permute-start(bf16[1,384,768]{2,1,0:T(8,128)(2,1)S(1)} %fusion.2), channel_id=1, source_target_pairs={{6,0},{8,2},{10,4},{12,6},{14,8},{16,10},{18,12},{20,14},{22,16},{... | collective-permute-start | bytes 1769480 | tf_op jit(solution)/shard_map/ppermute | solution.py:14
  119.4 1.1 constant_dynamic-update-slice_fusion.3
  120.5 1.9 %collective-permute-start.9 = (bf16[1,384,768]{2,1,0:T(8,128)(2,1)S(1)}, bf16[1,384,768]{2,1,0:T(8,128)(2,1)S(1)}, u32[]{:S(2)}, u32[]{:S(2)}) collective-permute-start(bf16[1,384,768]{2,1,0:T(8,128)(2,1)S(1)} %fusion.2), channel_id=1, source_target_pairs={{8,0},{10,2},{12,4},{14,6},{16,8},{18,10},{20,12},{22,14},{24,16},... | collective-permute-start | bytes 1769480 | tf_op jit(solution)/shard_map/ppermute | solution.py:14
  122.7 4.2 %collective-permute-done.7 = bf16[1,384,768]{2,1,0:T(8,128)(2,1)S(1)} collective-permute-done((bf16[1,384,768]{2,1,0:T(8,128)(2,1)S(1)}, bf16[1,384,768]{2,1,0:T(8,128)(2,1)S(1)}, u32[]{:S(2)}, u32[]{:S(2)}) %collective-permute-start.7) | collective-permute-done | bytes 589856 | tf_op jit(solution)/shard_map/ppermute | solution.py:14
  126.9 10.8 %collective-permute-done.8 = bf16[1,384,768]{2,1,0:T(8,128)(2,1)S(1)} collective-permute-done((bf16[1,384,768]{2,1,0:T(8,128)(2,1)S(1)}, bf16[1,384,768]{2,1,0:T(8,128)(2,1)S(1)}, u32[]{:S(2)}, u32[]{:S(2)}) %collective-permute-start.8) | collective-permute-done | bytes 589856 | tf_op jit(solution)/shard_map/ppermute | solution.py:14
  137.8 6.9 %collective-permute-done.9 = bf16[1,384,768]{2,1,0:T(8,128)(2,1)S(1)} collective-permute-done((bf16[1,384,768]{2,1,0:T(8,128)(2,1)S(1)}, bf16[1,384,768]{2,1,0:T(8,128)(2,1)S(1)}, u32[]{:S(2)}, u32[]{:S(2)}) %collective-permute-start.9) | collective-permute-done | bytes 589856 | tf_op jit(solution)/shard_map/ppermute | solution.py:14
  144.7 1.2 convolution_convert_fusion.2
  146.3 1.2 convolution_convert_fusion.1
  148.0 1.2 convolution_convert_fusion
  149.2 0.5 fusion.3
  149.7 1.1 copy.27
  (47 shorter events, 2.1 us)
Async XLA Ops:
  0.6 1.5 copy-start
  0.6 14.6 %copy-start.1 = (bf16[1,384,768]{2,1,0:T(8,128)(2,1)S(1)}, bf16[1,384,768]{2,1,0:T(8,128)(2,1)}, u32[]{:S(2)}) copy-start(bf16[1,384,768]{2,1,0:T(8,128)(2,1)} %param.7) | copy-start | bytes 1769476
  0.7 6.7 %copy-start.4 = (s32[3]{0:T(128)S(1)}, s32[3]{0:T(128)}, u32[]{:S(2)}) copy-start(s32[3]{0:T(128)} %param.10) | copy-start | bytes 40
  0.7 19.9 %collective-permute-start = (bf16[1,384,768]{2,1,0:T(8,128)(2,1)}, bf16[1,384,768]{2,1,0:T(8,128)(2,1)S(1)}, u32[]{:S(2)}, u32[]{:S(2)}) collective-permute-start(bf16[1,384,768]{2,1,0:T(8,128)(2,1)} %param.7), channel_id=1, source_target_pairs={{1,0},{3,2},{5,4},{7,6},{9,8},{11,10},{13,12},{15,14},{17,16},{19,... | collective-permute-start | bytes 1769480 | tf_op jit(solution)/shard_map/ppermute | solution.py:14
  3.7 12.3 %copy-start.5 = (f32[3]{0:T(128)S(1)}, f32[3]{0:T(128)}, u32[]{:S(2)}) copy-start(f32[3]{0:T(128)} %param.11) | copy-start | bytes 40
  4.2 17.3 %collective-permute-start.1 = (bf16[1,384,768]{1,2,0:T(8,128)(2,1)S(1)}, bf16[1,384,768]{1,2,0:T(8,128)(2,1)S(1)}, u32[]{:S(2)}, u32[]{:S(2)}) collective-permute-start(bf16[1,384,768]{1,2,0:T(8,128)(2,1)S(1)} %bitcast.97), channel_id=1, source_target_pairs={{0,1},{2,3},{4,5},{6,7},{8,9},{10,11},{12,13},{14,15},{16,17},{18,... | collective-permute-start | bytes 1769480 | tf_op jit(solution)/shard_map/ppermute | solution.py:14
  21.5 1.0 copy-start.3
  24.1 82.4 %collective-permute-start.2 = (bf16[1,384,768]{2,1,0:T(8,128)(2,1)S(1)}, bf16[1,384,768]{2,1,0:T(8,128)(2,1)}, u32[]{:S(2)}, u32[]{:S(2)}) collective-permute-start(bf16[1,384,768]{2,1,0:T(8,128)(2,1)S(1)} %fusion.2), channel_id=1, source_target_pairs={{0,8},{2,10},{4,12},{6,14},{8,16},{10,18},{12,20},{14,22},{16,24},... | collective-permute-start | bytes 1769480 | tf_op jit(solution)/shard_map/ppermute | solution.py:14
  27.6 86.7 %collective-permute-start.3 = (bf16[1,384,768]{2,1,0:T(8,128)(2,1)S(1)}, bf16[1,384,768]{2,1,0:T(8,128)(2,1)}, u32[]{:S(2)}, u32[]{:S(2)}) collective-permute-start(bf16[1,384,768]{2,1,0:T(8,128)(2,1)S(1)} %fusion.2), channel_id=1, source_target_pairs={{0,6},{2,8},{4,10},{6,12},{8,14},{10,16},{12,18},{14,20},{16,22},{... | collective-permute-start | bytes 1769480 | tf_op jit(solution)/shard_map/ppermute | solution.py:14
  31.0 89.5 %collective-permute-start.4 = (bf16[1,384,768]{2,1,0:T(8,128)(2,1)S(1)}, bf16[1,384,768]{2,1,0:T(8,128)(2,1)S(1)}, u32[]{:S(2)}, u32[]{:S(2)}) collective-permute-start(bf16[1,384,768]{2,1,0:T(8,128)(2,1)S(1)} %fusion.2), channel_id=1, source_target_pairs={{0,4},{2,6},{4,8},{6,10},{8,12},{10,14},{12,16},{14,18},{16,20},{1... | collective-permute-start | bytes 1769480 | tf_op jit(solution)/shard_map/ppermute | solution.py:14
  34.5 88.1 %collective-permute-start.5 = (bf16[1,384,768]{2,1,0:T(8,128)(2,1)S(1)}, bf16[1,384,768]{2,1,0:T(8,128)(2,1)S(1)}, u32[]{:S(2)}, u32[]{:S(2)}) collective-permute-start(bf16[1,384,768]{2,1,0:T(8,128)(2,1)S(1)} %fusion.2), channel_id=1, source_target_pairs={{0,2},{2,4},{4,6},{6,8},{8,10},{10,12},{12,14},{14,16},{16,18},{18... | collective-permute-start | bytes 1769480 | tf_op jit(solution)/shard_map/ppermute | solution.py:14
  38.8 83.9 %collective-permute-start.6 = (bf16[1,384,768]{2,1,0:T(8,128)(2,1)S(1)}, bf16[1,384,768]{2,1,0:T(8,128)(2,1)S(1)}, u32[]{:S(2)}, u32[]{:S(2)}) collective-permute-start(bf16[1,384,768]{2,1,0:T(8,128)(2,1)S(1)} %fusion.2), channel_id=1, source_target_pairs={{2,0},{4,2},{6,4},{8,6},{10,8},{12,10},{14,12},{16,14},{18,16},{20... | collective-permute-start | bytes 1769480 | tf_op jit(solution)/shard_map/ppermute | solution.py:14
  106.5 20.4 %collective-permute-start.7 = (bf16[1,384,768]{2,1,0:T(8,128)(2,1)S(1)}, bf16[1,384,768]{2,1,0:T(8,128)(2,1)S(1)}, u32[]{:S(2)}, u32[]{:S(2)}) collective-permute-start(bf16[1,384,768]{2,1,0:T(8,128)(2,1)S(1)} %fusion.2), channel_id=1, source_target_pairs={{4,0},{6,2},{8,4},{10,6},{12,8},{14,10},{16,12},{18,14},{20,16},{2... | collective-permute-start | bytes 1769480 | tf_op jit(solution)/shard_map/ppermute | solution.py:14
  114.2 23.5 %collective-permute-start.8 = (bf16[1,384,768]{2,1,0:T(8,128)(2,1)S(1)}, bf16[1,384,768]{2,1,0:T(8,128)(2,1)S(1)}, u32[]{:S(2)}, u32[]{:S(2)}) collective-permute-start(bf16[1,384,768]{2,1,0:T(8,128)(2,1)S(1)} %fusion.2), channel_id=1, source_target_pairs={{6,0},{8,2},{10,4},{12,6},{14,8},{16,10},{18,12},{20,14},{22,16},{... | collective-permute-start | bytes 1769480 | tf_op jit(solution)/shard_map/ppermute | solution.py:14
  120.5 24.1 %collective-permute-start.9 = (bf16[1,384,768]{2,1,0:T(8,128)(2,1)S(1)}, bf16[1,384,768]{2,1,0:T(8,128)(2,1)S(1)}, u32[]{:S(2)}, u32[]{:S(2)}) collective-permute-start(bf16[1,384,768]{2,1,0:T(8,128)(2,1)S(1)} %fusion.2), channel_id=1, source_target_pairs={{8,0},{10,2},{12,4},{14,6},{16,8},{18,10},{20,12},{22,14},{24,16},... | collective-permute-start | bytes 1769480 | tf_op jit(solution)/shard_map/ppermute | solution.py:14
  126.9 17.8 %copy-start.2 = (bf16[3,384,384]{2,1,0:T(8,128)(2,1)S(1)}, bf16[3,384,384]{2,1,0:T(8,128)(2,1)}, u32[]{:S(2)}) copy-start(bf16[3,384,384]{2,1,0:T(8,128)(2,1)} %param.9) | copy-start | bytes 2654212
where the time goes:
time: 154 us; the launch traced here: 151 us
  blocking collectives  61.2 us (40%)
  starting transfers between devices  34.8 us (23%)
  waiting for transfers between devices  21.8 us (14%)
  between operations  12.2 us (8%)
  local copies, waits for them, and re-layouts  9.95 us (6%)
  matrix products  9.61 us (6%)
    all_gather x1, blocking collectives, entering(): gathered = lax.all_gather(part, axis)  61.2 us
    ppermute x10, starting transfers between devices, from_behind(): lax.ppermute(value, axis, [(source, source + steps) for source in range(l...  34.8 us
    ppermute x10, waiting for transfers between devices, from_behind(): lax.ppermute(value, axis, [(source, source + steps) for source in range(l...  21.8 us
    dot_general x5, matrix products, left_real(): jnp.einsum('eab,ebc->eac', matrices, blocks, preferred_element_type=jnp.f...  5.59 us
    unnamed x22, local copies, waits for them, and re-layouts  4.19 us
    gather x1, local copies, waits for them, and re-layouts, body(): jnp.diagonal(greens[..., row_count:], axis1=1, axis2=2).astype(jnp.float32)  3.69 us
  transfers between devices with their start and end apart: 10, of which 3 were waited for; matrix products, arithmetic and copies ran while one was open for 8% of the time, Pallas kernels for 0%

commit v1 on v0

v1 whole, which is shorter than its diff:
```python
import functools

import jax
import jax.numpy as jnp
from jax import lax
from jax.experimental import pallas as pl
from jax.experimental.pallas import tpu as pltpu
from jax.sharding import PartitionSpec as P

OMAX = 4
GROUP = OMAX
VMEM_LIMIT = 24 * 1024 * 1024

WHOLE = pl.BlockSpec(memory_space=pltpu.VMEM)
SCALARS = pl.BlockSpec(memory_space=pltpu.SMEM)


def nn(a, b):
    return lax.dot_general(a, b, (((1,), (0,)), ((), ())), preferred_element_type=jnp.float32)


def nt(a, b):
    return lax.dot_general(a, b, (((1,), (1,)), ((), ())), preferred_element_type=jnp.float32)


def tn(a, b):
    return lax.dot_general(a, b, (((0,), (0,)), ((), ())), preferred_element_type=jnp.float32)


def bf(value):
    return value.astype(jnp.bfloat16)


def f32(value):
    return value.astype(jnp.float32)


def call(kernel, outs, ins, scratch, units, m):
    spaces = [SCALARS if i.ndim == 1 else WHOLE for i in ins]
    moved = sum(a.size * a.dtype.itemsize for a in (*ins, *outs))
    return pl.pallas_call(
        kernel,
        out_shape=outs,
        in_specs=spaces,
        out_specs=[WHOLE] * len(outs),
        scratch_shapes=scratch,
        compiler_params=pltpu.CompilerParams(vmem_limit_bytes=VMEM_LIMIT),
        cost_estimate=pl.CostEstimate(
            flops=2 * units * m * m * m, bytes_accessed=moved, transcendentals=0
        ),
    )(*ins)


def upper_term(link, block):
    m = link.shape[0]
    left = bf(nn(link, block))
    return bf(nt(left[:, :m], link)), bf(nt(left[:, m:], link))


def lower_term(link, block):
    m = link.shape[0]
    left = bf(tn(link, block))
    return bf(nn(left[:, :m], link)), bf(nn(left[:, m:], link))


def finish_greens(g, real, imag, greens_real, greens_imag):
    m = g.shape[0]
    g_real, g_imag = g[:, :m], g[:, m:]
    dressed = bf(
        nn(g_real, jnp.concatenate([real, imag], axis=1))
        + nn(g_imag, jnp.concatenate([-imag, real], axis=1))
    )
    swapped = jnp.concatenate([-g_imag, g_real], axis=1)
    greens = bf(f32(g) + (nn(dressed[:, :m], g) + nn(dressed[:, m:], swapped)) / m)
    greens_real[...] = greens[:, :m]
    greens_imag[...] = greens[:, m:]


def greens_of_pair(g_ref, other_ref, own_ref, below_ref, real_ref, imag_ref, couple):
    m = own_ref.shape[0]
    slab = lax.axis_index("slab")

    @pl.when(slab == 0)
    def _():
        real, imag = upper_term(own_ref[...], other_ref[...])
        couple[:, :m] = real
        couple[:, m:] = imag

    @pl.when(slab != 0)
    def _():
        real, imag = lower_term(below_ref[...], other_ref[...])
        couple[:, :m] = real
        couple[:, m:] = imag

    finish_greens(g_ref[...], couple[:, :m], couple[:, m:], real_ref, imag_ref)


def greens_of_chain(g_ref, above_ref, lower_ref, own_ref, below_ref, real_ref, imag_ref):
    up_real, up_imag = upper_term(own_ref[...], above_ref[...])
    low_real, low_imag = lower_term(below_ref[...], lower_ref[...])
    real = bf(f32(up_real) + f32(low_real))
    imag = bf(f32(up_imag) + f32(low_imag))
    finish_greens(g_ref[...], real, imag, real_ref, imag_ref)


def greens_halves(g, coupling):
    m = g.shape[0]
    slabs = lax.axis_size("slab")
    half = jax.ShapeDtypeStruct((m, m), jnp.bfloat16)
    up = [(s, s + 1) for s in range(slabs - 1)]
    down = [(s + 1, s) for s in range(slabs - 1)]
    if slabs == 2:
        other = lax.ppermute(g, "slab", up + down)
        below = lax.ppermute(coupling, "slab", up)
        scratch = [pltpu.VMEM(g.shape, jnp.bfloat16)]
        return call(greens_of_pair, [half] * 2, [g, other, coupling, below], scratch, 12, m)
    above = lax.ppermute(g, "slab", down)
    lower = lax.ppermute(g, "slab", up)
    below = lax.ppermute(coupling, "slab", up)
    return call(greens_of_chain, [half] * 2, [g, above, lower, coupling, below], [], 16, m)


def place():
    energy = lax.axis_index("energy")
    group = lax.div(energy, jnp.int32(GROUP))
    seat = lax.rem(energy, jnp.int32(GROUP))
    return energy, group, seat


def first_side(group):
    return 1 - 2 * lax.rem(group, jnp.int32(2))


def add_modes(total, sources, phonon_ref, offsets_ref, bose_ref):
    for mode in range(phonon_ref.shape[0]):
        shift, factor = offsets_ref[mode], bose_ref[mode]
        weights = []
        used = jnp.bool_(False)
        for _, distance in sources:
            below, above = distance == shift, distance == -shift
            weights.append(jnp.where(below, factor + 1.0, jnp.where(above, factor, 0.0)))
            used = jnp.logical_or(used, jnp.logical_or(below, above))

        @pl.when(used)
        def _(mode=mode, weights=weights):
            mixture = None
            for weight, (ref, _) in zip(weights, sources):
                term = weight * f32(ref[...])
                mixture = term if mixture is None else mixture + term
            matrix = phonon_ref[mode]
            total[...] += nt(bf(nn(matrix, bf(mixture))), matrix)


def to_seats(own_ref, first_ref, second_ref, phonon_ref, offsets_ref, bose_ref, *rest):
    *outs, total = rest
    _, group, seat = place()
    side = first_side(group)
    for j, out in enumerate(outs, 1):
        apart = jnp.bitwise_xor(seat, j) - seat
        sources = [
            (own_ref, apart),
            (first_ref, apart - GROUP * side),
            (second_ref, apart + GROUP * side),
        ]
        total[...] = jnp.zeros_like(total)
        add_modes(total, sources, phonon_ref, offsets_ref, bose_ref)
        out[...] = bf(total[...])


def dos(imag_ref, energy, energies):
    m = imag_ref.shape[0]
    rows = lax.broadcasted_iota(jnp.int32, (m, m), 0)
    columns = lax.broadcasted_iota(jnp.int32, (m, m), 1)
    diagonal = jnp.where(rows == columns, f32(imag_ref[...]), 0.0)
    position = jnp.full((1, m), f32(energy), jnp.float32)
    holes = 1.0 / (1.0 + jnp.exp(-((position + 0.5 - energies / 2) * 4.0 / energies)))
    return -holes * jnp.sum(diagonal, axis=0, keepdims=True)


def to_groups(energies, *refs):
    parts, (phonon_ref, offsets_ref, bose_ref) = refs[:GROUP], refs[GROUP : GROUP + 3]
    first_out, second_out, within_ref, sum_ref, total = refs[GROUP + 3 :]
    energy, group, seat = place()
    side = first_side(group)
    for out, toward in ((first_out, side), (second_out, -side)):
        sources = [
            (part, GROUP * toward + seat - jnp.bitwise_xor(seat, j)) for j, part in enumerate(parts)
        ]
        total[...] = jnp.zeros_like(total)
        add_modes(total, sources, phonon_ref, offsets_ref, bose_ref)
        out[...] = bf(total[...])
    within = jnp.zeros(within_ref.shape, jnp.float32)
    whole = jnp.zeros(sum_ref.shape, jnp.float32)
    for j, part in enumerate(parts):
        source = jnp.bitwise_xor(seat, j)
        terms = dos(part, energy - seat + source, energies)
        within = within + jnp.where(source <= seat, terms, 0.0)
        whole = whole + terms
    within_ref[...] = within
    sum_ref[...] = whole


def own_terms(*refs):
    parts = refs[: GROUP - 1]
    first_ref, second_ref, phonon_ref, offsets_ref, bose_ref, real_total, imag_total = refs[GROUP - 1 :]
    _, group, seat = place()
    side = first_side(group)
    real_total[...] = jnp.zeros_like(real_total)
    imag_total[...] = jnp.zeros_like(imag_total)
    column = [(first_ref, -GROUP * side), (second_ref, GROUP * side)]
    add_modes(real_total, column, phonon_ref, offsets_ref, bose_ref)
    sources = [(part, seat - jnp.bitwise_xor(seat, j)) for j, part in enumerate(parts, 1)]
    add_modes(imag_total, sources, phonon_ref, offsets_ref, bose_ref)


def last_sum(real_total, imag_total, a, b, c, first, second, out):
    m = real_total.shape[0]
    out[:, :m] = bf(real_total[...] + f32(a[...]) + f32(b[...]) + f32(c[...]))
    out[:, m:] = bf(imag_total[...] + f32(first[...]) + f32(second[...]))


def across_seats(value, j):
    energies = lax.axis_size("energy")
    return lax.ppermute(value, "energy", [(e, e ^ j) for e in range(energies)])


def across_groups(value, partner):
    groups = lax.axis_size("energy") // GROUP
    pairs = [(group, partner(group)) for group in range(groups)]
    return lax.ppermute(
        value,
        "energy",
        [(GROUP * a + i, GROUP * b + i) for a, b in pairs if 0 <= b < groups for i in range(GROUP)],
    )


def first_pair(group):
    return group ^ 1


def second_pair(group):
    return ((group + 1) ^ 1) - 1


def body(green_local, coupling, phonon_coupling, offsets, bose_factors):
    g = green_local[0]
    m = g.shape[0]
    energies = lax.axis_size("energy")
    half = jax.ShapeDtypeStruct((m, m), jnp.bfloat16)
    wide = jax.ShapeDtypeStruct((m, m), jnp.float32)
    line = jax.ShapeDtypeStruct((1, m), jnp.float32)
    total = [pltpu.VMEM((m, m), jnp.float32)]
    modes = [phonon_coupling, offsets, bose_factors]

    real, imag = greens_halves(g, coupling)
    first_real = across_groups(real, first_pair)
    second_real = across_groups(real, second_pair)
    imags = [imag] + [across_seats(imag, j) for j in range(1, GROUP)]

    sums = call(to_seats, [half] * (GROUP - 1), [real, first_real, second_real, *modes], total, 10, m)
    seat_terms = [across_seats(value, j) for j, value in enumerate(sums, 1)]

    first_out, second_out, within, group_sum = call(
        functools.partial(to_groups, energies), [half, half, line, line], [*imags, *modes], total, 12, m
    )
    first_term = across_groups(first_out, first_pair)
    second_term = across_groups(second_out, second_pair)

    real_total, imag_total = call(
        own_terms, [wide, wide], [*imags[1:], first_real, second_real, *modes], [], 6, m
    )

    group = place()[1]
    cumulative = within
    step = 1
    while step < energies // GROUP:
        received = across_groups(group_sum, lambda a, step=step: a ^ step)
        cumulative = cumulative + jnp.where(jnp.bitwise_and(group, step) > 0, received, 0.0)
        group_sum = group_sum + received
        step *= 2

    (sigma,) = call(
        last_sum,
        [jax.ShapeDtypeStruct(g.shape, jnp.bfloat16)],
        [real_total, imag_total, *seat_terms, first_term, second_term],
        [],
        0,
        m,
    )
    return sigma[None], cumulative


def solution(mesh):
    in_specs = (P("energy", "slab", None), P("slab", None), P(), P(), P())
    out_specs = (P("energy", "slab", None), P("energy", "slab"))
    return jax.shard_map(body, mesh=mesh, in_specs=in_specs, out_specs=out_specs, check_vma=False)
```

time: 154 us -> 59.3 us (0.39)
  the two profiles are of different devices: /device:TPU:10 before, /device:TPU:0 now
where the time goes in v1:
time: 59.3 us; the launch traced here: 59 us
  starting transfers between devices  22.5 us (38%)
  Pallas kernels  15.6 us (26%)
  waiting for transfers between devices  14.3 us (24%)
  local copies, waits for them, and re-layouts  5.21 us (9%)
  between operations  0.76 us (1%)
    pallas_call x5, Pallas kernels, call(): pl.pallas_call(kernel, out_shape=outs, in_specs=spaces, out_specs=[WHOLE]...  15.6 us
    ppermute x6, starting transfers between devices, across_groups(): lax.ppermute(value, 'energy', [(GROUP * a + i, GROUP * b + i) for a, b in...  11.9 us
    ppermute x6, waiting for transfers between devices, across_seats(): return lax.ppermute(value, 'energy', [(e, e ^ j) for e in range(energies)])  10.9 us
    ppermute x6, starting transfers between devices, across_seats(): return lax.ppermute(value, 'energy', [(e, e ^ j) for e in range(energies)])  7.99 us
    unnamed x22, local copies, waits for them, and re-layouts  5.21 us
    ppermute x1, starting transfers between devices, greens_halves(): below = lax.ppermute(coupling, 'slab', up)  2.1 us
    ppermute x6, waiting for transfers between devices, across_groups(): lax.ppermute(value, 'energy', [(GROUP * a + i, GROUP * b + i) for a, b in...  2.02 us
    ppermute x1, waiting for transfers between devices, greens_halves(): below = lax.ppermute(coupling, 'slab', up)  1.38 us
  transfers between devices with their start and end apart: 14, of which 6 were waited for; matrix products, arithmetic and copies ran while one was open for 1% of the time, Pallas kernels for 20%

profile of v1, /device:TPU:0, one launch (start us, length us, event | category | flops | bytes accessed | tf_op | source)
XLA Modules:
  0.0 59.0 jit_solution(8860248331547040308)
XLA Ops:
  0.6 0.5 collective-permute-start
  1.2 2.1 %collective-permute-start.1 = (bf16[384,384]{1,0:T(8,128)(2,1)}, bf16[384,384]{1,0:T(8,128)(2,1)S(1)}, u32[]{:S(2)}, u32[]{:S(2)}) collective-permute-start(bf16[384,384]{1,0:T(8,128)(2,1)} %own_ref.1), channel_id=1, source_target_pairs={{0,1},{2,3},{4,5},{6,7},{8,9},{10,11},{12,13},{14,15},{16,17},{18,... | collective-permute-start | bytes 884744 | tf_op jit(solution)/shard_map/ppermute | solution.py:114
  3.3 1.4 %collective-permute-done.1.below_ref = bf16[384,384]{1,0:T(8,128)(2,1)S(1)} collective-permute-done((bf16[384,384]{1,0:T(8,128)(2,1)}, bf16[384,384]{1,0:T(8,128)(2,1)S(1)}, u32[]{:S(2)}, u32[]{:S(2)}) %collective-permute-start.1) | collective-permute-done | bytes 294944 | tf_op jit(solution)/shard_map/ppermute | solution.py:114
  4.7 1.1 %copy-done.1 = bf16[1,384,768]{2,1,0:T(8,128)(2,1)S(1)} copy-done((bf16[1,384,768]{2,1,0:T(8,128)(2,1)S(1)}, bf16[1,384,768]{2,1,0:T(8,128)(2,1)}, u32[]{:S(2)}) %copy-start.1) | copy-done | bytes 589848
  5.7 1.0 %copy-done.2 = bf16[384,384]{1,0:T(8,128)(2,1)S(1)} copy-done((bf16[384,384]{1,0:T(8,128)(2,1)S(1)}, bf16[384,384]{1,0:T(8,128)(2,1)}, u32[]{:S(2)}) %copy-start.2) | copy-done | bytes 294936
  6.7 2.7 %shard_map.68 = (bf16[384,384]{1,0:T(8,128)(2,1)S(1)}, bf16[384,384]{1,0:T(8,128)(2,1)S(1)}) custom-call(bf16[384,768]{1,0:T(8,128)(2,1)S(1)} %bitcast.3, bf16[384,768]{1,0:T(8,128)(2,1)S(1)} %collective-permute-done.other_ref, bf16[384,384]{1,0:T(8,128)(2,1)S(1)} %copy-done.2, bf16[384,384]{1,0:T(8,128)(2,1)S(1)} %collective-permute-done.1.below_ref), custom_call_target="tpu_custom_call" | custom-call | flops 1358954496 | bytes 2359296 | tf_op jit(solution)/shard_map/pallas_call | solution.py:41
  9.4 3.8 %collective-permute-start.4 = (bf16[384,384]{1,0:T(8,128)(2,1)S(1)}, bf16[384,384]{1,0:T(8,128)(2,1)S(1)}, u32[]{:S(2)}, u32[]{:S(2)}) collective-permute-start(bf16[384,384]{1,0:T(8,128)(2,1)S(1)} %get-tuple-element.13.refs_0_), channel_id=1, source_target_pairs={{0,6},{2,4},{4,2},{6,0},{8,14},{10,12},{12,10},{14,8},{16,22},{18,... | collective-permute-start | bytes 884744 | tf_op jit(solution)/shard_map/ppermute | solution.py:224
  13.3 0.5 collective-permute-start.3
  13.8 0.1 collective-permute-start.2
  13.9 0.7 %collective-permute-start.6 = (bf16[384,384]{1,0:T(8,128)(2,1)S(1)}, bf16[384,384]{1,0:T(8,128)(2,1)S(1)}, u32[]{:S(2)}, u32[]{:S(2)}) collective-permute-start(bf16[384,384]{1,0:T(8,128)(2,1)S(1)} %get-tuple-element.14.own_ref), channel_id=1, source_target_pairs={{8,16},{10,18},{12,20},{14,22},{16,8},{18,10},{20,12},{22,14},{9,1... | collective-permute-start | bytes 884744 | tf_op jit(solution)/shard_map/ppermute | solution.py:230
  14.6 4.8 %collective-permute-start.5 = (bf16[384,384]{1,0:T(8,128)(2,1)S(1)}, bf16[384,384]{1,0:T(8,128)(2,1)S(1)}, u32[]{:S(2)}, u32[]{:S(2)}) collective-permute-start(bf16[384,384]{1,0:T(8,128)(2,1)S(1)} %get-tuple-element.14.own_ref), channel_id=1, source_target_pairs={{0,8},{2,10},{4,12},{6,14},{8,0},{10,2},{12,4},{14,6},{16,24},{18,... | collective-permute-start | bytes 884744 | tf_op jit(solution)/shard_map/ppermute | solution.py:230
  19.4 1.7 %collective-permute-done.4.refs_2_.refs_3_ = bf16[384,384]{1,0:T(8,128)(2,1)S(1)} collective-permute-done((bf16[384,384]{1,0:T(8,128)(2,1)S(1)}, bf16[384,384]{1,0:T(8,128)(2,1)S(1)}, u32[]{:S(2)}, u32[]{:S(2)}) %collective-permute-start.4) | collective-permute-done | bytes 294944 | tf_op jit(solution)/shard_map/ppermute | solution.py:224
  21.1 6.0 %collective-permute-done.3.refs_1_.refs_2_ = bf16[384,384]{1,0:T(8,128)(2,1)S(1)} collective-permute-done((bf16[384,384]{1,0:T(8,128)(2,1)S(1)}, bf16[384,384]{1,0:T(8,128)(2,1)S(1)}, u32[]{:S(2)}, u32[]{:S(2)}) %collective-permute-start.3) | collective-permute-done | bytes 294944 | tf_op jit(solution)/shard_map/ppermute | solution.py:224
  27.1 0.3 collective-permute-done.2.refs_0_.refs_1_
  27.4 4.4 %shard_map.71 = (bf16[384,384]{1,0:T(8,128)(2,1)}, bf16[384,384]{1,0:T(8,128)(2,1)S(1)}, f32[1,384]{1,0:T(1,128)S(1)}, f32[1,384]{1,0:T(1,128)S(1)}) custom-call(bf16[384,384]{1,0:T(8,128)(2,1)S(1)} %get-tuple-element.13.refs_0_, bf16[384,384]{1,0:T(8,128)(2,1)S(1)} %collective-permute-done.2.refs_0_.refs_1_, ...), custom_call_target="tpu_custom_call" | custom-call | flops 1358954496 | bytes 2657304 | tf_op jit(solution)/shard_map/pallas_call | solution.py:41
  31.8 1.6 %collective-permute-start.12 = (f32[1,384]{1,0:T(1,128)S(1)}, f32[1,384]{1,0:T(1,128)S(1)}, u32[]{:S(2)}, u32[]{:S(2)}) collective-permute-start(f32[1,384]{1,0:T(1,128)S(1)} %get-tuple-element.23), channel_id=1, source_target_pairs={{0,8},{2,10},{4,12},{6,14},{8,0},{10,2},{12,4},{14,6},{16,24},{18,... | collective-permute-start | bytes 4616 | tf_op jit(solution)/shard_map/ppermute | solution.py:230
  33.4 2.0 %collective-permute-done.12 = f32[1,384]{1,0:T(1,128)S(1)} collective-permute-done((f32[1,384]{1,0:T(1,128)S(1)}, f32[1,384]{1,0:T(1,128)S(1)}, u32[]{:S(2)}, u32[]{:S(2)}) %collective-permute-start.12) | collective-permute-done | bytes 1568 | tf_op jit(solution)/shard_map/ppermute | solution.py:230
  35.4 2.6 %collective-permute-start.13 = (f32[1,384]{1,0:T(1,128)S(1)}, f32[1,384]{1,0:T(1,128)S(1)}, u32[]{:S(2)}, u32[]{:S(2)}) collective-permute-start(f32[1,384]{1,0:T(1,128)S(1)} %add.10), channel_id=1, source_target_pairs={{0,16},{2,18},{4,20},{6,22},{8,24},{10,26},{12,28},{14,30},{16,0},... | collective-permute-start | bytes 4616 | tf_op jit(solution)/shard_map/ppermute | solution.py:230
  38.0 4.7 %shard_map.70 = (bf16[384,384]{1,0:T(8,128)(2,1)}, bf16[384,384]{1,0:T(8,128)(2,1)}, bf16[384,384]{1,0:T(8,128)(2,1)}) custom-call(bf16[384,384]{1,0:T(8,128)(2,1)S(1)} %get-tuple-element.14.own_ref, bf16[384,384]{1,0:T(8,128)(2,1)S(1)} %collective-permute-done.5.refs_3_.first_ref, bf16[384,384]{1,0:T(8,128)(2,1)S(1)} %collective-permute-done.6.refs_4_.second_ref, ...), custom_call_target="tpu_custom_call" | custom-call | flops 1132462080 | bytes 2654232 | tf_op jit(solution)/shard_map/pallas_call | solution.py:41
  42.7 1.5 %collective-permute-start.7 = (bf16[384,384]{1,0:T(8,128)(2,1)}, bf16[384,384]{1,0:T(8,128)(2,1)S(1)}, u32[]{:S(2)}, u32[]{:S(2)}) collective-permute-start(bf16[384,384]{1,0:T(8,128)(2,1)} %get-tuple-element.17), channel_id=1, source_target_pairs={{0,2},{2,0},{4,6},{6,4},{8,10},{10,8},{12,14},{14,12},{16,18},{18,... | collective-permute-start | bytes 884744 | tf_op jit(solution)/shard_map/ppermute | solution.py:224
  44.3 0.7 %collective-permute-start.8 = (bf16[384,384]{1,0:T(8,128)(2,1)}, bf16[384,384]{1,0:T(8,128)(2,1)S(1)}, u32[]{:S(2)}, u32[]{:S(2)}) collective-permute-start(bf16[384,384]{1,0:T(8,128)(2,1)} %get-tuple-element.18), channel_id=1, source_target_pairs={{0,4},{2,6},{4,0},{6,2},{8,12},{10,14},{12,8},{14,10},{16,20},{18,... | collective-permute-start | bytes 884744 | tf_op jit(solution)/shard_map/ppermute | solution.py:224
  45.0 1.3 %collective-permute-start.9 = (bf16[384,384]{1,0:T(8,128)(2,1)}, bf16[384,384]{1,0:T(8,128)(2,1)S(1)}, u32[]{:S(2)}, u32[]{:S(2)}) collective-permute-start(bf16[384,384]{1,0:T(8,128)(2,1)} %get-tuple-element.19), channel_id=1, source_target_pairs={{0,6},{2,4},{4,2},{6,0},{8,14},{10,12},{12,10},{14,8},{16,22},{18,... | collective-permute-start | bytes 884744 | tf_op jit(solution)/shard_map/ppermute | solution.py:224
  46.2 1.6 %collective-permute-start.10 = (bf16[384,384]{1,0:T(8,128)(2,1)}, bf16[384,384]{1,0:T(8,128)(2,1)S(1)}, u32[]{:S(2)}, u32[]{:S(2)}) collective-permute-start(bf16[384,384]{1,0:T(8,128)(2,1)} %get-tuple-element.20), channel_id=1, source_target_pairs={{0,8},{2,10},{4,12},{6,14},{8,0},{10,2},{12,4},{14,6},{16,24},{18,... | collective-permute-start | bytes 884744 | tf_op jit(solution)/shard_map/ppermute | solution.py:230
  47.8 0.6 copy-done.9
  48.4 0.7 %collective-permute-start.11 = (bf16[384,384]{1,0:T(8,128)(2,1)S(1)}, bf16[384,384]{1,0:T(8,128)(2,1)S(1)}, u32[]{:S(2)}, u32[]{:S(2)}) collective-permute-start(bf16[384,384]{1,0:T(8,128)(2,1)S(1)} %get-tuple-element.21), channel_id=1, source_target_pairs={{8,16},{10,18},{12,20},{14,22},{16,8},{18,10},{20,12},{22,14},{9,1... | collective-permute-start | bytes 884744 | tf_op jit(solution)/shard_map/ppermute | solution.py:230
  49.1 1.0 %copy-done.4 = bf16[384,384]{1,0:T(8,128)(2,1)S(1)} copy-done((bf16[384,384]{1,0:T(8,128)(2,1)S(1)}, bf16[384,384]{1,0:T(8,128)(2,1)}, u32[]{:S(2)}) %copy-start.4) | copy-done | bytes 294936
  50.0 1.0 %copy-done.6 = bf16[384,384]{1,0:T(8,128)(2,1)S(1)} copy-done((bf16[384,384]{1,0:T(8,128)(2,1)S(1)}, bf16[384,384]{1,0:T(8,128)(2,1)}, u32[]{:S(2)}) %copy-start.6) | copy-done | bytes 294936
  51.0 2.7 %shard_map.69 = (f32[384,384]{1,0:T(8,128)S(1)}, f32[384,384]{1,0:T(8,128)S(1)}) custom-call(bf16[384,384]{1,0:T(8,128)(2,1)S(1)} %collective-permute-done.2.refs_0_.refs_1_, bf16[384,384]{1,0:T(8,128)(2,1)S(1)} %collective-permute-done.3.refs_1_.refs_2_, bf16[384,384]{1,0:T(8,128)(2,1)S(1)} %collective-permute-done.4.refs_2_.refs_3_, ...), custom_call_target="tpu_custom_call" | custom-call | flops 679477248 | bytes 3538968 | tf_op jit(solution)/shard_map/pallas_call | solution.py:41
  53.8 0.7 %copy-done.10 = f32[1,384]{1,0:T(1,128)S(1)} copy-done((f32[1,384]{1,0:T(1,128)S(1)}, f32[1,384]{1,0:T(1,128)}, u32[]{:S(2)}) %copy-start.10) | copy-done | bytes 1560
  54.4 0.6 fusion.1
  55.0 2.9 %collective-permute-done.8.b = bf16[384,384]{1,0:T(8,128)(2,1)S(1)} collective-permute-done((bf16[384,384]{1,0:T(8,128)(2,1)}, bf16[384,384]{1,0:T(8,128)(2,1)S(1)}, u32[]{:S(2)}, u32[]{:S(2)}) %collective-permute-start.8) | collective-permute-done | bytes 294944 | tf_op jit(solution)/shard_map/ppermute | solution.py:224
  57.9 1.1 %shard_map.72 = bf16[384,768]{1,0:T(8,128)(2,1)} custom-call(f32[384,384]{1,0:T(8,128)S(1)} %get-tuple-element.15.real_total, f32[384,384]{1,0:T(8,128)S(1)} %get-tuple-element.16.imag_total, bf16[384,384]{1,0:T(8,128)(2,1)S(1)} %collective-permute-done.7.a, bf16[384,384]{1,0:T(8,128)(2,1)S(1)} %collective-permute-done.8.b, ...), custom_call_target="tpu_custom_call" | custom-call | bytes 3244032 | tf_op jit(solution)/shard_map/pallas_call | solution.py:41
  (25 shorter events, 0.1 us)
Async XLA Ops:
  0.6 26.8 %copy-start = (bf16[3,384,384]{2,1,0:T(8,128)(2,1)S(1)}, bf16[3,384,384]{2,1,0:T(8,128)(2,1)}, u32[]{:S(2)}) copy-start(bf16[3,384,384]{2,1,0:T(8,128)(2,1)} %refs_4_.1) | copy-start | bytes 2654212
  0.6 4.0 %collective-permute-start = (bf16[384,768]{1,0:T(8,128)(2,1)}, bf16[384,768]{1,0:T(8,128)(2,1)S(1)}, u32[]{:S(2)}, u32[]{:S(2)}) collective-permute-start(bf16[384,768]{1,0:T(8,128)(2,1)} %bitcast.2), channel_id=1, source_target_pairs={{0,1},{1,0},{2,3},{3,2},{4,5},{5,4},{6,7},{7,6},{8,9},{9,8},{10,11... | collective-permute-start | bytes 1769480 | tf_op jit(solution)/shard_map/ppermute | solution.py:113
  1.2 3.5 %collective-permute-start.1 = (bf16[384,384]{1,0:T(8,128)(2,1)}, bf16[384,384]{1,0:T(8,128)(2,1)S(1)}, u32[]{:S(2)}, u32[]{:S(2)}) collective-permute-start(bf16[384,384]{1,0:T(8,128)(2,1)} %own_ref.1), channel_id=1, source_target_pairs={{0,1},{2,3},{4,5},{6,7},{8,9},{10,11},{12,13},{14,15},{16,17},{18,... | collective-permute-start | bytes 884744 | tf_op jit(solution)/shard_map/ppermute | solution.py:114
  4.7 1.1 %copy-start.1 = (bf16[1,384,768]{2,1,0:T(8,128)(2,1)S(1)}, bf16[1,384,768]{2,1,0:T(8,128)(2,1)}, u32[]{:S(2)}) copy-start(bf16[1,384,768]{2,1,0:T(8,128)(2,1)} %param.5) | copy-start | bytes 1769476
  5.7 1.0 %copy-start.2 = (bf16[384,384]{1,0:T(8,128)(2,1)S(1)}, bf16[384,384]{1,0:T(8,128)(2,1)}, u32[]{:S(2)}) copy-start(bf16[384,384]{1,0:T(8,128)(2,1)} %own_ref.1) | copy-start | bytes 884740
  9.4 18.0 %copy-start.7 = (s32[3]{0:T(128)S(1)}, s32[3]{0:T(128)}, u32[]{:S(2)}) copy-start(s32[3]{0:T(128)} %refs_5_.3) | copy-start | bytes 40
  9.4 18.0 %copy-start.8 = (f32[3]{0:T(128)S(1)}, f32[3]{0:T(128)}, u32[]{:S(2)}) copy-start(f32[3]{0:T(128)} %refs_6_.3) | copy-start | bytes 40
  9.4 11.7 %collective-permute-start.4 = (bf16[384,384]{1,0:T(8,128)(2,1)S(1)}, bf16[384,384]{1,0:T(8,128)(2,1)S(1)}, u32[]{:S(2)}, u32[]{:S(2)}) collective-permute-start(bf16[384,384]{1,0:T(8,128)(2,1)S(1)} %get-tuple-element.13.refs_0_), channel_id=1, source_target_pairs={{0,6},{2,4},{4,2},{6,0},{8,14},{10,12},{12,10},{14,8},{16,22},{18,... | collective-permute-start | bytes 884744 | tf_op jit(solution)/shard_map/ppermute | solution.py:224
  13.3 13.9 %collective-permute-start.3 = (bf16[384,384]{1,0:T(8,128)(2,1)S(1)}, bf16[384,384]{1,0:T(8,128)(2,1)S(1)}, u32[]{:S(2)}, u32[]{:S(2)}) collective-permute-start(bf16[384,384]{1,0:T(8,128)(2,1)S(1)} %get-tuple-element.13.refs_0_), channel_id=1, source_target_pairs={{0,4},{2,6},{4,0},{6,2},{8,12},{10,14},{12,8},{14,10},{16,20},{18,... | collective-permute-start | bytes 884744 | tf_op jit(solution)/shard_map/ppermute | solution.py:224
  13.8 13.6 %collective-permute-start.2 = (bf16[384,384]{1,0:T(8,128)(2,1)S(1)}, bf16[384,384]{1,0:T(8,128)(2,1)S(1)}, u32[]{:S(2)}, u32[]{:S(2)}) collective-permute-start(bf16[384,384]{1,0:T(8,128)(2,1)S(1)} %get-tuple-element.13.refs_0_), channel_id=1, source_target_pairs={{0,2},{2,0},{4,6},{6,4},{8,10},{10,8},{12,14},{14,12},{16,18},{18,... | collective-permute-start | bytes 884744 | tf_op jit(solution)/shard_map/ppermute | solution.py:224
  13.9 24.1 %collective-permute-start.6 = (bf16[384,384]{1,0:T(8,128)(2,1)S(1)}, bf16[384,384]{1,0:T(8,128)(2,1)S(1)}, u32[]{:S(2)}, u32[]{:S(2)}) collective-permute-start(bf16[384,384]{1,0:T(8,128)(2,1)S(1)} %get-tuple-element.14.own_ref), channel_id=1, source_target_pairs={{8,16},{10,18},{12,20},{14,22},{16,8},{18,10},{20,12},{22,14},{9,1... | collective-permute-start | bytes 884744 | tf_op jit(solution)/shard_map/ppermute | solution.py:230
  14.6 23.4 %collective-permute-start.5 = (bf16[384,384]{1,0:T(8,128)(2,1)S(1)}, bf16[384,384]{1,0:T(8,128)(2,1)S(1)}, u32[]{:S(2)}, u32[]{:S(2)}) collective-permute-start(bf16[384,384]{1,0:T(8,128)(2,1)S(1)} %get-tuple-element.14.own_ref), channel_id=1, source_target_pairs={{0,8},{2,10},{4,12},{6,14},{8,0},{10,2},{12,4},{14,6},{16,24},{18,... | collective-permute-start | bytes 884744 | tf_op jit(solution)/shard_map/ppermute | solution.py:230
  31.8 3.6 %collective-permute-start.12 = (f32[1,384]{1,0:T(1,128)S(1)}, f32[1,384]{1,0:T(1,128)S(1)}, u32[]{:S(2)}, u32[]{:S(2)}) collective-permute-start(f32[1,384]{1,0:T(1,128)S(1)} %get-tuple-element.23), channel_id=1, source_target_pairs={{0,8},{2,10},{4,12},{6,14},{8,0},{10,2},{12,4},{14,6},{16,24},{18,... | collective-permute-start | bytes 4616 | tf_op jit(solution)/shard_map/ppermute | solution.py:230
  35.4 12.4 %collective-permute-start.13 = (f32[1,384]{1,0:T(1,128)S(1)}, f32[1,384]{1,0:T(1,128)S(1)}, u32[]{:S(2)}, u32[]{:S(2)}) collective-permute-start(f32[1,384]{1,0:T(1,128)S(1)} %add.10), channel_id=1, source_target_pairs={{0,16},{2,18},{4,20},{6,22},{8,24},{10,26},{12,28},{14,30},{16,0},... | collective-permute-start | bytes 4616 | tf_op jit(solution)/shard_map/ppermute | solution.py:230
  38.0 4.7 %copy-start.3 = (bf16[384,384]{1,0:T(8,128)(2,1)}, bf16[384,384]{1,0:T(8,128)(2,1)S(1)}, u32[]{:S(2)}) copy-start(bf16[384,384]{1,0:T(8,128)(2,1)S(1)} %collective-permute-done.6.refs_4_.second_ref) | copy-start | bytes 884740
  38.0 4.7 %copy-start.5 = (bf16[384,384]{1,0:T(8,128)(2,1)}, bf16[384,384]{1,0:T(8,128)(2,1)S(1)}, u32[]{:S(2)}) copy-start(bf16[384,384]{1,0:T(8,128)(2,1)S(1)} %collective-permute-done.5.refs_3_.first_ref) | copy-start | bytes 884740
  42.7 12.3 %collective-permute-start.7 = (bf16[384,384]{1,0:T(8,128)(2,1)}, bf16[384,384]{1,0:T(8,128)(2,1)S(1)}, u32[]{:S(2)}, u32[]{:S(2)}) collective-permute-start(bf16[384,384]{1,0:T(8,128)(2,1)} %get-tuple-element.17), channel_id=1, source_target_pairs={{0,2},{2,0},{4,6},{6,4},{8,10},{10,8},{12,14},{14,12},{16,18},{18,... | collective-permute-start | bytes 884744 | tf_op jit(solution)/shard_map/ppermute | solution.py:224
  44.3 13.7 %collective-permute-start.8 = (bf16[384,384]{1,0:T(8,128)(2,1)}, bf16[384,384]{1,0:T(8,128)(2,1)S(1)}, u32[]{:S(2)}, u32[]{:S(2)}) collective-permute-start(bf16[384,384]{1,0:T(8,128)(2,1)} %get-tuple-element.18), channel_id=1, source_target_pairs={{0,4},{2,6},{4,0},{6,2},{8,12},{10,14},{12,8},{14,10},{16,20},{18,... | collective-permute-start | bytes 884744 | tf_op jit(solution)/shard_map/ppermute | solution.py:224
  45.0 13.0 %collective-permute-start.9 = (bf16[384,384]{1,0:T(8,128)(2,1)}, bf16[384,384]{1,0:T(8,128)(2,1)S(1)}, u32[]{:S(2)}, u32[]{:S(2)}) collective-permute-start(bf16[384,384]{1,0:T(8,128)(2,1)} %get-tuple-element.19), channel_id=1, source_target_pairs={{0,6},{2,4},{4,2},{6,0},{8,14},{10,12},{12,10},{14,8},{16,22},{18,... | collective-permute-start | bytes 884744 | tf_op jit(solution)/shard_map/ppermute | solution.py:224
  46.2 11.7 %collective-permute-start.10 = (bf16[384,384]{1,0:T(8,128)(2,1)}, bf16[384,384]{1,0:T(8,128)(2,1)S(1)}, u32[]{:S(2)}, u32[]{:S(2)}) collective-permute-start(bf16[384,384]{1,0:T(8,128)(2,1)} %get-tuple-element.20), channel_id=1, source_target_pairs={{0,8},{2,10},{4,12},{6,14},{8,0},{10,2},{12,4},{14,6},{16,24},{18,... | collective-permute-start | bytes 884744 | tf_op jit(solution)/shard_map/ppermute | solution.py:230
  47.8 0.6 copy-start.9
  48.4 9.6 %collective-permute-start.11 = (bf16[384,384]{1,0:T(8,128)(2,1)S(1)}, bf16[384,384]{1,0:T(8,128)(2,1)S(1)}, u32[]{:S(2)}, u32[]{:S(2)}) collective-permute-start(bf16[384,384]{1,0:T(8,128)(2,1)S(1)} %get-tuple-element.21), channel_id=1, source_target_pairs={{8,16},{10,18},{12,20},{14,22},{16,8},{18,10},{20,12},{22,14},{9,1... | collective-permute-start | bytes 884744 | tf_op jit(solution)/shard_map/ppermute | solution.py:230
  49.1 1.0 %copy-start.4 = (bf16[384,384]{1,0:T(8,128)(2,1)S(1)}, bf16[384,384]{1,0:T(8,128)(2,1)}, u32[]{:S(2)}) copy-start(bf16[384,384]{1,0:T(8,128)(2,1)} %copy-done.3) | copy-start | bytes 884740
  50.0 1.0 %copy-start.6 = (bf16[384,384]{1,0:T(8,128)(2,1)S(1)}, bf16[384,384]{1,0:T(8,128)(2,1)}, u32[]{:S(2)}) copy-start(bf16[384,384]{1,0:T(8,128)(2,1)} %copy-done.5) | copy-start | bytes 884740
  53.7 0.7 %copy-start.10 = (f32[1,384]{1,0:T(1,128)S(1)}, f32[1,384]{1,0:T(1,128)}, u32[]{:S(2)}) copy-start(f32[1,384]{1,0:T(1,128)} %copy-done.9) | copy-start | bytes 4612

commit v2 on v1

v2 whole, which is shorter than its diff:
```python
import functools

import jax
import jax.numpy as jnp
from jax import lax
from jax.experimental import pallas as pl
from jax.experimental.pallas import tpu as pltpu
from jax.sharding import PartitionSpec as P

OMAX = 4
GROUP = OMAX
VMEM_LIMIT = 16 * 1024 * 1024

WHOLE = pl.BlockSpec(memory_space=pltpu.VMEM)
SCALARS = pl.BlockSpec(memory_space=pltpu.SMEM)


def nn(a, b):
    return lax.dot_general(a, b, (((1,), (0,)), ((), ())), preferred_element_type=jnp.float32)


def nt(a, b):
    return lax.dot_general(a, b, (((1,), (1,)), ((), ())), preferred_element_type=jnp.float32)


def tn(a, b):
    return lax.dot_general(a, b, (((0,), (0,)), ((), ())), preferred_element_type=jnp.float32)


def bf(value):
    return value.astype(jnp.bfloat16)


def f32(value):
    return value.astype(jnp.float32)


def call(kernel, outs, ins, scratch=(), flops=0):
    return pl.pallas_call(
        kernel,
        out_shape=outs,
        in_specs=[SCALARS if i.ndim == 1 else WHOLE for i in ins],
        out_specs=[WHOLE] * len(outs),
        scratch_shapes=scratch,
        compiler_params=pltpu.CompilerParams(vmem_limit_bytes=VMEM_LIMIT),
        cost_estimate=pl.CostEstimate(flops=flops, bytes_accessed=0, transcendentals=0),
    )(*ins)


def upper_term(link, block):
    m = link.shape[0]
    left = bf(nn(link, block))
    return bf(nt(left[:, :m], link)), bf(nt(left[:, m:], link))


def lower_term(link, block):
    m = link.shape[0]
    left = bf(tn(link, block))
    return bf(nn(left[:, :m], link)), bf(nn(left[:, m:], link))


def rotated(block):
    m = block.shape[0]
    return jnp.concatenate([-block[:, m:], block[:, :m]], axis=1)


def complex_product(first, second):
    m = first.shape[0]
    return nn(first[:, :m], second) + nn(first[:, m:], rotated(second))


def holes_at(energy, energies, shape):
    position = jnp.full(shape, f32(energy), jnp.float32)
    return 1.0 / (1.0 + jnp.exp(-((position + 0.5 - energies / 2) * 4.0 / energies)))


def hole_line(energies, out):
    out[...] = holes_at(lax.axis_index("energy"), energies, out.shape)


def diagonal_of(block_ref):
    m = block_ref.shape[0]
    tile = 128 if m % 128 == 0 else m
    rows = lax.broadcasted_iota(jnp.int32, (tile, tile), 0)
    columns = lax.broadcasted_iota(jnp.int32, (tile, tile), 1)
    parts = []
    for start in range(0, m, tile):
        block = f32(block_ref[start : start + tile, start : start + tile])
        parts.append(jnp.sum(jnp.where(rows == columns, block, 0.0), axis=0, keepdims=True))
    return jnp.concatenate(parts, axis=1)


def finish(g, dressed, holes_ref, real_ref, imag_ref, dos_ref):
    m = g.shape[0]
    greens = bf(f32(g) + complex_product(dressed, g) / m)
    real_ref[...] = greens[:, :m]
    imag_ref[...] = greens[:, m:]
    dos_ref[...] = -holes_ref[...] * diagonal_of(imag_ref)


def greens_of_pair(g_ref, other_ref, own_ref, below_ref, holes_ref, *rest):
    *outs, couple = rest
    m = own_ref.shape[0]
    slab = lax.axis_index("slab")

    @pl.when(slab == 0)
    def _():
        couple[:, :m], couple[:, m:] = upper_term(own_ref[...], other_ref[...])

    @pl.when(slab != 0)
    def _():
        couple[:, :m], couple[:, m:] = lower_term(below_ref[...], other_ref[...])

    g = g_ref[...]
    finish(g, bf(complex_product(g, couple[...])), holes_ref, *outs)


def greens_of_chain(g_ref, above_ref, lower_ref, own_ref, below_ref, holes_ref, *outs):
    up_real, up_imag = upper_term(own_ref[...], above_ref[...])
    low_real, low_imag = lower_term(below_ref[...], lower_ref[...])
    real = bf(f32(up_real) + f32(low_real))
    imag = bf(f32(up_imag) + f32(low_imag))
    g = g_ref[...]
    couple = jnp.concatenate([real, imag], axis=1)
    finish(g, bf(complex_product(g, couple)), holes_ref, *outs)


def greens_halves(g, coupling):
    m = g.shape[0]
    slabs = lax.axis_size("slab")
    half = jax.ShapeDtypeStruct((m, m), jnp.bfloat16)
    line = jax.ShapeDtypeStruct((1, m), jnp.float32)
    up = [(s, s + 1) for s in range(slabs - 1)]
    down = [(s + 1, s) for s in range(slabs - 1)]
    below = lax.ppermute(coupling, "slab", up)
    energies = lax.axis_size("energy")
    (holes,) = call(functools.partial(hole_line, energies), [line], [], flops=24 * m**3)
    if slabs == 2:
        other = lax.ppermute(g, "slab", up + down)
        couple = [pltpu.VMEM(g.shape, jnp.bfloat16)]
        ins = [g, other, coupling, below, holes]
        return call(greens_of_pair, [half, half, line], ins, couple)
    above = lax.ppermute(g, "slab", down)
    lower = lax.ppermute(g, "slab", up)
    ins = [g, above, lower, coupling, below, holes]
    return call(greens_of_chain, [half, half, line], ins)


def place():
    energy = lax.axis_index("energy")
    group = lax.div(energy, jnp.int32(GROUP))
    seat = lax.rem(energy, jnp.int32(GROUP))
    return energy, group, seat


def first_side(group):
    return 1 - 2 * lax.rem(group, jnp.int32(2))


def product(matrix, block, scale=None):
    left = nn(matrix, block)
    return nt(bf(left if scale is None else scale * left), matrix)


def mixed(first, first_weight, second, second_weight):
    return bf(first_weight * f32(first) + second_weight * f32(second))


def modes_of(offsets_ref):
    assert offsets_ref.shape == (3,)
    far = jnp.where(offsets_ref[1] == GROUP, 1, jnp.where(offsets_ref[2] == GROUP, 2, 0))
    return far, jnp.where(far == 0, 1, 0), jnp.where(far == 2, 1, 2)


def split_rows(line):
    high = bf(line)
    rest = line - f32(high)
    middle = bf(rest)
    low = bf(rest - f32(middle))
    rows = [f32(high), f32(middle), f32(low), jnp.zeros((13, line.shape[1]), jnp.float32)]
    return bf(jnp.concatenate(rows, axis=0))


def to_seats(own_ref, first_ref, second_ref, phonon_ref, offsets_ref, bose_ref, dos_ref, before_ref, *rest):
    *outs, bank, total = rest
    m = own_ref.shape[0]
    _, group, seat = place()
    side = first_side(group)
    bank[0] = own_ref[...]
    bank[1] = first_ref[...]
    bank[2] = second_ref[...]
    _, one, two = modes_of(offsets_ref)
    odd = jnp.where(lax.rem(offsets_ref[one], 2) == 1, one, two)
    left = one + two - odd

    def towards(j):
        apart = jnp.bitwise_xor(seat, j) - seat
        upward = apart > 0
        beside = jnp.where(upward == (side > 0), 1, 2)
        return jnp.abs(apart), upward, beside

    def single(j, mode):
        size, upward, beside = towards(j)
        shift, factor = offsets_ref[mode], bose_ref[mode]
        own = shift == size
        weight = jnp.where(own == upward, factor + 1.0, factor)
        return product(phonon_ref[mode], bank[jnp.where(own, 0, beside)], weight)

    for j in range(1, GROUP, 2):
        total[j // 2] = single(j, odd)

    @pl.when(lax.rem(offsets_ref[left], 2) == 0)
    def _():
        for j in range(1, GROUP, 2):
            outs[j - 1][:m] = bf(total[j // 2])
        factor = bose_ref[left]
        for j in range(2, GROUP, 2):
            _, upward, beside = towards(j)
            own_weight = jnp.where(upward, factor + 1.0, factor)
            beside_weight = jnp.where(upward, factor, factor + 1.0)
            block = mixed(bank[0], own_weight, bank[beside], beside_weight)
            outs[j - 1][:m] = bf(product(phonon_ref[left], block))

    @pl.when(lax.rem(offsets_ref[left], 2) == 1)
    def _():
        for j in range(1, GROUP, 2):
            outs[j - 1][:m] = bf(total[j // 2] + single(j, left))
        for j in range(2, GROUP, 2):
            outs[j - 1][:m] = jnp.zeros((m, m), jnp.bfloat16)

    for j, out in enumerate(outs, 1):
        counts = jnp.bitwise_xor(seat, j) > seat
        out[m:] = split_rows(before_ref[...] + jnp.where(counts, dos_ref[...], 0.0))


def to_groups(*refs):
    parts, (phonon_ref, offsets_ref, bose_ref) = refs[:GROUP], refs[GROUP : GROUP + 3]
    first_out, second_out, bank, total = refs[GROUP + 3 :]
    _, group, seat = place()
    upward = seat < GROUP // 2
    for j, part in enumerate(parts):
        bank[j] = part[...]
    far, _, _ = modes_of(offsets_ref)

    def gives(mode, up):
        shift, factor = offsets_ref[mode], bose_ref[mode]
        source = seat + jnp.where(up, GROUP - shift, shift - GROUP)
        inside = jnp.logical_and(source >= 0, source < GROUP)
        place_of = jnp.where(inside, jnp.bitwise_xor(seat, source), 0)
        return inside, place_of, jnp.where(up, factor + 1.0, factor)

    most = None
    for mode in range(phonon_ref.shape[0]):
        inside, place_of, weight = gives(mode, upward)
        whole = product(phonon_ref[mode], bank[place_of])
        total[mode] = whole
        term = jnp.where(inside, weight, 0.0) * whole
        most = term if most is None else most + term
    _, _, weight = gives(far, jnp.logical_not(upward))
    less = weight * total[far]
    total[0] = most
    total[1] = less
    for mode in range(phonon_ref.shape[0]):
        inside, place_of, weight = gives(mode, jnp.logical_not(upward))

        @pl.when(jnp.logical_and(mode != far, inside))
        def _(mode=mode, place_of=place_of, weight=weight):
            total[1] += product(phonon_ref[mode], bank[place_of], weight)

    most_first = upward == (first_side(group) > 0)
    first_out[...] = bf(total[jnp.where(most_first, 0, 1)])
    second_out[...] = bf(total[jnp.where(most_first, 1, 0)])


def column_terms(first_ref, second_ref, phonon_ref, offsets_ref, bose_ref, out):
    _, group, _ = place()
    side = first_side(group)
    far, _, _ = modes_of(offsets_ref)
    factor = bose_ref[far]
    first_weight = jnp.where(side > 0, factor, factor + 1.0)
    second_weight = jnp.where(side > 0, factor + 1.0, factor)
    block = mixed(first_ref[...], first_weight, second_ref[...], second_weight)
    out[...] = product(phonon_ref[far], block)


def group_terms(*refs):
    parts, (phonon_ref, offsets_ref, bose_ref, out, bank) = refs[: GROUP - 1], refs[GROUP - 1 :]
    _, _, seat = place()
    for j, part in enumerate(parts):
        bank[j] = part[...]
    _, *others = modes_of(offsets_ref)
    sum_of_modes = None
    for mode in others:
        shift, factor = offsets_ref[mode], bose_ref[mode]
        below, above = seat - shift, seat + shift
        has_below, has_above = below >= 0, above < GROUP
        first = jnp.where(has_below, jnp.bitwise_xor(seat, below) - 1, 0)
        second = jnp.where(has_above, jnp.bitwise_xor(seat, above) - 1, 0)
        block = mixed(
            bank[first],
            jnp.where(has_below, factor + 1.0, 0.0),
            bank[second],
            jnp.where(has_above, factor, 0.0),
        )
        term = product(phonon_ref[mode], block)
        sum_of_modes = term if sum_of_modes is None else sum_of_modes + term
    out[...] = sum_of_modes


def add_lines(a, b, out):
    out[...] = a[...] + b[...]


def column_sums(energies, first_ref, dos_ref, pair_out, dos_first_out):
    energy, group, _ = place()
    terms = -holes_at(energy + GROUP * first_side(group), energies, dos_ref.shape)
    terms = terms * diagonal_of(first_ref)
    dos_first_out[...] = terms
    pair_out[...] = terms + dos_ref[...]


def sums_before(*refs):
    *received, out = refs
    _, group, _ = place()
    line = jnp.zeros(out.shape, jnp.float32)
    for power, part in enumerate(received):
        line = line + jnp.where(jnp.bitwise_and(group, 1 << power) > 0, part[...], 0.0)
    out[...] = line


def last_sum(*refs):
    real_total, imag_total, first, second, before, dos = refs[:6]
    *seats, out, cumulative = refs[6:]
    m = real_total.shape[0]
    out[:, :m] = bf(real_total[...] + f32(first[...]) + f32(second[...]))
    imag = imag_total[...]
    line = before[...] + dos[...]
    for part in seats:
        imag = imag + f32(part[:m])
        line = line + jnp.sum(f32(part[m:]), axis=0, keepdims=True)
    out[:, m:] = bf(imag)
    cumulative[...] = line


def across_seats(value, j):
    energies = lax.axis_size("energy")
    return lax.ppermute(value, "energy", [(e, e ^ j) for e in range(energies)])


def across_groups(value, partner):
    groups = lax.axis_size("energy") // GROUP
    pairs = [(group, partner(group)) for group in range(groups)]
    return lax.ppermute(
        value,
        "energy",
        [(GROUP * a + i, GROUP * b + i) for a, b in pairs if 0 <= b < groups for i in range(GROUP)],
    )


def first_pair(group):
    return group ^ 1


def second_pair(group):
    return ((group + 1) ^ 1) - 1


def body(green_local, coupling, phonon_coupling, offsets, bose_factors):
    g = green_local[0]
    m = g.shape[0]
    groups = lax.axis_size("energy") // GROUP
    half = jax.ShapeDtypeStruct((m, m), jnp.bfloat16)
    taller = jax.ShapeDtypeStruct((m + 16, m), jnp.bfloat16)
    wide = jax.ShapeDtypeStruct((m, m), jnp.float32)
    line = jax.ShapeDtypeStruct((1, m), jnp.float32)
    modes = [phonon_coupling, offsets, bose_factors]

    def bank(blocks):
        return pltpu.VMEM((blocks, m, m), jnp.bfloat16)

    def totals(blocks):
        return pltpu.VMEM((blocks, m, m), jnp.float32)

    real, imag, dos = greens_halves(g, coupling)
    first_imag = across_groups(imag, first_pair)
    second_imag = across_groups(imag, second_pair)
    reals = [real] + [across_seats(real, j) for j in range(1, GROUP)]

    group_sum, dos_first = call(
        functools.partial(column_sums, lax.axis_size("energy")), [line, line], [first_imag, dos]
    )
    received = [dos_first]
    step = 2
    while step < groups:
        if step > 2:
            (group_sum,) = call(add_lines, [line], [group_sum, received[-1]])
        received.append(across_groups(group_sum, lambda a, step=step: a ^ step))
        step *= 2
    (imag_total,) = call(column_terms, [wide], [first_imag, second_imag, *modes])
    (before,) = call(sums_before, [line], received)

    sums = call(
        to_seats,
        [taller] * (GROUP - 1),
        [imag, first_imag, second_imag, *modes, dos, before],
        [bank(3), totals(GROUP // 2)],
    )
    seat_terms = [across_seats(value, j) for j, value in enumerate(sums, 1)]

    reals[0], _ = lax.optimization_barrier((reals[0], sums[0]))
    first_out, second_out = call(
        to_groups, [half, half], [*reals, *modes], [bank(GROUP), totals(len(offsets))]
    )
    first_term = across_groups(first_out, first_pair)
    second_term = across_groups(second_out, second_pair)
    (real_total,) = call(group_terms, [wide], [*reals[1:], *modes], [bank(GROUP - 1)])

    sigma, cumulative = call(
        last_sum,
        [jax.ShapeDtypeStruct(g.shape, jnp.bfloat16), line],
        [real_total, imag_total, first_term, second_term, before, dos, *seat_terms],
    )
    return sigma[None], cumulative


def solution(mesh):
    in_specs = (P("energy", "slab", None), P("slab", None), P(), P(), P())
    out_specs = (P("energy", "slab", None), P("energy", "slab"))
    return jax.shard_map(body, mesh=mesh, in_specs=in_specs, out_specs=out_specs, check_vma=False)
```

time: 59.3 us -> 43.2 us (0.73)
  the two profiles are of different devices: /device:TPU:0 before, /device:TPU:10 now
where the time goes in v2:
time: 43.2 us; the launch traced here: 42.7 us
  starting transfers between devices  20.6 us (48%)
  Pallas kernels  12.1 us (28%)
  waiting for transfers between devices  8.65 us (20%)
  between operations  0.76 us (2%)
  local copies, waits for them, and re-layouts  0.66 us (2%)
    pallas_call x9, Pallas kernels, call(): pl.pallas_call(kernel, out_shape=outs, in_specs=[SCALARS if i.ndim == 1 e...  12.1 us
    ppermute x5, starting transfers between devices, across_groups(): lax.ppermute(value, 'energy', [(GROUP * a + i, GROUP * b + i) for a, b in...  11 us
    ppermute x6, starting transfers between devices, across_seats(): return lax.ppermute(value, 'energy', [(e, e ^ j) for e in range(energies)])  7.11 us
    ppermute x5, waiting for transfers between devices, across_groups(): lax.ppermute(value, 'energy', [(GROUP * a + i, GROUP * b + i) for a, b in...  5.19 us
    ppermute x1, starting transfers between devices, greens_halves(): below = lax.ppermute(coupling, 'slab', up)  2.41 us
    ppermute x6, waiting for transfers between devices, across_seats(): return lax.ppermute(value, 'energy', [(e, e ^ j) for e in range(energies)])  2.11 us
    ppermute x1, waiting for transfers between devices, greens_halves(): below = lax.ppermute(coupling, 'slab', up)  1.35 us
  transfers between devices with their start and end apart: 13, of which 7 were waited for; matrix products, arithmetic and copies ran while one was open for 0% of the time, Pallas kernels for 19%

profile of v2, /device:TPU:10, one launch (start us, length us, event | category | flops | bytes accessed | tf_op | source)
XLA Modules:
  0.0 42.7 jit_solution(15676224593287292745)
XLA Ops:
  0.6 0.1 collective-permute-start
  0.7 2.4 %collective-permute-start.1 = (bf16[384,384]{1,0:T(8,128)(2,1)}, bf16[384,384]{1,0:T(8,128)(2,1)S(1)}, u32[]{:S(2)}, u32[]{:S(2)}) collective-permute-start(bf16[384,384]{1,0:T(8,128)(2,1)} %own_ref.1), channel_id=1, source_target_pairs={{0,1},{2,3},{4,5},{6,7},{8,9},{10,11},{12,13},{14,15},{16,17},{18,... | collective-permute-start | bytes 884744 | tf_op jit(solution)/shard_map/ppermute | solution.py:135
  3.2 0.0 copy-start
  3.2 1.3 %collective-permute-done.1.below_ref = bf16[384,384]{1,0:T(8,128)(2,1)S(1)} collective-permute-done((bf16[384,384]{1,0:T(8,128)(2,1)}, bf16[384,384]{1,0:T(8,128)(2,1)S(1)}, u32[]{:S(2)}, u32[]{:S(2)}) %collective-permute-start.1) | collective-permute-done | bytes 294944 | tf_op jit(solution)/shard_map/ppermute | solution.py:135
  4.5 0.0 collective-permute-done.other_ref
  4.5 2.7 %shard_map.69 = (bf16[384,384]{1,0:T(8,128)(2,1)S(1)}, bf16[384,384]{1,0:T(8,128)(2,1)S(1)}, f32[1,384]{1,0:T(1,128)S(1)}) custom-call(bf16[384,768]{1,0:T(8,128)(2,1)S(1)} %bitcast.3, bf16[384,768]{1,0:T(8,128)(2,1)S(1)} %collective-permute-done.other_ref, bf16[384,384]{1,0:T(8,128)(2,1)S(1)} %copy-done.2, ...), custom_call_target="tpu_custom_call" | custom-call | tf_op jit(solution)/shard_map/pallas_call | solution.py:39
  7.3 0.5 %collective-permute-start.5 = (bf16[384,384]{1,0:T(8,128)(2,1)S(1)}, bf16[384,384]{1,0:T(8,128)(2,1)S(1)}, u32[]{:S(2)}, u32[]{:S(2)}) collective-permute-start(bf16[384,384]{1,0:T(8,128)(2,1)S(1)} %get-tuple-element.16.own_ref), channel_id=1, source_target_pairs={{0,8},{2,10},{4,12},{6,14},{8,0},{10,2},{12,4},{14,6},{16,24},{18,... | collective-permute-start | bytes 884744 | tf_op jit(solution)/shard_map/ppermute | solution.py:353
  7.8 4.6 %collective-permute-start.6 = (bf16[384,384]{1,0:T(8,128)(2,1)S(1)}, bf16[384,384]{1,0:T(8,128)(2,1)S(1)}, u32[]{:S(2)}, u32[]{:S(2)}) collective-permute-start(bf16[384,384]{1,0:T(8,128)(2,1)S(1)} %get-tuple-element.16.own_ref), channel_id=1, source_target_pairs={{8,16},{10,18},{12,20},{14,22},{16,8},{18,10},{20,12},{22,14},{9,1... | collective-permute-start | bytes 884744 | tf_op jit(solution)/shard_map/ppermute | solution.py:353
  12.4 0.6 %collective-permute-start.2 = (bf16[384,384]{1,0:T(8,128)(2,1)S(1)}, bf16[384,384]{1,0:T(8,128)(2,1)S(1)}, u32[]{:S(2)}, u32[]{:S(2)}) collective-permute-start(bf16[384,384]{1,0:T(8,128)(2,1)S(1)} %get-tuple-element.21.refs_0_), channel_id=1, source_target_pairs={{0,2},{2,0},{4,6},{6,4},{8,10},{10,8},{12,14},{14,12},{16,18},{18,... | collective-permute-start | bytes 884744 | tf_op jit(solution)/shard_map/ppermute | solution.py:347
  13.0 1.5 %collective-permute-start.3 = (bf16[384,384]{1,0:T(8,128)(2,1)S(1)}, bf16[384,384]{1,0:T(8,128)(2,1)S(1)}, u32[]{:S(2)}, u32[]{:S(2)}) collective-permute-start(bf16[384,384]{1,0:T(8,128)(2,1)S(1)} %get-tuple-element.21.refs_0_), channel_id=1, source_target_pairs={{0,4},{2,6},{4,0},{6,2},{8,12},{10,14},{12,8},{14,10},{16,20},{18,... | collective-permute-start | bytes 884744 | tf_op jit(solution)/shard_map/ppermute | solution.py:347
  14.5 1.4 %collective-permute-start.4 = (bf16[384,384]{1,0:T(8,128)(2,1)S(1)}, bf16[384,384]{1,0:T(8,128)(2,1)S(1)}, u32[]{:S(2)}, u32[]{:S(2)}) collective-permute-start(bf16[384,384]{1,0:T(8,128)(2,1)S(1)} %get-tuple-element.21.refs_0_), channel_id=1, source_target_pairs={{0,6},{2,4},{4,2},{6,0},{8,14},{10,12},{12,10},{14,8},{16,22},{18,... | collective-permute-start | bytes 884744 | tf_op jit(solution)/shard_map/ppermute | solution.py:347
  16.0 0.7 %collective-permute-done.5.first_ref = bf16[384,384]{1,0:T(8,128)(2,1)S(1)} collective-permute-done((bf16[384,384]{1,0:T(8,128)(2,1)S(1)}, bf16[384,384]{1,0:T(8,128)(2,1)S(1)}, u32[]{:S(2)}, u32[]{:S(2)}) %collective-permute-start.5) | collective-permute-done | bytes 294944 | tf_op jit(solution)/shard_map/ppermute | solution.py:353
  16.7 2.6 %collective-permute-start.7 = (f32[1,384]{1,0:T(1,128)S(1)}, f32[1,384]{1,0:T(1,128)S(1)}, u32[]{:S(2)}, u32[]{:S(2)}) collective-permute-start(f32[1,384]{1,0:T(1,128)S(1)} %get-tuple-element.19), channel_id=1, source_target_pairs={{0,16},{2,18},{4,20},{6,22},{8,24},{10,26},{12,28},{14,30},{16,0},... | collective-permute-start | bytes 4616 | tf_op jit(solution)/shard_map/ppermute | solution.py:353
  19.3 1.9 %collective-permute-done.7.refs_1_ = f32[1,384]{1,0:T(1,128)S(1)} collective-permute-done((f32[1,384]{1,0:T(1,128)S(1)}, f32[1,384]{1,0:T(1,128)S(1)}, u32[]{:S(2)}, u32[]{:S(2)}) %collective-permute-start.7) | collective-permute-done | bytes 1568 | tf_op jit(solution)/shard_map/ppermute | solution.py:353
  21.3 0.0 collective-permute-done.6.second_ref
  21.3 0.6 %copy-done.3 = s32[3]{0:T(128)S(1)} copy-done((s32[3]{0:T(128)S(1)}, s32[3]{0:T(128)}, u32[]{:S(2)}) %copy-start.3) | copy-done | bytes 36
  21.9 0.0 copy-done.4
  21.9 2.4 %shard_map.74 = (bf16[400,384]{1,0:T(8,128)(2,1)S(1)}, bf16[400,384]{1,0:T(8,128)(2,1)S(1)}, bf16[400,384]{1,0:T(8,128)(2,1)S(1)}) custom-call(bf16[384,384]{1,0:T(8,128)(2,1)S(1)} %get-tuple-element.16.own_ref, bf16[384,384]{1,0:T(8,128)(2,1)S(1)} %collective-permute-done.5.first_ref, bf16[384,384]{1,0:T(8,128)(2,1)S(1)} %collective-permute-done.6.second_ref, ...), custom_call_target="tpu_custom_call" | custom-call | tf_op jit(solution)/shard_map/pallas_call | solution.py:39
  24.3 0.6 %collective-permute-start.10 = (bf16[400,384]{1,0:T(8,128)(2,1)S(1)}, bf16[400,384]{1,0:T(8,128)(2,1)S(1)}, u32[]{:S(2)}, u32[]{:S(2)}) collective-permute-start(bf16[400,384]{1,0:T(8,128)(2,1)S(1)} %get-tuple-element.20), channel_id=1, source_target_pairs={{0,2},{2,0},{4,6},{6,4},{8,10},{10,8},{12,14},{14,12},{16,18},{18,... | collective-permute-start | bytes 921608 | tf_op jit(solution)/shard_map/ppermute | solution.py:347
  24.9 1.5 %collective-permute-start.11 = (bf16[400,384]{1,0:T(8,128)(2,1)S(1)}, bf16[400,384]{1,0:T(8,128)(2,1)S(1)}, u32[]{:S(2)}, u32[]{:S(2)}) collective-permute-start(bf16[400,384]{1,0:T(8,128)(2,1)S(1)} %get-tuple-element.24), channel_id=1, source_target_pairs={{0,4},{2,6},{4,0},{6,2},{8,12},{10,14},{12,8},{14,10},{16,20},{18,... | collective-permute-start | bytes 921608 | tf_op jit(solution)/shard_map/ppermute | solution.py:347
  26.4 1.5 %collective-permute-start.12 = (bf16[400,384]{1,0:T(8,128)(2,1)S(1)}, bf16[400,384]{1,0:T(8,128)(2,1)S(1)}, u32[]{:S(2)}, u32[]{:S(2)}) collective-permute-start(bf16[400,384]{1,0:T(8,128)(2,1)S(1)} %get-tuple-element.25), channel_id=1, source_target_pairs={{0,6},{2,4},{4,2},{6,0},{8,14},{10,12},{12,10},{14,8},{16,22},{18,... | collective-permute-start | bytes 921608 | tf_op jit(solution)/shard_map/ppermute | solution.py:347
  27.9 1.8 %collective-permute-done.4.refs_2_.refs_3_ = bf16[384,384]{1,0:T(8,128)(2,1)S(1)} collective-permute-done((bf16[384,384]{1,0:T(8,128)(2,1)S(1)}, bf16[384,384]{1,0:T(8,128)(2,1)S(1)}, u32[]{:S(2)}, u32[]{:S(2)}) %collective-permute-start.4) | collective-permute-done | bytes 294944 | tf_op jit(solution)/shard_map/ppermute | solution.py:347
  29.7 2.9 %shard_map.75 = (bf16[384,384]{1,0:T(8,128)(2,1)S(1)}, bf16[384,384]{1,0:T(8,128)(2,1)S(1)}) custom-call(bf16[384,384]{1,0:T(8,128)(2,1)S(1)} %get-tuple-element.21.refs_0_, bf16[384,384]{1,0:T(8,128)(2,1)S(1)} %collective-permute-done.2.refs_0_.refs_1_, bf16[384,384]{1,0:T(8,128)(2,1)S(1)} %collective-permute-done.3.refs_1_.refs_2_, ...), custom_call_target="tpu_custom_call" | custom-call | tf_op jit(solution)/shard_map/pallas_call | solution.py:39
  32.6 0.1 collective-permute-start.8
  32.7 3.2 %collective-permute-start.9 = (bf16[384,384]{1,0:T(8,128)(2,1)S(1)}, bf16[384,384]{1,0:T(8,128)(2,1)S(1)}, u32[]{:S(2)}, u32[]{:S(2)}) collective-permute-start(bf16[384,384]{1,0:T(8,128)(2,1)S(1)} %get-tuple-element.23), channel_id=1, source_target_pairs={{8,16},{10,18},{12,20},{14,22},{16,8},{18,10},{20,12},{22,14},{9,1... | collective-permute-start | bytes 884744 | tf_op jit(solution)/shard_map/ppermute | solution.py:353
  35.9 1.6 %shard_map.70.refs_0_ = f32[384,384]{1,0:T(8,128)S(1)} custom-call(bf16[384,384]{1,0:T(8,128)(2,1)S(1)} %collective-permute-done.2.refs_0_.refs_1_, bf16[384,384]{1,0:T(8,128)(2,1)S(1)} %collective-permute-done.3.refs_1_.refs_2_, bf16[384,384]{1,0:T(8,128)(2,1)S(1)} %collective-permute-done.4.refs_2_.refs_3_, bf16[3,384,384]{2,1,0:T(8,128)(2,1)S(1)} %copy-done, ...), custom_call_target="tpu_custom_call" | custom-call | tf_op jit(solution)/shard_map/pallas_call | solution.py:39
  37.6 1.2 %shard_map.71.refs_1_ = f32[384,384]{1,0:T(8,128)S(1)} custom-call(bf16[384,384]{1,0:T(8,128)(2,1)S(1)} %collective-permute-done.5.first_ref, bf16[384,384]{1,0:T(8,128)(2,1)S(1)} %collective-permute-done.6.second_ref, bf16[3,384,384]{2,1,0:T(8,128)(2,1)S(1)} %copy-done, s32[3]{0:T(128)S(1)} %copy-done.3, f32[3]{0:T(128)S(1)} %copy-done.4), custom_call_target="tpu_custom_call" | custom-call | tf_op jit(solution)/shard_map/pallas_call | solution.py:39
  38.8 0.7 %collective-permute-done.8.refs_2_ = bf16[384,384]{1,0:T(8,128)(2,1)S(1)} collective-permute-done((bf16[384,384]{1,0:T(8,128)(2,1)S(1)}, bf16[384,384]{1,0:T(8,128)(2,1)S(1)}, u32[]{:S(2)}, u32[]{:S(2)}) %collective-permute-start.8) | collective-permute-done | bytes 294944 | tf_op jit(solution)/shard_map/ppermute | solution.py:353
  39.4 1.9 %collective-permute-done.9.refs_3_ = bf16[384,384]{1,0:T(8,128)(2,1)S(1)} collective-permute-done((bf16[384,384]{1,0:T(8,128)(2,1)S(1)}, bf16[384,384]{1,0:T(8,128)(2,1)S(1)}, u32[]{:S(2)}, u32[]{:S(2)}) %collective-permute-start.9) | collective-permute-done | bytes 294944 | tf_op jit(solution)/shard_map/ppermute | solution.py:353
  41.3 0.0 collective-permute-done.11.refs_7_
  41.3 0.3 collective-permute-done.12.refs_8_
  41.7 1.1 %shard_map.76 = (bf16[384,768]{1,0:T(8,128)(2,1)}, f32[1,384]{1,0:T(1,128)}) custom-call(f32[384,384]{1,0:T(8,128)S(1)} %shard_map.70.refs_0_, f32[384,384]{1,0:T(8,128)S(1)} %shard_map.71.refs_1_, bf16[384,384]{1,0:T(8,128)(2,1)S(1)} %collective-permute-done.8.refs_2_, bf16[384,384]{1,0:T(8,128)(2,1)S(1)} %collective-permute-done.9.refs_3_, ...), custom_call_target="tpu_custom_call" | custom-call | tf_op jit(solution)/shard_map/pallas_call | solution.py:39
  (13 shorter events, 0.1 us)
Async XLA Ops:
  0.6 3.9 %copy-start.1 = (bf16[1,384,768]{2,1,0:T(8,128)(2,1)S(1)}, bf16[1,384,768]{2,1,0:T(8,128)(2,1)}, u32[]{:S(2)}) copy-start(bf16[1,384,768]{2,1,0:T(8,128)(2,1)} %param.5) | copy-start | bytes 1769476
  0.6 3.9 %copy-start.2 = (bf16[384,384]{1,0:T(8,128)(2,1)S(1)}, bf16[384,384]{1,0:T(8,128)(2,1)}, u32[]{:S(2)}) copy-start(bf16[384,384]{1,0:T(8,128)(2,1)} %own_ref.1) | copy-start | bytes 884740
  0.6 3.9 %collective-permute-start = (bf16[384,768]{1,0:T(8,128)(2,1)}, bf16[384,768]{1,0:T(8,128)(2,1)S(1)}, u32[]{:S(2)}, u32[]{:S(2)}) collective-permute-start(bf16[384,768]{1,0:T(8,128)(2,1)} %bitcast.2), channel_id=1, source_target_pairs={{0,1},{1,0},{2,3},{3,2},{4,5},{5,4},{6,7},{7,6},{8,9},{9,8},{10,11... | collective-permute-start | bytes 1769480 | tf_op jit(solution)/shard_map/ppermute | solution.py:139
  0.7 3.8 %collective-permute-start.1 = (bf16[384,384]{1,0:T(8,128)(2,1)}, bf16[384,384]{1,0:T(8,128)(2,1)S(1)}, u32[]{:S(2)}, u32[]{:S(2)}) collective-permute-start(bf16[384,384]{1,0:T(8,128)(2,1)} %own_ref.1), channel_id=1, source_target_pairs={{0,1},{2,3},{4,5},{6,7},{8,9},{10,11},{12,13},{14,15},{16,17},{18,... | collective-permute-start | bytes 884744 | tf_op jit(solution)/shard_map/ppermute | solution.py:135
  3.2 18.1 %copy-start = (bf16[3,384,384]{2,1,0:T(8,128)(2,1)S(1)}, bf16[3,384,384]{2,1,0:T(8,128)(2,1)}, u32[]{:S(2)}) copy-start(bf16[3,384,384]{2,1,0:T(8,128)(2,1)} %refs_4_.3) | copy-start | bytes 2654212
  7.3 9.4 %collective-permute-start.5 = (bf16[384,384]{1,0:T(8,128)(2,1)S(1)}, bf16[384,384]{1,0:T(8,128)(2,1)S(1)}, u32[]{:S(2)}, u32[]{:S(2)}) collective-permute-start(bf16[384,384]{1,0:T(8,128)(2,1)S(1)} %get-tuple-element.16.own_ref), channel_id=1, source_target_pairs={{0,8},{2,10},{4,12},{6,14},{8,0},{10,2},{12,4},{14,6},{16,24},{18,... | collective-permute-start | bytes 884744 | tf_op jit(solution)/shard_map/ppermute | solution.py:353
  7.8 13.5 %collective-permute-start.6 = (bf16[384,384]{1,0:T(8,128)(2,1)S(1)}, bf16[384,384]{1,0:T(8,128)(2,1)S(1)}, u32[]{:S(2)}, u32[]{:S(2)}) collective-permute-start(bf16[384,384]{1,0:T(8,128)(2,1)S(1)} %get-tuple-element.16.own_ref), channel_id=1, source_target_pairs={{8,16},{10,18},{12,20},{14,22},{16,8},{18,10},{20,12},{22,14},{9,1... | collective-permute-start | bytes 884744 | tf_op jit(solution)/shard_map/ppermute | solution.py:353
  12.4 14.0 %collective-permute-start.2 = (bf16[384,384]{1,0:T(8,128)(2,1)S(1)}, bf16[384,384]{1,0:T(8,128)(2,1)S(1)}, u32[]{:S(2)}, u32[]{:S(2)}) collective-permute-start(bf16[384,384]{1,0:T(8,128)(2,1)S(1)} %get-tuple-element.21.refs_0_), channel_id=1, source_target_pairs={{0,2},{2,0},{4,6},{6,4},{8,10},{10,8},{12,14},{14,12},{16,18},{18,... | collective-permute-start | bytes 884744 | tf_op jit(solution)/shard_map/ppermute | solution.py:347
  13.0 14.9 %collective-permute-start.3 = (bf16[384,384]{1,0:T(8,128)(2,1)S(1)}, bf16[384,384]{1,0:T(8,128)(2,1)S(1)}, u32[]{:S(2)}, u32[]{:S(2)}) collective-permute-start(bf16[384,384]{1,0:T(8,128)(2,1)S(1)} %get-tuple-element.21.refs_0_), channel_id=1, source_target_pairs={{0,4},{2,6},{4,0},{6,2},{8,12},{10,14},{12,8},{14,10},{16,20},{18,... | collective-permute-start | bytes 884744 | tf_op jit(solution)/shard_map/ppermute | solution.py:347
  14.5 15.1 %collective-permute-start.4 = (bf16[384,384]{1,0:T(8,128)(2,1)S(1)}, bf16[384,384]{1,0:T(8,128)(2,1)S(1)}, u32[]{:S(2)}, u32[]{:S(2)}) collective-permute-start(bf16[384,384]{1,0:T(8,128)(2,1)S(1)} %get-tuple-element.21.refs_0_), channel_id=1, source_target_pairs={{0,6},{2,4},{4,2},{6,0},{8,14},{10,12},{12,10},{14,8},{16,22},{18,... | collective-permute-start | bytes 884744 | tf_op jit(solution)/shard_map/ppermute | solution.py:347
  16.7 4.5 %collective-permute-start.7 = (f32[1,384]{1,0:T(1,128)S(1)}, f32[1,384]{1,0:T(1,128)S(1)}, u32[]{:S(2)}, u32[]{:S(2)}) collective-permute-start(f32[1,384]{1,0:T(1,128)S(1)} %get-tuple-element.19), channel_id=1, source_target_pairs={{0,16},{2,18},{4,20},{6,22},{8,24},{10,26},{12,28},{14,30},{16,0},... | collective-permute-start | bytes 4616 | tf_op jit(solution)/shard_map/ppermute | solution.py:353
  21.3 0.7 %copy-start.3 = (s32[3]{0:T(128)S(1)}, s32[3]{0:T(128)}, u32[]{:S(2)}) copy-start(s32[3]{0:T(128)} %refs_5_.3) | copy-start | bytes 40
  21.3 0.7 %copy-start.4 = (f32[3]{0:T(128)S(1)}, f32[3]{0:T(128)}, u32[]{:S(2)}) copy-start(f32[3]{0:T(128)} %refs_6_.1) | copy-start | bytes 40
  24.3 17.0 %collective-permute-start.10 = (bf16[400,384]{1,0:T(8,128)(2,1)S(1)}, bf16[400,384]{1,0:T(8,128)(2,1)S(1)}, u32[]{:S(2)}, u32[]{:S(2)}) collective-permute-start(bf16[400,384]{1,0:T(8,128)(2,1)S(1)} %get-tuple-element.20), channel_id=1, source_target_pairs={{0,2},{2,0},{4,6},{6,4},{8,10},{10,8},{12,14},{14,12},{16,18},{18,... | collective-permute-start | bytes 921608 | tf_op jit(solution)/shard_map/ppermute | solution.py:347
  24.9 16.4 %collective-permute-start.11 = (bf16[400,384]{1,0:T(8,128)(2,1)S(1)}, bf16[400,384]{1,0:T(8,128)(2,1)S(1)}, u32[]{:S(2)}, u32[]{:S(2)}) collective-permute-start(bf16[400,384]{1,0:T(8,128)(2,1)S(1)} %get-tuple-element.24), channel_id=1, source_target_pairs={{0,4},{2,6},{4,0},{6,2},{8,12},{10,14},{12,8},{14,10},{16,20},{18,... | collective-permute-start | bytes 921608 | tf_op jit(solution)/shard_map/ppermute | solution.py:347
  26.4 15.2 %collective-permute-start.12 = (bf16[400,384]{1,0:T(8,128)(2,1)S(1)}, bf16[400,384]{1,0:T(8,128)(2,1)S(1)}, u32[]{:S(2)}, u32[]{:S(2)}) collective-permute-start(bf16[400,384]{1,0:T(8,128)(2,1)S(1)} %get-tuple-element.25), channel_id=1, source_target_pairs={{0,6},{2,4},{4,2},{6,0},{8,14},{10,12},{12,10},{14,8},{16,22},{18,... | collective-permute-start | bytes 921608 | tf_op jit(solution)/shard_map/ppermute | solution.py:347
  32.6 6.8 %collective-permute-start.8 = (bf16[384,384]{1,0:T(8,128)(2,1)S(1)}, bf16[384,384]{1,0:T(8,128)(2,1)S(1)}, u32[]{:S(2)}, u32[]{:S(2)}) collective-permute-start(bf16[384,384]{1,0:T(8,128)(2,1)S(1)} %get-tuple-element.22), channel_id=1, source_target_pairs={{0,8},{2,10},{4,12},{6,14},{8,0},{10,2},{12,4},{14,6},{16,24},{18,... | collective-permute-start | bytes 884744 | tf_op jit(solution)/shard_map/ppermute | solution.py:353
  32.7 8.6 %collective-permute-start.9 = (bf16[384,384]{1,0:T(8,128)(2,1)S(1)}, bf16[384,384]{1,0:T(8,128)(2,1)S(1)}, u32[]{:S(2)}, u32[]{:S(2)}) collective-permute-start(bf16[384,384]{1,0:T(8,128)(2,1)S(1)} %get-tuple-element.23), channel_id=1, source_target_pairs={{8,16},{10,18},{12,20},{14,22},{16,8},{18,10},{20,12},{22,14},{9,1... | collective-permute-start | bytes 884744 | tf_op jit(solution)/shard_map/ppermute | solution.py:353

commit v3 on v2

--- a/solution.py
+++ b/solution.py
@@ -9,6 +9,8 @@
 
 OMAX = 4
 GROUP = OMAX
+EXTRA = 16
+LANES = 128
 VMEM_LIMIT = 16 * 1024 * 1024
 
 WHOLE = pl.BlockSpec(memory_space=pltpu.VMEM)
@@ -35,13 +37,14 @@
     return value.astype(jnp.float32)
 
 
-def call(kernel, outs, ins, scratch=(), flops=0):
+def call(kernel, outs, ins, scratch=(), flops=0, aliases=None):
     return pl.pallas_call(
         kernel,
         out_shape=outs,
         in_specs=[SCALARS if i.ndim == 1 else WHOLE for i in ins],
         out_specs=[WHOLE] * len(outs),
         scratch_shapes=scratch,
+        input_output_aliases=aliases or {},
         compiler_params=pltpu.CompilerParams(vmem_limit_bytes=VMEM_LIMIT),
         cost_estimate=pl.CostEstimate(flops=flops, bytes_accessed=0, transcendentals=0),
     )(*ins)
@@ -74,8 +77,20 @@
     return 1.0 / (1.0 + jnp.exp(-((position + 0.5 - energies / 2) * 4.0 / energies)))
 
 
-def hole_line(energies, out):
-    out[...] = holes_at(lax.axis_index("energy"), energies, out.shape)
+def prepare(energies, offsets_ref, bose_ref, holes_out, places_out, factors_out):
+    assert offsets_ref.shape == (3,)
+    holes_out[...] = holes_at(lax.axis_index("energy"), energies, holes_out.shape)
+    far = jnp.where(offsets_ref[1] == GROUP, 1, jnp.where(offsets_ref[2] == GROUP, 2, 0))
+    one, two = jnp.where(far == 0, 1, 0), jnp.where(far == 2, 1, 2)
+    odd = jnp.where(lax.rem(offsets_ref[one], 2) == 1, one, two)
+    for row, mode in enumerate((far, odd, one + two - odd)):
+        places_out[row : row + 1] = jnp.full((1, LANES), mode, jnp.int32)
+        places_out[row + 3 : row + 4] = jnp.full((1, LANES), offsets_ref[mode], jnp.int32)
+        factors_out[row : row + 1] = jnp.full((1, LANES), bose_ref[mode], jnp.float32)
+
+
+def modes_of(phonon_ref, places_ref, factors_ref):
+    return [(places_ref[row, 0], places_ref[row + 3, 0], factors_ref[row, 0]) for row in range(3)]
 
 
 def diagonal_of(block_ref):
@@ -125,25 +140,32 @@
     finish(g, bf(complex_product(g, couple)), holes_ref, *outs)
 
 
-def greens_halves(g, coupling):
+def greens_halves(g, coupling, offsets, bose_factors):
     m = g.shape[0]
     slabs = lax.axis_size("slab")
     half = jax.ShapeDtypeStruct((m, m), jnp.bfloat16)
     line = jax.ShapeDtypeStruct((1, m), jnp.float32)
+    places = jax.ShapeDtypeStruct((8, LANES), jnp.int32)
+    factors = jax.ShapeDtypeStruct((8, LANES), jnp.float32)
     up = [(s, s + 1) for s in range(slabs - 1)]
     down = [(s + 1, s) for s in range(slabs - 1)]
     below = lax.ppermute(coupling, "slab", up)
     energies = lax.axis_size("energy")
-    (holes,) = call(functools.partial(hole_line, energies), [line], [], flops=24 * m**3)
+    holes, *table = call(
+        functools.partial(prepare, energies),
+        [line, places, factors],
+        [offsets, bose_factors],
+        flops=24 * m**3,
+    )
     if slabs == 2:
         other = lax.ppermute(g, "slab", up + down)
         couple = [pltpu.VMEM(g.shape, jnp.bfloat16)]
         ins = [g, other, coupling, below, holes]
-        return call(greens_of_pair, [half, half, line], ins, couple)
+        return *call(greens_of_pair, [half, half, line], ins, couple), table
     above = lax.ppermute(g, "slab", down)
     lower = lax.ppermute(g, "slab", up)
     ins = [g, above, lower, coupling, below, holes]
-    return call(greens_of_chain, [half, half, line], ins)
+    return *call(greens_of_chain, [half, half, line], ins), table
 
 
 def place():
@@ -166,22 +188,16 @@
     return bf(first_weight * f32(first) + second_weight * f32(second))
 
 
-def modes_of(offsets_ref):
-    assert offsets_ref.shape == (3,)
-    far = jnp.where(offsets_ref[1] == GROUP, 1, jnp.where(offsets_ref[2] == GROUP, 2, 0))
-    return far, jnp.where(far == 0, 1, 0), jnp.where(far == 2, 1, 2)
-
-
 def split_rows(line):
     high = bf(line)
     rest = line - f32(high)
     middle = bf(rest)
     low = bf(rest - f32(middle))
-    rows = [f32(high), f32(middle), f32(low), jnp.zeros((13, line.shape[1]), jnp.float32)]
+    rows = [f32(high), f32(middle), f32(low), jnp.zeros((EXTRA - 3, line.shape[1]), jnp.float32)]
     return bf(jnp.concatenate(rows, axis=0))
 
 
-def to_seats(own_ref, first_ref, second_ref, phonon_ref, offsets_ref, bose_ref, dos_ref, before_ref, *rest):
+def to_seats(own_ref, first_ref, second_ref, phonon_ref, places_ref, factors_ref, *rest):
     *outs, bank, total = rest
     m = own_ref.shape[0]
     _, group, seat = place()
@@ -189,9 +205,7 @@
     bank[0] = own_ref[...]
     bank[1] = first_ref[...]
     bank[2] = second_ref[...]
-    _, one, two = modes_of(offsets_ref)
-    odd = jnp.where(lax.rem(offsets_ref[one], 2) == 1, one, two)
-    left = one + two - odd
+    _, odd, left = modes_of(phonon_ref, places_ref, factors_ref)
 
     def towards(j):
         apart = jnp.bitwise_xor(seat, j) - seat
@@ -199,99 +213,107 @@
         beside = jnp.where(upward == (side > 0), 1, 2)
         return jnp.abs(apart), upward, beside
 
-    def single(j, mode):
-        size, upward, beside = towards(j)
-        shift, factor = offsets_ref[mode], bose_ref[mode]
-        own = shift == size
-        weight = jnp.where(own == upward, factor + 1.0, factor)
-        return product(phonon_ref[mode], bank[jnp.where(own, 0, beside)], weight)
-
-    for j in range(1, GROUP, 2):
-        total[j // 2] = single(j, odd)
-
-    @pl.when(lax.rem(offsets_ref[left], 2) == 0)
+    def odd_seats(mode):
+        index, shift, factor = mode
+        blocks, weights = [], []
+        for j in range(1, GROUP, 2):
+            size, upward, beside = towards(j)
+            own = shift == size
+            blocks.append(bank[jnp.where(own, 0, beside)])
+            weights.append(jnp.where(own == upward, factor + 1.0, factor))
+        matrix = phonon_ref[index]
+        wide = nn(matrix, jnp.concatenate(blocks, axis=1))
+        parts = [bf(w * wide[:, i * m : (i + 1) * m]) for i, w in enumerate(weights)]
+        return nt(jnp.concatenate(parts, axis=0), matrix)
+
+    total[...] = odd_seats(odd)
+    index, shift, factor = left
+
+    @pl.when(lax.rem(shift, 2) == 0)
     def _():
-        for j in range(1, GROUP, 2):
-            outs[j - 1][:m] = bf(total[j // 2])
-        factor = bose_ref[left]
         for j in range(2, GROUP, 2):
             _, upward, beside = towards(j)
             own_weight = jnp.where(upward, factor + 1.0, factor)
             beside_weight = jnp.where(upward, factor, factor + 1.0)
             block = mixed(bank[0], own_weight, bank[beside], beside_weight)
-            outs[j - 1][:m] = bf(product(phonon_ref[left], block))
-
-    @pl.when(lax.rem(offsets_ref[left], 2) == 1)
+            outs[j - 1][:m] = bf(product(phonon_ref[index], block))
+
+    @pl.when(lax.rem(shift, 2) == 1)
     def _():
-        for j in range(1, GROUP, 2):
-            outs[j - 1][:m] = bf(total[j // 2] + single(j, left))
+        total[...] += odd_seats(left)
         for j in range(2, GROUP, 2):
             outs[j - 1][:m] = jnp.zeros((m, m), jnp.bfloat16)
 
-    for j, out in enumerate(outs, 1):
+    for j in range(1, GROUP, 2):
+        outs[j - 1][:m] = bf(total[j // 2 * m : (j // 2 + 1) * m])
+        outs[j - 1][m:] = jnp.zeros((EXTRA, m), jnp.bfloat16)
+    for j in range(2, GROUP, 2):
+        outs[j - 1][m:] = jnp.zeros((EXTRA, m), jnp.bfloat16)
+
+
+def with_lines(dos_ref, before_ref, *refs):
+    m = dos_ref.shape[1]
+    _, _, seat = place()
+    for j, out in enumerate(refs[GROUP - 1 :], 1):
         counts = jnp.bitwise_xor(seat, j) > seat
         out[m:] = split_rows(before_ref[...] + jnp.where(counts, dos_ref[...], 0.0))
 
 
 def to_groups(*refs):
-    parts, (phonon_ref, offsets_ref, bose_ref) = refs[:GROUP], refs[GROUP : GROUP + 3]
+    parts, (phonon_ref, places_ref, factors_ref) = refs[:GROUP], refs[GROUP : GROUP + 3]
     first_out, second_out, bank, total = refs[GROUP + 3 :]
     _, group, seat = place()
     upward = seat < GROUP // 2
     for j, part in enumerate(parts):
         bank[j] = part[...]
-    far, _, _ = modes_of(offsets_ref)
-
-    def gives(mode, up):
-        shift, factor = offsets_ref[mode], bose_ref[mode]
+    modes = modes_of(phonon_ref, places_ref, factors_ref)
+
+    def gives(shift, factor, up):
         source = seat + jnp.where(up, GROUP - shift, shift - GROUP)
         inside = jnp.logical_and(source >= 0, source < GROUP)
         place_of = jnp.where(inside, jnp.bitwise_xor(seat, source), 0)
         return inside, place_of, jnp.where(up, factor + 1.0, factor)
 
-    most = None
-    for mode in range(phonon_ref.shape[0]):
-        inside, place_of, weight = gives(mode, upward)
-        whole = product(phonon_ref[mode], bank[place_of])
-        total[mode] = whole
+    most = less = None
+    for index, shift, factor in modes:
+        inside, place_of, weight = gives(shift, factor, upward)
+        whole = product(phonon_ref[index], bank[place_of])
         term = jnp.where(inside, weight, 0.0) * whole
-        most = term if most is None else most + term
-    _, _, weight = gives(far, jnp.logical_not(upward))
-    less = weight * total[far]
+        if most is None:
+            most, less = term, gives(shift, factor, jnp.logical_not(upward))[2] * whole
+        else:
+            most = most + term
     total[0] = most
     total[1] = less
-    for mode in range(phonon_ref.shape[0]):
-        inside, place_of, weight = gives(mode, jnp.logical_not(upward))
-
-        @pl.when(jnp.logical_and(mode != far, inside))
-        def _(mode=mode, place_of=place_of, weight=weight):
-            total[1] += product(phonon_ref[mode], bank[place_of], weight)
+    for index, shift, factor in modes[1:]:
+        inside, place_of, weight = gives(shift, factor, jnp.logical_not(upward))
+
+        @pl.when(inside)
+        def _(index=index, place_of=place_of, weight=weight):
+            total[1] += product(phonon_ref[index], bank[place_of], weight)
 
     most_first = upward == (first_side(group) > 0)
     first_out[...] = bf(total[jnp.where(most_first, 0, 1)])
     second_out[...] = bf(total[jnp.where(most_first, 1, 0)])
 
 
-def column_terms(first_ref, second_ref, phonon_ref, offsets_ref, bose_ref, out):
+def column_terms(first_ref, second_ref, phonon_ref, places_ref, factors_ref, out):
     _, group, _ = place()
     side = first_side(group)
-    far, _, _ = modes_of(offsets_ref)
-    factor = bose_ref[far]
+    (index, _, factor), _, _ = modes_of(phonon_ref, places_ref, factors_ref)
     first_weight = jnp.where(side > 0, factor, factor + 1.0)
     second_weight = jnp.where(side > 0, factor + 1.0, factor)
     block = mixed(first_ref[...], first_weight, second_ref[...], second_weight)
-    out[...] = product(phonon_ref[far], block)
+    out[...] = product(phonon_ref[index], block)
 
 
 def group_terms(*refs):
-    parts, (phonon_ref, offsets_ref, bose_ref, out, bank) = refs[: GROUP - 1], refs[GROUP - 1 :]
+    parts, (phonon_ref, places_ref, factors_ref, out, bank) = refs[: GROUP - 1], refs[GROUP - 1 :]
     _, _, seat = place()
     for j, part in enumerate(parts):
         bank[j] = part[...]
-    _, *others = modes_of(offsets_ref)
     sum_of_modes = None
-    for mode in others:
-        shift, factor = offsets_ref[mode], bose_ref[mode]
+    for index, shift, factor in modes_of(phonon_ref, places_ref, factors_ref)[1:]:
         below, above = seat - shift, seat + shift
         has_below, has_above = below >= 0, above < GROUP
         first = jnp.where(has_below, jnp.bitwise_xor(seat, below) - 1, 0)
@@ -302,7 +324,7 @@
             bank[second],
             jnp.where(has_above, factor, 0.0),
         )
-        term = product(phonon_ref[mode], block)
+        term = product(phonon_ref[index], block)
         sum_of_modes = term if sum_of_modes is None else sum_of_modes + term
     out[...] = sum_of_modes
 
@@ -373,7 +395,6 @@
     taller = jax.ShapeDtypeStruct((m + 16, m), jnp.bfloat16)
     wide = jax.ShapeDtypeStruct((m, m), jnp.float32)
     line = jax.ShapeDtypeStruct((1, m), jnp.float32)
-    modes = [phonon_coupling, offsets, bose_factors]
 
     def bank(blocks):
         return pltpu.VMEM((blocks, m, m), jnp.bfloat16)
@@ -381,10 +402,13 @@
     def totals(blocks):
         return pltpu.VMEM((blocks, m, m), jnp.float32)
 
-    real, imag, dos = greens_halves(g, coupling)
+    real, imag, dos, table = greens_halves(g, coupling, offsets, bose_factors)
+    modes = [phonon_coupling, *table]
     first_imag = across_groups(imag, first_pair)
     second_imag = across_groups(imag, second_pair)
     reals = [real] + [across_seats(real, j) for j in range(1, GROUP)]
+
+    first_imag, reals[-1] = lax.optimization_barrier((first_imag, reals[-1]))
 
     group_sum, dos_first = call(
         functools.partial(column_sums, lax.axis_size("energy")), [line, line], [first_imag, dos]
@@ -396,20 +420,27 @@
             (group_sum,) = call(add_lines, [line], [group_sum, received[-1]])
         received.append(across_groups(group_sum, lambda a, step=step: a ^ step))
         step *= 2
-    (imag_total,) = call(column_terms, [wide], [first_imag, second_imag, *modes])
-    (before,) = call(sums_before, [line], received)
 
     sums = call(
         to_seats,
         [taller] * (GROUP - 1),
-        [imag, first_imag, second_imag, *modes, dos, before],
-        [bank(3), totals(GROUP // 2)],
+        [imag, first_imag, second_imag, *modes],
+        [bank(3), pltpu.VMEM((GROUP // 2 * m, m), jnp.float32)],
+    )
+    (imag_total,) = call(column_terms, [wide], [first_imag, second_imag, *modes])
+    received[-1], imag_total = lax.optimization_barrier((received[-1], imag_total))
+    (before,) = call(sums_before, [line], received)
+    sums = call(
+        with_lines,
+        [taller] * (GROUP - 1),
+        [dos, before, *sums],
+        aliases={2 + i: i for i in range(GROUP - 1)},
     )
     seat_terms = [across_seats(value, j) for j, value in enumerate(sums, 1)]
 
     reals[0], _ = lax.optimization_barrier((reals[0], sums[0]))
     first_out, second_out = call(
-        to_groups, [half, half], [*reals, *modes], [bank(GROUP), totals(len(offsets))]
+        to_groups, [half, half], [*reals, *modes], [bank(GROUP), totals(2)]
     )
     first_term = across_groups(first_out, first_pair)
     second_term = across_groups(second_out, second_pair)

time: 43.2 us -> 41.9 us (0.970)
  the two profiles are of different devices: /device:TPU:10 before, /device:TPU:0 now
where the time goes in v3:
time: 41.9 us; the launch traced here: 41.7 us
  starting transfers between devices  18.7 us (45%)
  waiting for transfers between devices  12.7 us (30%)
  Pallas kernels  9.54 us (23%)
  between operations  0.78 us (2%)
    pallas_call x10, Pallas kernels, call(): pl.pallas_call(kernel, out_shape=outs, in_specs=[SCALARS if i.ndim == 1 e...  9.54 us
    ppermute x6, starting transfers between devices, across_seats(): return lax.ppermute(value, 'energy', [(e, e ^ j) for e in range(energies)])  8.49 us
    ppermute x5, starting transfers between devices, across_groups(): lax.ppermute(value, 'energy', [(GROUP * a + i, GROUP * b + i) for a, b in...  7.56 us
    ppermute x6, waiting for transfers between devices, across_seats(): return lax.ppermute(value, 'energy', [(e, e ^ j) for e in range(energies)])  6.91 us
    ppermute x5, waiting for transfers between devices, across_groups(): lax.ppermute(value, 'energy', [(GROUP * a + i, GROUP * b + i) for a, b in...  5 us
    ppermute x1, starting transfers between devices, greens_halves(): below = lax.ppermute(coupling, 'slab', up)  2.1 us
  transfers between devices with their start and end apart: 13, of which 5 were waited for; matrix products, arithmetic and copies ran while one was open for 0% of the time, Pallas kernels for 14%

profile of v3, /device:TPU:0, one launch (start us, length us, event | category | flops | bytes accessed | tf_op | source)
XLA Modules:
  0.0 41.7 jit_solution(5133173747436948014)
XLA Ops:
  0.7 0.5 %collective-permute-start = (bf16[384,768]{1,0:T(8,128)(2,1)}, bf16[384,768]{1,0:T(8,128)(2,1)S(1)}, u32[]{:S(2)}, u32[]{:S(2)}) collective-permute-start(bf16[384,768]{1,0:T(8,128)(2,1)} %bitcast.2), channel_id=1, source_target_pairs={{0,1},{1,0},{2,3},{3,2},{4,5},{5,4},{6,7},{7,6},{8,9},{9,8},{10,11... | collective-permute-start | bytes 1769480 | tf_op jit(solution)/shard_map/ppermute | solution.py:161
  1.2 2.1 %collective-permute-start.1 = (bf16[384,384]{1,0:T(8,128)(2,1)}, bf16[384,384]{1,0:T(8,128)(2,1)S(1)}, u32[]{:S(2)}, u32[]{:S(2)}) collective-permute-start(bf16[384,384]{1,0:T(8,128)(2,1)} %own_ref.1), channel_id=1, source_target_pairs={{0,1},{2,3},{4,5},{6,7},{8,9},{10,11},{12,13},{14,15},{16,17},{18,... | collective-permute-start | bytes 884744 | tf_op jit(solution)/shard_map/ppermute | solution.py:152
  3.3 0.6 %shard_map.68 = (f32[1,384]{1,0:T(1,128)S(1)}, s32[8,128]{1,0:T(8,128)S(1)}, f32[8,128]{1,0:T(8,128)S(1)}) custom-call(s32[3]{0:T(128)S(1)} %copy-done.3, f32[3]{0:T(128)S(1)} %copy-done.4), custom_call_target="tpu_custom_call" | custom-call | flops 1358954496 | tf_op jit(solution)/shard_map/pallas_call | solution.py:41
  3.9 0.8 %collective-permute-done.1.below_ref = bf16[384,384]{1,0:T(8,128)(2,1)S(1)} collective-permute-done((bf16[384,384]{1,0:T(8,128)(2,1)}, bf16[384,384]{1,0:T(8,128)(2,1)S(1)}, u32[]{:S(2)}, u32[]{:S(2)}) %collective-permute-start.1) | collective-permute-done | bytes 294944 | tf_op jit(solution)/shard_map/ppermute | solution.py:152
  4.7 0.0 collective-permute-done.other_ref
  4.7 2.7 %shard_map.69 = (bf16[384,384]{1,0:T(8,128)(2,1)S(1)}, bf16[384,384]{1,0:T(8,128)(2,1)S(1)}, f32[1,384]{1,0:T(1,128)S(1)}) custom-call(bf16[384,768]{1,0:T(8,128)(2,1)S(1)} %bitcast.3, bf16[384,768]{1,0:T(8,128)(2,1)S(1)} %collective-permute-done.other_ref, bf16[384,384]{1,0:T(8,128)(2,1)S(1)} %copy-done.2, ...), custom_call_target="tpu_custom_call" | custom-call | tf_op jit(solution)/shard_map/pallas_call | solution.py:41
  7.4 3.8 %collective-permute-start.5 = (bf16[384,384]{1,0:T(8,128)(2,1)S(1)}, bf16[384,384]{1,0:T(8,128)(2,1)S(1)}, u32[]{:S(2)}, u32[]{:S(2)}) collective-permute-start(bf16[384,384]{1,0:T(8,128)(2,1)S(1)} %get-tuple-element.41.refs_0_), channel_id=1, source_target_pairs={{0,6},{2,4},{4,2},{6,0},{8,14},{10,12},{12,10},{14,8},{16,22},{18,... | collective-permute-start | bytes 884744 | tf_op jit(solution)/shard_map/ppermute | solution.py:369
  11.3 1.6 %collective-permute-start.4 = (bf16[384,384]{1,0:T(8,128)(2,1)S(1)}, bf16[384,384]{1,0:T(8,128)(2,1)S(1)}, u32[]{:S(2)}, u32[]{:S(2)}) collective-permute-start(bf16[384,384]{1,0:T(8,128)(2,1)S(1)} %get-tuple-element.27.own_ref), channel_id=1, source_target_pairs={{0,8},{2,10},{4,12},{6,14},{8,0},{10,2},{12,4},{14,6},{16,24},{18,... | collective-permute-start | bytes 884744 | tf_op jit(solution)/shard_map/ppermute | solution.py:375
  12.8 0.7 %collective-permute-start.7 = (bf16[384,384]{1,0:T(8,128)(2,1)S(1)}, bf16[384,384]{1,0:T(8,128)(2,1)S(1)}, u32[]{:S(2)}, u32[]{:S(2)}) collective-permute-start(bf16[384,384]{1,0:T(8,128)(2,1)S(1)} %get-tuple-element.27.own_ref), channel_id=1, source_target_pairs={{8,16},{10,18},{12,20},{14,22},{16,8},{18,10},{20,12},{22,14},{9,1... | collective-permute-start | bytes 884744 | tf_op jit(solution)/shard_map/ppermute | solution.py:375
  13.5 0.6 %collective-permute-start.2 = (bf16[384,384]{1,0:T(8,128)(2,1)S(1)}, bf16[384,384]{1,0:T(8,128)(2,1)S(1)}, u32[]{:S(2)}, u32[]{:S(2)}) collective-permute-start(bf16[384,384]{1,0:T(8,128)(2,1)S(1)} %get-tuple-element.41.refs_0_), channel_id=1, source_target_pairs={{0,2},{2,0},{4,6},{6,4},{8,10},{10,8},{12,14},{14,12},{16,18},{18,... | collective-permute-start | bytes 884744 | tf_op jit(solution)/shard_map/ppermute | solution.py:369
  14.1 0.5 %collective-permute-start.3 = (bf16[384,384]{1,0:T(8,128)(2,1)S(1)}, bf16[384,384]{1,0:T(8,128)(2,1)S(1)}, u32[]{:S(2)}, u32[]{:S(2)}) collective-permute-start(bf16[384,384]{1,0:T(8,128)(2,1)S(1)} %get-tuple-element.41.refs_0_), channel_id=1, source_target_pairs={{0,4},{2,6},{4,0},{6,2},{8,12},{10,14},{12,8},{14,10},{16,20},{18,... | collective-permute-start | bytes 884744 | tf_op jit(solution)/shard_map/ppermute | solution.py:369
  14.6 4.5 %collective-permute-done.5.refs_2_.refs_3_ = bf16[384,384]{1,0:T(8,128)(2,1)S(1)} collective-permute-done((bf16[384,384]{1,0:T(8,128)(2,1)S(1)}, bf16[384,384]{1,0:T(8,128)(2,1)S(1)}, u32[]{:S(2)}, u32[]{:S(2)}) %collective-permute-start.5) | collective-permute-done | bytes 294944 | tf_op jit(solution)/shard_map/ppermute | solution.py:369
  19.2 1.2 %collective-permute-done.4.first_ref = bf16[384,384]{1,0:T(8,128)(2,1)S(1)} collective-permute-done((bf16[384,384]{1,0:T(8,128)(2,1)S(1)}, bf16[384,384]{1,0:T(8,128)(2,1)S(1)}, u32[]{:S(2)}, u32[]{:S(2)}) %collective-permute-start.4) | collective-permute-done | bytes 294944 | tf_op jit(solution)/shard_map/ppermute | solution.py:375
  20.4 2.7 %collective-permute-start.6 = (f32[1,384]{1,0:T(1,128)S(1)}, f32[1,384]{1,0:T(1,128)S(1)}, u32[]{:S(2)}, u32[]{:S(2)}) collective-permute-start(f32[1,384]{1,0:T(1,128)S(1)} %get-tuple-element.33), channel_id=1, source_target_pairs={{0,16},{2,18},{4,20},{6,22},{8,24},{10,26},{12,28},{14,30},{16,0},... | collective-permute-start | bytes 4616 | tf_op jit(solution)/shard_map/ppermute | solution.py:375
  23.0 0.0 collective-permute-done.7.second_ref
  23.0 0.7 %shard_map.72.refs_1_ = f32[384,384]{1,0:T(8,128)S(1)} custom-call(bf16[384,384]{1,0:T(8,128)(2,1)S(1)} %collective-permute-done.4.first_ref, bf16[384,384]{1,0:T(8,128)(2,1)S(1)} %collective-permute-done.7.second_ref, bf16[3,384,384]{2,1,0:T(8,128)(2,1)S(1)} %copy-done, s32[8,128]{1,0:T(8,128)S(1)} %get-tuple-element.29.refs_4_.places_ref.refs_5_, ...), custom_call_target="tpu_custom_call" | custom-call | tf_op jit(solution)/shard_map/pallas_call | solution.py:41
  23.7 1.7 %shard_map.74 = (bf16[400,384]{1,0:T(8,128)(2,1)S(1)}, bf16[400,384]{1,0:T(8,128)(2,1)S(1)}, bf16[400,384]{1,0:T(8,128)(2,1)S(1)}) custom-call(bf16[384,384]{1,0:T(8,128)(2,1)S(1)} %get-tuple-element.27.own_ref, bf16[384,384]{1,0:T(8,128)(2,1)S(1)} %collective-permute-done.4.first_ref, bf16[384,384]{1,0:T(8,128)(2,1)S(1)} %collective-permute-done.7.second_ref, ...), custom_call_target="tpu_custom_call" | custom-call | tf_op jit(solution)/shard_map/pallas_call | solution.py:41
  25.4 0.0 collective-permute-done.6.refs_1_
  25.5 0.8 %collective-permute-start.10 = (bf16[400,384]{1,0:T(8,128)(2,1)S(1)}, bf16[400,384]{1,0:T(8,128)(2,1)S(1)}, u32[]{:S(2)}, u32[]{:S(2)}) collective-permute-start(bf16[400,384]{1,0:T(8,128)(2,1)S(1)} %get-tuple-element.40), channel_id=1, source_target_pairs={{0,2},{2,0},{4,6},{6,4},{8,10},{10,8},{12,14},{14,12},{16,18},{18,... | collective-permute-start | bytes 921608 | tf_op jit(solution)/shard_map/ppermute | solution.py:369
  26.2 1.6 %collective-permute-start.11 = (bf16[400,384]{1,0:T(8,128)(2,1)S(1)}, bf16[400,384]{1,0:T(8,128)(2,1)S(1)}, u32[]{:S(2)}, u32[]{:S(2)}) collective-permute-start(bf16[400,384]{1,0:T(8,128)(2,1)S(1)} %get-tuple-element.44), channel_id=1, source_target_pairs={{0,4},{2,6},{4,0},{6,2},{8,12},{10,14},{12,8},{14,10},{16,20},{18,... | collective-permute-start | bytes 921608 | tf_op jit(solution)/shard_map/ppermute | solution.py:369
  27.8 1.2 %collective-permute-start.12 = (bf16[400,384]{1,0:T(8,128)(2,1)S(1)}, bf16[400,384]{1,0:T(8,128)(2,1)S(1)}, u32[]{:S(2)}, u32[]{:S(2)}) collective-permute-start(bf16[400,384]{1,0:T(8,128)(2,1)S(1)} %get-tuple-element.45), channel_id=1, source_target_pairs={{0,6},{2,4},{4,2},{6,0},{8,14},{10,12},{12,10},{14,8},{16,22},{18,... | collective-permute-start | bytes 921608 | tf_op jit(solution)/shard_map/ppermute | solution.py:369
  29.0 0.0 collective-permute-done.2.refs_0_.refs_1_
  29.0 0.0 collective-permute-done.3.refs_1_.refs_2_
  29.0 1.6 %shard_map.76 = (bf16[384,384]{1,0:T(8,128)(2,1)S(1)}, bf16[384,384]{1,0:T(8,128)(2,1)S(1)}) custom-call(bf16[384,384]{1,0:T(8,128)(2,1)S(1)} %get-tuple-element.41.refs_0_, bf16[384,384]{1,0:T(8,128)(2,1)S(1)} %collective-permute-done.2.refs_0_.refs_1_, bf16[384,384]{1,0:T(8,128)(2,1)S(1)} %collective-permute-done.3.refs_1_.refs_2_, ...), custom_call_target="tpu_custom_call" | custom-call | tf_op jit(solution)/shard_map/pallas_call | solution.py:41
  30.6 2.0 %collective-permute-start.8 = (bf16[384,384]{1,0:T(8,128)(2,1)S(1)}, bf16[384,384]{1,0:T(8,128)(2,1)S(1)}, u32[]{:S(2)}, u32[]{:S(2)}) collective-permute-start(bf16[384,384]{1,0:T(8,128)(2,1)S(1)} %get-tuple-element.42), channel_id=1, source_target_pairs={{0,8},{2,10},{4,12},{6,14},{8,0},{10,2},{12,4},{14,6},{16,24},{18,... | collective-permute-start | bytes 884744 | tf_op jit(solution)/shard_map/ppermute | solution.py:375
  32.6 0.7 %collective-permute-start.9 = (bf16[384,384]{1,0:T(8,128)(2,1)S(1)}, bf16[384,384]{1,0:T(8,128)(2,1)S(1)}, u32[]{:S(2)}, u32[]{:S(2)}) collective-permute-start(bf16[384,384]{1,0:T(8,128)(2,1)S(1)} %get-tuple-element.43), channel_id=1, source_target_pairs={{8,16},{10,18},{12,20},{14,22},{16,8},{18,10},{20,12},{22,14},{9,1... | collective-permute-start | bytes 884744 | tf_op jit(solution)/shard_map/ppermute | solution.py:375
  33.3 1.1 %shard_map.70.refs_0_ = f32[384,384]{1,0:T(8,128)S(1)} custom-call(bf16[384,384]{1,0:T(8,128)(2,1)S(1)} %collective-permute-done.2.refs_0_.refs_1_, bf16[384,384]{1,0:T(8,128)(2,1)S(1)} %collective-permute-done.3.refs_1_.refs_2_, bf16[384,384]{1,0:T(8,128)(2,1)S(1)} %collective-permute-done.5.refs_2_.refs_3_, bf16[3,384,384]{2,1,0:T(8,128)(2,1)S(1)} %copy-done, ...), custom_call_target="tpu_custom_call" | custom-call | tf_op jit(solution)/shard_map/pallas_call | solution.py:41
  34.4 3.8 %collective-permute-done.8.refs_2_ = bf16[384,384]{1,0:T(8,128)(2,1)S(1)} collective-permute-done((bf16[384,384]{1,0:T(8,128)(2,1)S(1)}, bf16[384,384]{1,0:T(8,128)(2,1)S(1)}, u32[]{:S(2)}, u32[]{:S(2)}) %collective-permute-start.8) | collective-permute-done | bytes 294944 | tf_op jit(solution)/shard_map/ppermute | solution.py:375
  38.2 0.0 collective-permute-done.9.refs_3_
  38.3 2.3 %collective-permute-done.11.refs_7_ = bf16[400,384]{1,0:T(8,128)(2,1)S(1)} collective-permute-done((bf16[400,384]{1,0:T(8,128)(2,1)S(1)}, bf16[400,384]{1,0:T(8,128)(2,1)S(1)}, u32[]{:S(2)}, u32[]{:S(2)}) %collective-permute-start.11) | collective-permute-done | bytes 307232 | tf_op jit(solution)/shard_map/ppermute | solution.py:369
  40.6 0.0 collective-permute-done.12.refs_8_
  40.6 1.1 %shard_map.77 = (bf16[384,768]{1,0:T(8,128)(2,1)}, f32[1,384]{1,0:T(1,128)}) custom-call(f32[384,384]{1,0:T(8,128)S(1)} %shard_map.70.refs_0_, f32[384,384]{1,0:T(8,128)S(1)} %shard_map.72.refs_1_, bf16[384,384]{1,0:T(8,128)(2,1)S(1)} %collective-permute-done.8.refs_2_, bf16[384,384]{1,0:T(8,128)(2,1)S(1)} %collective-permute-done.9.refs_3_, ...), custom_call_target="tpu_custom_call" | custom-call | tf_op jit(solution)/shard_map/pallas_call | solution.py:41
  (14 shorter events, 0.1 us)
Async XLA Ops:
  0.6 2.7 %copy-start.3 = (s32[3]{0:T(128)S(1)}, s32[3]{0:T(128)}, u32[]{:S(2)}) copy-start(s32[3]{0:T(128)} %offsets_ref.1) | copy-start | bytes 40
  0.6 2.7 %copy-start.4 = (f32[3]{0:T(128)S(1)}, f32[3]{0:T(128)}, u32[]{:S(2)}) copy-start(f32[3]{0:T(128)} %bose_ref.1) | copy-start | bytes 40
  0.7 4.0 %copy-start.1 = (bf16[1,384,768]{2,1,0:T(8,128)(2,1)S(1)}, bf16[1,384,768]{2,1,0:T(8,128)(2,1)}, u32[]{:S(2)}) copy-start(bf16[1,384,768]{2,1,0:T(8,128)(2,1)} %param.5) | copy-start | bytes 1769476
  0.7 4.0 %copy-start.2 = (bf16[384,384]{1,0:T(8,128)(2,1)S(1)}, bf16[384,384]{1,0:T(8,128)(2,1)}, u32[]{:S(2)}) copy-start(bf16[384,384]{1,0:T(8,128)(2,1)} %own_ref.1) | copy-start | bytes 884740
  0.7 4.0 %collective-permute-start = (bf16[384,768]{1,0:T(8,128)(2,1)}, bf16[384,768]{1,0:T(8,128)(2,1)S(1)}, u32[]{:S(2)}, u32[]{:S(2)}) collective-permute-start(bf16[384,768]{1,0:T(8,128)(2,1)} %bitcast.2), channel_id=1, source_target_pairs={{0,1},{1,0},{2,3},{3,2},{4,5},{5,4},{6,7},{7,6},{8,9},{9,8},{10,11... | collective-permute-start | bytes 1769480 | tf_op jit(solution)/shard_map/ppermute | solution.py:161
  1.2 3.5 %collective-permute-start.1 = (bf16[384,384]{1,0:T(8,128)(2,1)}, bf16[384,384]{1,0:T(8,128)(2,1)S(1)}, u32[]{:S(2)}, u32[]{:S(2)}) collective-permute-start(bf16[384,384]{1,0:T(8,128)(2,1)} %own_ref.1), channel_id=1, source_target_pairs={{0,1},{2,3},{4,5},{6,7},{8,9},{10,11},{12,13},{14,15},{16,17},{18,... | collective-permute-start | bytes 884744 | tf_op jit(solution)/shard_map/ppermute | solution.py:152
  4.7 18.3 %copy-start = (bf16[3,384,384]{2,1,0:T(8,128)(2,1)S(1)}, bf16[3,384,384]{2,1,0:T(8,128)(2,1)}, u32[]{:S(2)}) copy-start(bf16[3,384,384]{2,1,0:T(8,128)(2,1)} %refs_4_.1) | copy-start | bytes 2654212
  7.4 11.7 %collective-permute-start.5 = (bf16[384,384]{1,0:T(8,128)(2,1)S(1)}, bf16[384,384]{1,0:T(8,128)(2,1)S(1)}, u32[]{:S(2)}, u32[]{:S(2)}) collective-permute-start(bf16[384,384]{1,0:T(8,128)(2,1)S(1)} %get-tuple-element.41.refs_0_), channel_id=1, source_target_pairs={{0,6},{2,4},{4,2},{6,0},{8,14},{10,12},{12,10},{14,8},{16,22},{18,... | collective-permute-start | bytes 884744 | tf_op jit(solution)/shard_map/ppermute | solution.py:369
  11.3 9.1 %collective-permute-start.4 = (bf16[384,384]{1,0:T(8,128)(2,1)S(1)}, bf16[384,384]{1,0:T(8,128)(2,1)S(1)}, u32[]{:S(2)}, u32[]{:S(2)}) collective-permute-start(bf16[384,384]{1,0:T(8,128)(2,1)S(1)} %get-tuple-element.27.own_ref), channel_id=1, source_target_pairs={{0,8},{2,10},{4,12},{6,14},{8,0},{10,2},{12,4},{14,6},{16,24},{18,... | collective-permute-start | bytes 884744 | tf_op jit(solution)/shard_map/ppermute | solution.py:375
  12.8 10.2 %collective-permute-start.7 = (bf16[384,384]{1,0:T(8,128)(2,1)S(1)}, bf16[384,384]{1,0:T(8,128)(2,1)S(1)}, u32[]{:S(2)}, u32[]{:S(2)}) collective-permute-start(bf16[384,384]{1,0:T(8,128)(2,1)S(1)} %get-tuple-element.27.own_ref), channel_id=1, source_target_pairs={{8,16},{10,18},{12,20},{14,22},{16,8},{18,10},{20,12},{22,14},{9,1... | collective-permute-start | bytes 884744 | tf_op jit(solution)/shard_map/ppermute | solution.py:375
  13.5 15.5 %collective-permute-start.2 = (bf16[384,384]{1,0:T(8,128)(2,1)S(1)}, bf16[384,384]{1,0:T(8,128)(2,1)S(1)}, u32[]{:S(2)}, u32[]{:S(2)}) collective-permute-start(bf16[384,384]{1,0:T(8,128)(2,1)S(1)} %get-tuple-element.41.refs_0_), channel_id=1, source_target_pairs={{0,2},{2,0},{4,6},{6,4},{8,10},{10,8},{12,14},{14,12},{16,18},{18,... | collective-permute-start | bytes 884744 | tf_op jit(solution)/shard_map/ppermute | solution.py:369
  14.1 14.9 %collective-permute-start.3 = (bf16[384,384]{1,0:T(8,128)(2,1)S(1)}, bf16[384,384]{1,0:T(8,128)(2,1)S(1)}, u32[]{:S(2)}, u32[]{:S(2)}) collective-permute-start(bf16[384,384]{1,0:T(8,128)(2,1)S(1)} %get-tuple-element.41.refs_0_), channel_id=1, source_target_pairs={{0,4},{2,6},{4,0},{6,2},{8,12},{10,14},{12,8},{14,10},{16,20},{18,... | collective-permute-start | bytes 884744 | tf_op jit(solution)/shard_map/ppermute | solution.py:369
  20.4 5.0 %collective-permute-start.6 = (f32[1,384]{1,0:T(1,128)S(1)}, f32[1,384]{1,0:T(1,128)S(1)}, u32[]{:S(2)}, u32[]{:S(2)}) collective-permute-start(f32[1,384]{1,0:T(1,128)S(1)} %get-tuple-element.33), channel_id=1, source_target_pairs={{0,16},{2,18},{4,20},{6,22},{8,24},{10,26},{12,28},{14,30},{16,0},... | collective-permute-start | bytes 4616 | tf_op jit(solution)/shard_map/ppermute | solution.py:375
  25.5 12.8 %collective-permute-start.10 = (bf16[400,384]{1,0:T(8,128)(2,1)S(1)}, bf16[400,384]{1,0:T(8,128)(2,1)S(1)}, u32[]{:S(2)}, u32[]{:S(2)}) collective-permute-start(bf16[400,384]{1,0:T(8,128)(2,1)S(1)} %get-tuple-element.40), channel_id=1, source_target_pairs={{0,2},{2,0},{4,6},{6,4},{8,10},{10,8},{12,14},{14,12},{16,18},{18,... | collective-permute-start | bytes 921608 | tf_op jit(solution)/shard_map/ppermute | solution.py:369
  26.2 14.4 %collective-permute-start.11 = (bf16[400,384]{1,0:T(8,128)(2,1)S(1)}, bf16[400,384]{1,0:T(8,128)(2,1)S(1)}, u32[]{:S(2)}, u32[]{:S(2)}) collective-permute-start(bf16[400,384]{1,0:T(8,128)(2,1)S(1)} %get-tuple-element.44), channel_id=1, source_target_pairs={{0,4},{2,6},{4,0},{6,2},{8,12},{10,14},{12,8},{14,10},{16,20},{18,... | collective-permute-start | bytes 921608 | tf_op jit(solution)/shard_map/ppermute | solution.py:369
  27.8 12.8 %collective-permute-start.12 = (bf16[400,384]{1,0:T(8,128)(2,1)S(1)}, bf16[400,384]{1,0:T(8,128)(2,1)S(1)}, u32[]{:S(2)}, u32[]{:S(2)}) collective-permute-start(bf16[400,384]{1,0:T(8,128)(2,1)S(1)} %get-tuple-element.45), channel_id=1, source_target_pairs={{0,6},{2,4},{4,2},{6,0},{8,14},{10,12},{12,10},{14,8},{16,22},{18,... | collective-permute-start | bytes 921608 | tf_op jit(solution)/shard_map/ppermute | solution.py:369
  30.6 7.6 %collective-permute-start.8 = (bf16[384,384]{1,0:T(8,128)(2,1)S(1)}, bf16[384,384]{1,0:T(8,128)(2,1)S(1)}, u32[]{:S(2)}, u32[]{:S(2)}) collective-permute-start(bf16[384,384]{1,0:T(8,128)(2,1)S(1)} %get-tuple-element.42), channel_id=1, source_target_pairs={{0,8},{2,10},{4,12},{6,14},{8,0},{10,2},{12,4},{14,6},{16,24},{18,... | collective-permute-start | bytes 884744 | tf_op jit(solution)/shard_map/ppermute | solution.py:375
  32.6 5.6 %collective-permute-start.9 = (bf16[384,384]{1,0:T(8,128)(2,1)S(1)}, bf16[384,384]{1,0:T(8,128)(2,1)S(1)}, u32[]{:S(2)}, u32[]{:S(2)}) collective-permute-start(bf16[384,384]{1,0:T(8,128)(2,1)S(1)} %get-tuple-element.43), channel_id=1, source_target_pairs={{8,16},{10,18},{12,20},{14,22},{16,8},{18,10},{20,12},{22,14},{9,1... | collective-permute-start | bytes 884744 | tf_op jit(solution)/shard_map/ppermute | solution.py:375

commit v4 on v3

--- a/solution.py
+++ b/solution.py
@@ -14,6 +14,7 @@
 VMEM_LIMIT = 16 * 1024 * 1024
 
 WHOLE = pl.BlockSpec(memory_space=pltpu.VMEM)
+OUTSIDE = pl.BlockSpec(memory_space=pl.ANY)
 SCALARS = pl.BlockSpec(memory_space=pltpu.SMEM)
 
 
@@ -37,12 +38,12 @@
     return value.astype(jnp.float32)
 
 
-def call(kernel, outs, ins, scratch=(), flops=0, aliases=None):
+def call(kernel, outs, ins, scratch=(), flops=0, aliases=None, outside=()):
     return pl.pallas_call(
         kernel,
         out_shape=outs,
         in_specs=[SCALARS if i.ndim == 1 else WHOLE for i in ins],
-        out_specs=[WHOLE] * len(outs),
+        out_specs=[OUTSIDE if o in outside else WHOLE for o in range(len(outs))],
         scratch_shapes=scratch,
         input_output_aliases=aliases or {},
         compiler_params=pltpu.CompilerParams(vmem_limit_bytes=VMEM_LIMIT),
@@ -68,8 +69,7 @@
 
 
 def complex_product(first, second):
-    m = first.shape[0]
-    return nn(first[:, :m], second) + nn(first[:, m:], rotated(second))
+    return nn(first, jnp.concatenate([second, rotated(second)], axis=0))
 
 
 def holes_at(energy, energies, shape):
@@ -198,7 +198,7 @@
 
 
 def to_seats(own_ref, first_ref, second_ref, phonon_ref, places_ref, factors_ref, *rest):
-    *outs, bank, total = rest
+    *outs, bank = rest
     m = own_ref.shape[0]
     _, group, seat = place()
     side = first_side(group)
@@ -226,29 +226,31 @@
         parts = [bf(w * wide[:, i * m : (i + 1) * m]) for i, w in enumerate(weights)]
         return nt(jnp.concatenate(parts, axis=0), matrix)
 
-    total[...] = odd_seats(odd)
+    def put(wide):
+        for j in range(1, GROUP, 2):
+            outs[j - 1][:m] = bf(wide[j // 2 * m : (j // 2 + 1) * m])
+
     index, shift, factor = left
 
     @pl.when(lax.rem(shift, 2) == 0)
     def _():
+        wide = odd_seats(odd)
         for j in range(2, GROUP, 2):
             _, upward, beside = towards(j)
             own_weight = jnp.where(upward, factor + 1.0, factor)
             beside_weight = jnp.where(upward, factor, factor + 1.0)
             block = mixed(bank[0], own_weight, bank[beside], beside_weight)
             outs[j - 1][:m] = bf(product(phonon_ref[index], block))
+        put(wide)
 
     @pl.when(lax.rem(shift, 2) == 1)
     def _():
-        total[...] += odd_seats(left)
+        put(odd_seats(odd) + odd_seats(left))
         for j in range(2, GROUP, 2):
             outs[j - 1][:m] = jnp.zeros((m, m), jnp.bfloat16)
 
-    for j in range(1, GROUP, 2):
-        outs[j - 1][:m] = bf(total[j // 2 * m : (j // 2 + 1) * m])
-        outs[j - 1][m:] = jnp.zeros((EXTRA, m), jnp.bfloat16)
-    for j in range(2, GROUP, 2):
-        outs[j - 1][m:] = jnp.zeros((EXTRA, m), jnp.bfloat16)
+    for out in outs:
+        out[m:] = jnp.zeros((EXTRA, m), jnp.bfloat16)
 
 
 def with_lines(dos_ref, before_ref, *refs):
@@ -352,16 +354,26 @@
 
 def last_sum(*refs):
     real_total, imag_total, first, second, before, dos = refs[:6]
-    *seats, out, cumulative = refs[6:]
+    *seats, out, cumulative, held, line, sems, line_sem = refs[6:]
     m = real_total.shape[0]
-    out[:, :m] = bf(real_total[...] + f32(first[...]) + f32(second[...]))
-    imag = imag_total[...]
-    line = before[...] + dos[...]
+    density = before[...] + dos[...]
     for part in seats:
-        imag = imag + f32(part[:m])
-        line = line + jnp.sum(f32(part[m:]), axis=0, keepdims=True)
-    out[:, m:] = bf(imag)
-    cumulative[...] = line
+        density = density + jnp.sum(f32(part[m:]), axis=0, keepdims=True)
+    line[...] = density
+    copies = [pltpu.make_async_copy(line, cumulative, line_sem)]
+    copies[0].start()
+    pieces = sems.shape[0]
+    for piece in range(pieces):
+        rows = pl.ds(piece * (m // pieces), m // pieces)
+        held[rows, :m] = bf(real_total[rows] + f32(first[rows]) + f32(second[rows]))
+        imag = imag_total[rows]
+        for part in seats:
+            imag = imag + f32(part[rows])
+        held[rows, m:] = bf(imag)
+        copies.append(pltpu.make_async_copy(held.at[rows], out.at[rows], sems.at[piece]))
+        copies[-1].start()
+    for copy in copies:
+        copy.wait()
 
 
 def across_seats(value, j):
@@ -425,10 +437,9 @@
         to_seats,
         [taller] * (GROUP - 1),
         [imag, first_imag, second_imag, *modes],
-        [bank(3), pltpu.VMEM((GROUP // 2 * m, m), jnp.float32)],
+        [bank(3)],
     )
     (imag_total,) = call(column_terms, [wide], [first_imag, second_imag, *modes])
-    received[-1], imag_total = lax.optimization_barrier((received[-1], imag_total))
     (before,) = call(sums_before, [line], received)
     sums = call(
         with_lines,
@@ -446,10 +457,18 @@
     second_term = across_groups(second_out, second_pair)
     (real_total,) = call(group_terms, [wide], [*reals[1:], *modes], [bank(GROUP - 1)])
 
+    pieces = 4 if m % 64 == 0 else 1
     sigma, cumulative = call(
         last_sum,
         [jax.ShapeDtypeStruct(g.shape, jnp.bfloat16), line],
         [real_total, imag_total, first_term, second_term, before, dos, *seat_terms],
+        [
+            pltpu.VMEM(g.shape, jnp.bfloat16),
+            pltpu.VMEM((1, m), jnp.float32),
+            pltpu.SemaphoreType.DMA((pieces,)),
+            pltpu.SemaphoreType.DMA,
+        ],
+        outside=(0, 1),
     )
     return sigma[None], cumulative
 

time: 41.9 us -> 40.3 us (0.962)
  Pallas kernels: 9.54 us -> 8.68 us
    pallas_call x10, Pallas kernels: 9.54 us -> 8.68 us  [call(): pl.pallas_call(kernel, out_shape=outs, in_specs=[SCALARS if i.ndim == 1 e...]
  transfers between devices with their start and end apart: 13 -> 13, of which waited for: 5 -> 6; matrix products, arithmetic and copies ran while one was open for 0% -> 0% of each run, Pallas kernels for 14% -> 14%
where the time goes in v4:
time: 40.3 us; the launch traced here: 40.1 us
  starting transfers between devices  18.3 us (45%)
  waiting for transfers between devices  12.4 us (31%)
  Pallas kernels  8.68 us (22%)
  between operations  0.76 us (2%)
    pallas_call x10, Pallas kernels, call(): pl.pallas_call(kernel, out_shape=outs, in_specs=[SCALARS if i.ndim == 1 e...  8.68 us
    ppermute x6, starting transfers between devices, across_seats(): return lax.ppermute(value, 'energy', [(e, e ^ j) for e in range(energies)])  8.48 us
    ppermute x5, starting transfers between devices, across_groups(): lax.ppermute(value, 'energy', [(GROUP * a + i, GROUP * b + i) for a, b in...  7.22 us
    ppermute x6, waiting for transfers between devices, across_seats(): return lax.ppermute(value, 'energy', [(e, e ^ j) for e in range(energies)])  6.9 us
    ppermute x5, waiting for transfers between devices, across_groups(): lax.ppermute(value, 'energy', [(GROUP * a + i, GROUP * b + i) for a, b in...  4.68 us
    ppermute x1, starting transfers between devices, greens_halves(): below = lax.ppermute(coupling, 'slab', up)  2.1 us
  transfers between devices with their start and end apart: 13, of which 6 were waited for; matrix products, arithmetic and copies ran while one was open for 0% of the time, Pallas kernels for 14%

profile of v4, /device:TPU:0, one launch (start us, length us, event | category | flops | bytes accessed | tf_op | source)
XLA Modules:
  0.0 40.1 jit_solution(2782102965700999148)
XLA Ops:
  0.7 0.5 %collective-permute-start = (bf16[384,768]{1,0:T(8,128)(2,1)}, bf16[384,768]{1,0:T(8,128)(2,1)S(1)}, u32[]{:S(2)}, u32[]{:S(2)}) collective-permute-start(bf16[384,768]{1,0:T(8,128)(2,1)} %bitcast.2), channel_id=1, source_target_pairs={{0,1},{1,0},{2,3},{3,2},{4,5},{5,4},{6,7},{7,6},{8,9},{9,8},{10,11... | collective-permute-start | bytes 1769480 | tf_op jit(solution)/shard_map/ppermute | solution.py:161
  1.2 2.1 %collective-permute-start.1 = (bf16[384,384]{1,0:T(8,128)(2,1)}, bf16[384,384]{1,0:T(8,128)(2,1)S(1)}, u32[]{:S(2)}, u32[]{:S(2)}) collective-permute-start(bf16[384,384]{1,0:T(8,128)(2,1)} %own_ref.1), channel_id=1, source_target_pairs={{0,1},{2,3},{4,5},{6,7},{8,9},{10,11},{12,13},{14,15},{16,17},{18,... | collective-permute-start | bytes 884744 | tf_op jit(solution)/shard_map/ppermute | solution.py:152
  3.3 0.6 %shard_map.68 = (f32[1,384]{1,0:T(1,128)S(1)}, s32[8,128]{1,0:T(8,128)S(1)}, f32[8,128]{1,0:T(8,128)S(1)}) custom-call(s32[3]{0:T(128)S(1)} %copy-done.3, f32[3]{0:T(128)S(1)} %copy-done.4), custom_call_target="tpu_custom_call" | custom-call | flops 1358954496 | tf_op jit(solution)/shard_map/pallas_call | solution.py:42
  3.9 0.8 %collective-permute-done.1.below_ref = bf16[384,384]{1,0:T(8,128)(2,1)S(1)} collective-permute-done((bf16[384,384]{1,0:T(8,128)(2,1)}, bf16[384,384]{1,0:T(8,128)(2,1)S(1)}, u32[]{:S(2)}, u32[]{:S(2)}) %collective-permute-start.1) | collective-permute-done | bytes 294944 | tf_op jit(solution)/shard_map/ppermute | solution.py:152
  4.7 0.0 collective-permute-done.other_ref
  4.7 2.1 %shard_map.69 = (bf16[384,384]{1,0:T(8,128)(2,1)S(1)}, bf16[384,384]{1,0:T(8,128)(2,1)S(1)}, f32[1,384]{1,0:T(1,128)S(1)}) custom-call(bf16[384,768]{1,0:T(8,128)(2,1)S(1)} %bitcast.3, bf16[384,768]{1,0:T(8,128)(2,1)S(1)} %collective-permute-done.other_ref, bf16[384,384]{1,0:T(8,128)(2,1)S(1)} %copy-done.2, ...), custom_call_target="tpu_custom_call" | custom-call | tf_op jit(solution)/shard_map/pallas_call | solution.py:42
  6.8 3.8 %collective-permute-start.5 = (bf16[384,384]{1,0:T(8,128)(2,1)S(1)}, bf16[384,384]{1,0:T(8,128)(2,1)S(1)}, u32[]{:S(2)}, u32[]{:S(2)}) collective-permute-start(bf16[384,384]{1,0:T(8,128)(2,1)S(1)} %get-tuple-element.37.refs_0_), channel_id=1, source_target_pairs={{0,6},{2,4},{4,2},{6,0},{8,14},{10,12},{12,10},{14,8},{16,22},{18,... | collective-permute-start | bytes 884744 | tf_op jit(solution)/shard_map/ppermute | solution.py:381
  10.7 1.6 %collective-permute-start.4 = (bf16[384,384]{1,0:T(8,128)(2,1)S(1)}, bf16[384,384]{1,0:T(8,128)(2,1)S(1)}, u32[]{:S(2)}, u32[]{:S(2)}) collective-permute-start(bf16[384,384]{1,0:T(8,128)(2,1)S(1)} %get-tuple-element.25.own_ref), channel_id=1, source_target_pairs={{0,8},{2,10},{4,12},{6,14},{8,0},{10,2},{12,4},{14,6},{16,24},{18,... | collective-permute-start | bytes 884744 | tf_op jit(solution)/shard_map/ppermute | solution.py:387
  12.2 0.7 %collective-permute-start.6 = (bf16[384,384]{1,0:T(8,128)(2,1)S(1)}, bf16[384,384]{1,0:T(8,128)(2,1)S(1)}, u32[]{:S(2)}, u32[]{:S(2)}) collective-permute-start(bf16[384,384]{1,0:T(8,128)(2,1)S(1)} %get-tuple-element.25.own_ref), channel_id=1, source_target_pairs={{8,16},{10,18},{12,20},{14,22},{16,8},{18,10},{20,12},{22,14},{9,1... | collective-permute-start | bytes 884744 | tf_op jit(solution)/shard_map/ppermute | solution.py:387
  12.9 0.6 %collective-permute-start.2 = (bf16[384,384]{1,0:T(8,128)(2,1)S(1)}, bf16[384,384]{1,0:T(8,128)(2,1)S(1)}, u32[]{:S(2)}, u32[]{:S(2)}) collective-permute-start(bf16[384,384]{1,0:T(8,128)(2,1)S(1)} %get-tuple-element.37.refs_0_), channel_id=1, source_target_pairs={{0,2},{2,0},{4,6},{6,4},{8,10},{10,8},{12,14},{14,12},{16,18},{18,... | collective-permute-start | bytes 884744 | tf_op jit(solution)/shard_map/ppermute | solution.py:381
  13.5 0.5 %collective-permute-start.3 = (bf16[384,384]{1,0:T(8,128)(2,1)S(1)}, bf16[384,384]{1,0:T(8,128)(2,1)S(1)}, u32[]{:S(2)}, u32[]{:S(2)}) collective-permute-start(bf16[384,384]{1,0:T(8,128)(2,1)S(1)} %get-tuple-element.37.refs_0_), channel_id=1, source_target_pairs={{0,4},{2,6},{4,0},{6,2},{8,12},{10,14},{12,8},{14,10},{16,20},{18,... | collective-permute-start | bytes 884744 | tf_op jit(solution)/shard_map/ppermute | solution.py:381
  14.0 4.5 %collective-permute-done.5.refs_2_.refs_3_ = bf16[384,384]{1,0:T(8,128)(2,1)S(1)} collective-permute-done((bf16[384,384]{1,0:T(8,128)(2,1)S(1)}, bf16[384,384]{1,0:T(8,128)(2,1)S(1)}, u32[]{:S(2)}, u32[]{:S(2)}) %collective-permute-start.5) | collective-permute-done | bytes 294944 | tf_op jit(solution)/shard_map/ppermute | solution.py:381
  18.6 1.2 %collective-permute-done.4.first_ref = bf16[384,384]{1,0:T(8,128)(2,1)S(1)} collective-permute-done((bf16[384,384]{1,0:T(8,128)(2,1)S(1)}, bf16[384,384]{1,0:T(8,128)(2,1)S(1)}, u32[]{:S(2)}, u32[]{:S(2)}) %collective-permute-start.4) | collective-permute-done | bytes 294944 | tf_op jit(solution)/shard_map/ppermute | solution.py:387
  19.8 2.7 %collective-permute-start.7 = (f32[1,384]{1,0:T(1,128)S(1)}, f32[1,384]{1,0:T(1,128)S(1)}, u32[]{:S(2)}, u32[]{:S(2)}) collective-permute-start(f32[1,384]{1,0:T(1,128)S(1)} %get-tuple-element.32), channel_id=1, source_target_pairs={{0,16},{2,18},{4,20},{6,22},{8,24},{10,26},{12,28},{14,30},{16,0},... | collective-permute-start | bytes 4616 | tf_op jit(solution)/shard_map/ppermute | solution.py:387
  22.4 0.0 collective-permute-done.6.second_ref
  22.4 1.5 %shard_map.74 = (bf16[400,384]{1,0:T(8,128)(2,1)S(1)}, bf16[400,384]{1,0:T(8,128)(2,1)S(1)}, bf16[400,384]{1,0:T(8,128)(2,1)S(1)}) custom-call(bf16[384,384]{1,0:T(8,128)(2,1)S(1)} %get-tuple-element.25.own_ref, bf16[384,384]{1,0:T(8,128)(2,1)S(1)} %collective-permute-done.4.first_ref, bf16[384,384]{1,0:T(8,128)(2,1)S(1)} %collective-permute-done.6.second_ref, ...), custom_call_target="tpu_custom_call" | custom-call | tf_op jit(solution)/shard_map/pallas_call | solution.py:42
  23.9 0.4 collective-permute-done.7.refs_1_
  24.4 0.8 %collective-permute-start.10 = (bf16[400,384]{1,0:T(8,128)(2,1)S(1)}, bf16[400,384]{1,0:T(8,128)(2,1)S(1)}, u32[]{:S(2)}, u32[]{:S(2)}) collective-permute-start(bf16[400,384]{1,0:T(8,128)(2,1)S(1)} %get-tuple-element.36), channel_id=1, source_target_pairs={{0,2},{2,0},{4,6},{6,4},{8,10},{10,8},{12,14},{14,12},{16,18},{18,... | collective-permute-start | bytes 921608 | tf_op jit(solution)/shard_map/ppermute | solution.py:381
  25.2 1.5 %collective-permute-start.11 = (bf16[400,384]{1,0:T(8,128)(2,1)S(1)}, bf16[400,384]{1,0:T(8,128)(2,1)S(1)}, u32[]{:S(2)}, u32[]{:S(2)}) collective-permute-start(bf16[400,384]{1,0:T(8,128)(2,1)S(1)} %get-tuple-element.40), channel_id=1, source_target_pairs={{0,4},{2,6},{4,0},{6,2},{8,12},{10,14},{12,8},{14,10},{16,20},{18,... | collective-permute-start | bytes 921608 | tf_op jit(solution)/shard_map/ppermute | solution.py:381
  26.7 1.2 %collective-permute-start.12 = (bf16[400,384]{1,0:T(8,128)(2,1)S(1)}, bf16[400,384]{1,0:T(8,128)(2,1)S(1)}, u32[]{:S(2)}, u32[]{:S(2)}) collective-permute-start(bf16[400,384]{1,0:T(8,128)(2,1)S(1)} %get-tuple-element.41), channel_id=1, source_target_pairs={{0,6},{2,4},{4,2},{6,0},{8,14},{10,12},{12,10},{14,8},{16,22},{18,... | collective-permute-start | bytes 921608 | tf_op jit(solution)/shard_map/ppermute | solution.py:381
  27.9 0.0 collective-permute-done.2.refs_0_.refs_1_
  27.9 0.0 collective-permute-done.3.refs_1_.refs_2_
  27.9 1.6 %shard_map.76 = (bf16[384,384]{1,0:T(8,128)(2,1)S(1)}, bf16[384,384]{1,0:T(8,128)(2,1)S(1)}) custom-call(bf16[384,384]{1,0:T(8,128)(2,1)S(1)} %get-tuple-element.37.refs_0_, bf16[384,384]{1,0:T(8,128)(2,1)S(1)} %collective-permute-done.2.refs_0_.refs_1_, bf16[384,384]{1,0:T(8,128)(2,1)S(1)} %collective-permute-done.3.refs_1_.refs_2_, ...), custom_call_target="tpu_custom_call" | custom-call | tf_op jit(solution)/shard_map/pallas_call | solution.py:42
  29.5 1.6 %collective-permute-start.8 = (bf16[384,384]{1,0:T(8,128)(2,1)S(1)}, bf16[384,384]{1,0:T(8,128)(2,1)S(1)}, u32[]{:S(2)}, u32[]{:S(2)}) collective-permute-start(bf16[384,384]{1,0:T(8,128)(2,1)S(1)} %get-tuple-element.38), channel_id=1, source_target_pairs={{0,8},{2,10},{4,12},{6,14},{8,0},{10,2},{12,4},{14,6},{16,24},{18,... | collective-permute-start | bytes 884744 | tf_op jit(solution)/shard_map/ppermute | solution.py:387
  31.2 0.7 %collective-permute-start.9 = (bf16[384,384]{1,0:T(8,128)(2,1)S(1)}, bf16[384,384]{1,0:T(8,128)(2,1)S(1)}, u32[]{:S(2)}, u32[]{:S(2)}) collective-permute-start(bf16[384,384]{1,0:T(8,128)(2,1)S(1)} %get-tuple-element.39), channel_id=1, source_target_pairs={{8,16},{10,18},{12,20},{14,22},{16,8},{18,10},{20,12},{22,14},{9,1... | collective-permute-start | bytes 884744 | tf_op jit(solution)/shard_map/ppermute | solution.py:387
  31.8 1.1 %shard_map.70.refs_0_ = f32[384,384]{1,0:T(8,128)S(1)} custom-call(bf16[384,384]{1,0:T(8,128)(2,1)S(1)} %collective-permute-done.2.refs_0_.refs_1_, bf16[384,384]{1,0:T(8,128)(2,1)S(1)} %collective-permute-done.3.refs_1_.refs_2_, bf16[384,384]{1,0:T(8,128)(2,1)S(1)} %collective-permute-done.5.refs_2_.refs_3_, bf16[3,384,384]{2,1,0:T(8,128)(2,1)S(1)} %copy-done, ...), custom_call_target="tpu_custom_call" | custom-call | tf_op jit(solution)/shard_map/pallas_call | solution.py:42
  33.0 0.7 %shard_map.71.refs_1_ = f32[384,384]{1,0:T(8,128)S(1)} custom-call(bf16[384,384]{1,0:T(8,128)(2,1)S(1)} %collective-permute-done.4.first_ref, bf16[384,384]{1,0:T(8,128)(2,1)S(1)} %collective-permute-done.6.second_ref, bf16[3,384,384]{2,1,0:T(8,128)(2,1)S(1)} %copy-done, s32[8,128]{1,0:T(8,128)S(1)} %get-tuple-element.27.refs_4_.places_ref.refs_5_, ...), custom_call_target="tpu_custom_call" | custom-call | tf_op jit(solution)/shard_map/pallas_call | solution.py:42
  33.7 3.1 %collective-permute-done.8.refs_2_ = bf16[384,384]{1,0:T(8,128)(2,1)S(1)} collective-permute-done((bf16[384,384]{1,0:T(8,128)(2,1)S(1)}, bf16[384,384]{1,0:T(8,128)(2,1)S(1)}, u32[]{:S(2)}, u32[]{:S(2)}) %collective-permute-start.8) | collective-permute-done | bytes 294944 | tf_op jit(solution)/shard_map/ppermute | solution.py:387
  36.8 0.0 collective-permute-done.9.refs_3_
  36.8 0.0 collective-permute-done.10.refs_6_
  36.8 2.3 %collective-permute-done.11.refs_7_ = bf16[400,384]{1,0:T(8,128)(2,1)S(1)} collective-permute-done((bf16[400,384]{1,0:T(8,128)(2,1)S(1)}, bf16[400,384]{1,0:T(8,128)(2,1)S(1)}, u32[]{:S(2)}, u32[]{:S(2)}) %collective-permute-start.11) | collective-permute-done | bytes 307232 | tf_op jit(solution)/shard_map/ppermute | solution.py:381
  39.1 1.0 %shard_map.77 = (bf16[384,768]{1,0:T(8,128)(2,1)}, f32[1,384]{1,0:T(1,128)}) custom-call(f32[384,384]{1,0:T(8,128)S(1)} %shard_map.70.refs_0_, f32[384,384]{1,0:T(8,128)S(1)} %shard_map.71.refs_1_, bf16[384,384]{1,0:T(8,128)(2,1)S(1)} %collective-permute-done.8.refs_2_, bf16[384,384]{1,0:T(8,128)(2,1)S(1)} %collective-permute-done.9.refs_3_, ...), custom_call_target="tpu_custom_call" | custom-call | tf_op jit(solution)/shard_map/pallas_call | solution.py:42
  (14 shorter events, 0.1 us)
Async XLA Ops:
  0.6 2.7 %copy-start.3 = (s32[3]{0:T(128)S(1)}, s32[3]{0:T(128)}, u32[]{:S(2)}) copy-start(s32[3]{0:T(128)} %offsets_ref.1) | copy-start | bytes 40
  0.6 2.7 %copy-start.4 = (f32[3]{0:T(128)S(1)}, f32[3]{0:T(128)}, u32[]{:S(2)}) copy-start(f32[3]{0:T(128)} %bose_ref.1) | copy-start | bytes 40
  0.7 4.0 %copy-start.1 = (bf16[1,384,768]{2,1,0:T(8,128)(2,1)S(1)}, bf16[1,384,768]{2,1,0:T(8,128)(2,1)}, u32[]{:S(2)}) copy-start(bf16[1,384,768]{2,1,0:T(8,128)(2,1)} %param.5) | copy-start | bytes 1769476
  0.7 4.0 %copy-start.2 = (bf16[384,384]{1,0:T(8,128)(2,1)S(1)}, bf16[384,384]{1,0:T(8,128)(2,1)}, u32[]{:S(2)}) copy-start(bf16[384,384]{1,0:T(8,128)(2,1)} %own_ref.1) | copy-start | bytes 884740
  0.7 4.0 %collective-permute-start = (bf16[384,768]{1,0:T(8,128)(2,1)}, bf16[384,768]{1,0:T(8,128)(2,1)S(1)}, u32[]{:S(2)}, u32[]{:S(2)}) collective-permute-start(bf16[384,768]{1,0:T(8,128)(2,1)} %bitcast.2), channel_id=1, source_target_pairs={{0,1},{1,0},{2,3},{3,2},{4,5},{5,4},{6,7},{7,6},{8,9},{9,8},{10,11... | collective-permute-start | bytes 1769480 | tf_op jit(solution)/shard_map/ppermute | solution.py:161
  1.2 3.5 %collective-permute-start.1 = (bf16[384,384]{1,0:T(8,128)(2,1)}, bf16[384,384]{1,0:T(8,128)(2,1)S(1)}, u32[]{:S(2)}, u32[]{:S(2)}) collective-permute-start(bf16[384,384]{1,0:T(8,128)(2,1)} %own_ref.1), channel_id=1, source_target_pairs={{0,1},{2,3},{4,5},{6,7},{8,9},{10,11},{12,13},{14,15},{16,17},{18,... | collective-permute-start | bytes 884744 | tf_op jit(solution)/shard_map/ppermute | solution.py:152
  4.7 17.7 %copy-start = (bf16[3,384,384]{2,1,0:T(8,128)(2,1)S(1)}, bf16[3,384,384]{2,1,0:T(8,128)(2,1)}, u32[]{:S(2)}) copy-start(bf16[3,384,384]{2,1,0:T(8,128)(2,1)} %refs_4_.1) | copy-start | bytes 2654212
  6.8 11.7 %collective-permute-start.5 = (bf16[384,384]{1,0:T(8,128)(2,1)S(1)}, bf16[384,384]{1,0:T(8,128)(2,1)S(1)}, u32[]{:S(2)}, u32[]{:S(2)}) collective-permute-start(bf16[384,384]{1,0:T(8,128)(2,1)S(1)} %get-tuple-element.37.refs_0_), channel_id=1, source_target_pairs={{0,6},{2,4},{4,2},{6,0},{8,14},{10,12},{12,10},{14,8},{16,22},{18,... | collective-permute-start | bytes 884744 | tf_op jit(solution)/shard_map/ppermute | solution.py:381
  10.7 9.1 %collective-permute-start.4 = (bf16[384,384]{1,0:T(8,128)(2,1)S(1)}, bf16[384,384]{1,0:T(8,128)(2,1)S(1)}, u32[]{:S(2)}, u32[]{:S(2)}) collective-permute-start(bf16[384,384]{1,0:T(8,128)(2,1)S(1)} %get-tuple-element.25.own_ref), channel_id=1, source_target_pairs={{0,8},{2,10},{4,12},{6,14},{8,0},{10,2},{12,4},{14,6},{16,24},{18,... | collective-permute-start | bytes 884744 | tf_op jit(solution)/shard_map/ppermute | solution.py:387
  12.2 10.2 %collective-permute-start.6 = (bf16[384,384]{1,0:T(8,128)(2,1)S(1)}, bf16[384,384]{1,0:T(8,128)(2,1)S(1)}, u32[]{:S(2)}, u32[]{:S(2)}) collective-permute-start(bf16[384,384]{1,0:T(8,128)(2,1)S(1)} %get-tuple-element.25.own_ref), channel_id=1, source_target_pairs={{8,16},{10,18},{12,20},{14,22},{16,8},{18,10},{20,12},{22,14},{9,1... | collective-permute-start | bytes 884744 | tf_op jit(solution)/shard_map/ppermute | solution.py:387
  12.9 15.0 %collective-permute-start.2 = (bf16[384,384]{1,0:T(8,128)(2,1)S(1)}, bf16[384,384]{1,0:T(8,128)(2,1)S(1)}, u32[]{:S(2)}, u32[]{:S(2)}) collective-permute-start(bf16[384,384]{1,0:T(8,128)(2,1)S(1)} %get-tuple-element.37.refs_0_), channel_id=1, source_target_pairs={{0,2},{2,0},{4,6},{6,4},{8,10},{10,8},{12,14},{14,12},{16,18},{18,... | collective-permute-start | bytes 884744 | tf_op jit(solution)/shard_map/ppermute | solution.py:381
  13.5 14.4 %collective-permute-start.3 = (bf16[384,384]{1,0:T(8,128)(2,1)S(1)}, bf16[384,384]{1,0:T(8,128)(2,1)S(1)}, u32[]{:S(2)}, u32[]{:S(2)}) collective-permute-start(bf16[384,384]{1,0:T(8,128)(2,1)S(1)} %get-tuple-element.37.refs_0_), channel_id=1, source_target_pairs={{0,4},{2,6},{4,0},{6,2},{8,12},{10,14},{12,8},{14,10},{16,20},{18,... | collective-permute-start | bytes 884744 | tf_op jit(solution)/shard_map/ppermute | solution.py:381
  19.8 4.5 %collective-permute-start.7 = (f32[1,384]{1,0:T(1,128)S(1)}, f32[1,384]{1,0:T(1,128)S(1)}, u32[]{:S(2)}, u32[]{:S(2)}) collective-permute-start(f32[1,384]{1,0:T(1,128)S(1)} %get-tuple-element.32), channel_id=1, source_target_pairs={{0,16},{2,18},{4,20},{6,22},{8,24},{10,26},{12,28},{14,30},{16,0},... | collective-permute-start | bytes 4616 | tf_op jit(solution)/shard_map/ppermute | solution.py:387
  24.4 12.4 %collective-permute-start.10 = (bf16[400,384]{1,0:T(8,128)(2,1)S(1)}, bf16[400,384]{1,0:T(8,128)(2,1)S(1)}, u32[]{:S(2)}, u32[]{:S(2)}) collective-permute-start(bf16[400,384]{1,0:T(8,128)(2,1)S(1)} %get-tuple-element.36), channel_id=1, source_target_pairs={{0,2},{2,0},{4,6},{6,4},{8,10},{10,8},{12,14},{14,12},{16,18},{18,... | collective-permute-start | bytes 921608 | tf_op jit(solution)/shard_map/ppermute | solution.py:381
  25.2 14.0 %collective-permute-start.11 = (bf16[400,384]{1,0:T(8,128)(2,1)S(1)}, bf16[400,384]{1,0:T(8,128)(2,1)S(1)}, u32[]{:S(2)}, u32[]{:S(2)}) collective-permute-start(bf16[400,384]{1,0:T(8,128)(2,1)S(1)} %get-tuple-element.40), channel_id=1, source_target_pairs={{0,4},{2,6},{4,0},{6,2},{8,12},{10,14},{12,8},{14,10},{16,20},{18,... | collective-permute-start | bytes 921608 | tf_op jit(solution)/shard_map/ppermute | solution.py:381
  26.7 12.5 %collective-permute-start.12 = (bf16[400,384]{1,0:T(8,128)(2,1)S(1)}, bf16[400,384]{1,0:T(8,128)(2,1)S(1)}, u32[]{:S(2)}, u32[]{:S(2)}) collective-permute-start(bf16[400,384]{1,0:T(8,128)(2,1)S(1)} %get-tuple-element.41), channel_id=1, source_target_pairs={{0,6},{2,4},{4,2},{6,0},{8,14},{10,12},{12,10},{14,8},{16,22},{18,... | collective-permute-start | bytes 921608 | tf_op jit(solution)/shard_map/ppermute | solution.py:381
  29.5 7.3 %collective-permute-start.8 = (bf16[384,384]{1,0:T(8,128)(2,1)S(1)}, bf16[384,384]{1,0:T(8,128)(2,1)S(1)}, u32[]{:S(2)}, u32[]{:S(2)}) collective-permute-start(bf16[384,384]{1,0:T(8,128)(2,1)S(1)} %get-tuple-element.38), channel_id=1, source_target_pairs={{0,8},{2,10},{4,12},{6,14},{8,0},{10,2},{12,4},{14,6},{16,24},{18,... | collective-permute-start | bytes 884744 | tf_op jit(solution)/shard_map/ppermute | solution.py:387
  31.2 5.6 %collective-permute-start.9 = (bf16[384,384]{1,0:T(8,128)(2,1)S(1)}, bf16[384,384]{1,0:T(8,128)(2,1)S(1)}, u32[]{:S(2)}, u32[]{:S(2)}) collective-permute-start(bf16[384,384]{1,0:T(8,128)(2,1)S(1)} %get-tuple-element.39), channel_id=1, source_target_pairs={{8,16},{10,18},{12,20},{14,22},{16,8},{18,10},{20,12},{22,14},{9,1... | collective-permute-start | bytes 884744 | tf_op jit(solution)/shard_map/ppermute | solution.py:387

commit v5 on v4

--- a/solution.py
+++ b/solution.py
@@ -10,6 +10,8 @@
 OMAX = 4
 GROUP = OMAX
 EXTRA = 16
+EXTRA_C = 16
+EXTRA_B = 16
 LANES = 128
 VMEM_LIMIT = 16 * 1024 * 1024
 
@@ -77,9 +79,12 @@
     return 1.0 / (1.0 + jnp.exp(-((position + 0.5 - energies / 2) * 4.0 / energies)))
 
 
-def prepare(energies, offsets_ref, bose_ref, holes_out, places_out, factors_out):
+def hole_line(energies, out):
+    out[...] = holes_at(lax.axis_index("energy"), energies, out.shape)
+
+
+def mode_table(offsets_ref, bose_ref, places_out, factors_out):
     assert offsets_ref.shape == (3,)
-    holes_out[...] = holes_at(lax.axis_index("energy"), energies, holes_out.shape)
     far = jnp.where(offsets_ref[1] == GROUP, 1, jnp.where(offsets_ref[2] == GROUP, 2, 0))
     one, two = jnp.where(far == 0, 1, 0), jnp.where(far == 2, 1, 2)
     odd = jnp.where(lax.rem(offsets_ref[one], 2) == 1, one, two)
@@ -113,21 +118,26 @@
     dos_ref[...] = -holes_ref[...] * diagonal_of(imag_ref)
 
 
-def greens_of_pair(g_ref, other_ref, own_ref, below_ref, holes_ref, *rest):
+def greens_of_first(g_ref, other_ref, own_ref, holes_ref, *rest):
     *outs, couple = rest
-    m = own_ref.shape[0]
-    slab = lax.axis_index("slab")
-
-    @pl.when(slab == 0)
+
+    @pl.when(lax.axis_index("slab") == 0)
     def _():
+        m = own_ref.shape[0]
         couple[:, :m], couple[:, m:] = upper_term(own_ref[...], other_ref[...])
-
-    @pl.when(slab != 0)
+        g = g_ref[...]
+        finish(g, bf(complex_product(g, couple[...])), holes_ref, *outs)
+
+
+def greens_of_second(g_ref, other_ref, below_ref, holes_ref, *rest):
+    *outs, couple = rest[3:]
+
+    @pl.when(lax.axis_index("slab") != 0)
     def _():
+        m = below_ref.shape[0]
         couple[:, :m], couple[:, m:] = lower_term(below_ref[...], other_ref[...])
-
-    g = g_ref[...]
-    finish(g, bf(complex_product(g, couple[...])), holes_ref, *outs)
+        g = g_ref[...]
+        finish(g, bf(complex_product(g, couple[...])), holes_ref, *outs)
 
 
 def greens_of_chain(g_ref, above_ref, lower_ref, own_ref, below_ref, holes_ref, *outs):
@@ -140,32 +150,26 @@
     finish(g, bf(complex_product(g, couple)), holes_ref, *outs)
 
 
-def greens_halves(g, coupling, offsets, bose_factors):
+def greens_halves(g, coupling):
     m = g.shape[0]
     slabs = lax.axis_size("slab")
     half = jax.ShapeDtypeStruct((m, m), jnp.bfloat16)
     line = jax.ShapeDtypeStruct((1, m), jnp.float32)
-    places = jax.ShapeDtypeStruct((8, LANES), jnp.int32)
-    factors = jax.ShapeDtypeStruct((8, LANES), jnp.float32)
+    outs = [half, half, line]
     up = [(s, s + 1) for s in range(slabs - 1)]
     down = [(s + 1, s) for s in range(slabs - 1)]
     below = lax.ppermute(coupling, "slab", up)
     energies = lax.axis_size("energy")
-    holes, *table = call(
-        functools.partial(prepare, energies),
-        [line, places, factors],
-        [offsets, bose_factors],
-        flops=24 * m**3,
-    )
+    (holes,) = call(functools.partial(hole_line, energies), [line], [], flops=24 * m**3)
     if slabs == 2:
         other = lax.ppermute(g, "slab", up + down)
         couple = [pltpu.VMEM(g.shape, jnp.bfloat16)]
-        ins = [g, other, coupling, below, holes]
-        return *call(greens_of_pair, [half, half, line], ins, couple), table
+        first = call(greens_of_first, outs, [g, other, coupling, holes], couple)
+        ins = [g, other, below, holes, *first]
+        return call(greens_of_second, outs, ins, couple, aliases={4: 0, 5: 1, 6: 2})
     above = lax.ppermute(g, "slab", down)
     lower = lax.ppermute(g, "slab", up)
-    ins = [g, above, lower, coupling, below, holes]
-    return *call(greens_of_chain, [half, half, line], ins), table
+    return call(greens_of_chain, outs, [g, above, lower, coupling, below, holes])
 
 
 def place():
@@ -173,6 +177,11 @@
     group = lax.div(energy, jnp.int32(GROUP))
     seat = lax.rem(energy, jnp.int32(GROUP))
     return energy, group, seat
+
+
+def hops():
+    bit = 2 - lax.rem(lax.axis_index("slab"), 2)
+    return bit, (GROUP - 1) - bit
 
 
 def first_side(group):
@@ -198,7 +207,7 @@
 
 
 def to_seats(own_ref, first_ref, second_ref, phonon_ref, places_ref, factors_ref, *rest):
-    *outs, bank = rest
+    across, direct, merged, bank, sums = rest
     m = own_ref.shape[0]
     _, group, seat = place()
     side = first_side(group)
@@ -216,7 +225,7 @@
     def odd_seats(mode):
         index, shift, factor = mode
         blocks, weights = [], []
-        for j in range(1, GROUP, 2):
+        for j in (1, 3):
             size, upward, beside = towards(j)
             own = shift == size
             blocks.append(bank[jnp.where(own, 0, beside)])
@@ -227,38 +236,49 @@
         return nt(jnp.concatenate(parts, axis=0), matrix)
 
     def put(wide):
-        for j in range(1, GROUP, 2):
-            outs[j - 1][:m] = bf(wide[j // 2 * m : (j // 2 + 1) * m])
+        sums[0] = bf(wide[:m])
+        across[:m] = bf(wide[m:])
 
     index, shift, factor = left
 
     @pl.when(lax.rem(shift, 2) == 0)
     def _():
         wide = odd_seats(odd)
-        for j in range(2, GROUP, 2):
-            _, upward, beside = towards(j)
-            own_weight = jnp.where(upward, factor + 1.0, factor)
-            beside_weight = jnp.where(upward, factor, factor + 1.0)
-            block = mixed(bank[0], own_weight, bank[beside], beside_weight)
-            outs[j - 1][:m] = bf(product(phonon_ref[index], block))
+        _, upward, beside = towards(2)
+        own_weight = jnp.where(upward, factor + 1.0, factor)
+        beside_weight = jnp.where(upward, factor, factor + 1.0)
+        block = mixed(bank[0], own_weight, bank[beside], beside_weight)
+        sums[1] = bf(product(phonon_ref[index], block))
         put(wide)
 
     @pl.when(lax.rem(shift, 2) == 1)
     def _():
         put(odd_seats(odd) + odd_seats(left))
-        for j in range(2, GROUP, 2):
-            outs[j - 1][:m] = jnp.zeros((m, m), jnp.bfloat16)
-
-    for out in outs:
-        out[m:] = jnp.zeros((EXTRA, m), jnp.bfloat16)
+        sums[1] = jnp.zeros((m, m), jnp.bfloat16)
+
+    first, second = hops()
+    direct[:m] = sums[first - 1]
+    merged[:m] = sums[second - 1]
+    for out in (across, direct, merged):
+        out[m:] = jnp.zeros((out.shape[0] - m, m), jnp.bfloat16)
 
 
 def with_lines(dos_ref, before_ref, *refs):
     m = dos_ref.shape[1]
     _, _, seat = place()
-    for j, out in enumerate(refs[GROUP - 1 :], 1):
+    first, second = hops()
+    for out, j in zip(refs[3:], (GROUP - 1, first, second)):
         counts = jnp.bitwise_xor(seat, j) > seat
-        out[m:] = split_rows(before_ref[...] + jnp.where(counts, dos_ref[...], 0.0))
+        out[m : m + EXTRA] = split_rows(
+            before_ref[...] + jnp.where(counts, dos_ref[...], 0.0)
+        )
+
+
+def merge(received_ref, merged_ref, out):
+    m = received_ref.shape[1]
+    out[:m] = bf(f32(merged_ref[:m]) + f32(received_ref[:m]))
+    lines = f32(merged_ref[m : m + EXTRA]) + f32(received_ref[m : m + EXTRA])
+    out[m : m + EXTRA] = split_rows(jnp.sum(lines, axis=0, keepdims=True))
 
 
 def to_groups(*refs):
@@ -266,7 +286,8 @@
     first_out, second_out, bank, total = refs[GROUP + 3 :]
     _, group, seat = place()
     upward = seat < GROUP // 2
-    for j, part in enumerate(parts):
+    first, second = hops()
+    for j, part in zip((0, first, second, GROUP - 1), parts):
         bank[j] = part[...]
     modes = modes_of(phonon_ref, places_ref, factors_ref)
 
@@ -295,8 +316,11 @@
             total[1] += product(phonon_ref[index], bank[place_of], weight)
 
     most_first = upward == (first_side(group) > 0)
-    first_out[...] = bf(total[jnp.where(most_first, 0, 1)])
-    second_out[...] = bf(total[jnp.where(most_first, 1, 0)])
+    m = bank.shape[1]
+    first_out[:m] = bf(total[jnp.where(most_first, 0, 1)])
+    second_out[:m] = bf(total[jnp.where(most_first, 1, 0)])
+    for out in (first_out, second_out) if first_out.shape[0] > m else ():
+        out[m:] = jnp.zeros((out.shape[0] - m, m), jnp.bfloat16)
 
 
 def column_terms(first_ref, second_ref, phonon_ref, places_ref, factors_ref, out):
@@ -312,8 +336,9 @@
 def group_terms(*refs):
     parts, (phonon_ref, places_ref, factors_ref, out, bank) = refs[: GROUP - 1], refs[GROUP - 1 :]
     _, _, seat = place()
-    for j, part in enumerate(parts):
-        bank[j] = part[...]
+    first, second = hops()
+    for j, part in zip((first, second, GROUP - 1), parts):
+        bank[j - 1] = part[...]
     sum_of_modes = None
     for index, shift, factor in modes_of(phonon_ref, places_ref, factors_ref)[1:]:
         below, above = seat - shift, seat + shift
@@ -358,7 +383,7 @@
     m = real_total.shape[0]
     density = before[...] + dos[...]
     for part in seats:
-        density = density + jnp.sum(f32(part[m:]), axis=0, keepdims=True)
+        density = density + jnp.sum(f32(part[m : m + EXTRA]), axis=0, keepdims=True)
     line[...] = density
     copies = [pltpu.make_async_copy(line, cumulative, line_sem)]
     copies[0].start()
@@ -376,9 +401,17 @@
         copy.wait()
 
 
-def across_seats(value, j):
-    energies = lax.axis_size("energy")
-    return lax.ppermute(value, "energy", [(e, e ^ j) for e in range(energies)])
+def hop(value, second):
+    energies, slabs = lax.axis_size("energy"), lax.axis_size("slab")
+    bits = [2 - slab % 2 for slab in range(slabs)]
+    if second:
+        bits = [GROUP - 1 - bit for bit in bits]
+    pairs = [
+        (e * slabs + slab, (e ^ bit) * slabs + slab)
+        for e in range(energies)
+        for slab, bit in enumerate(bits)
+    ]
+    return lax.ppermute(value, ("energy", "slab"), pairs)
 
 
 def across_groups(value, partner):
@@ -414,13 +447,18 @@
     def totals(blocks):
         return pltpu.VMEM((blocks, m, m), jnp.float32)
 
-    real, imag, dos, table = greens_halves(g, coupling, offsets, bose_factors)
+    real, imag, dos = greens_halves(g, coupling)
+    places = jax.ShapeDtypeStruct((8, LANES), jnp.int32)
+    factors = jax.ShapeDtypeStruct((8, LANES), jnp.float32)
+    table = call(mode_table, [places, factors], [offsets, bose_factors])
     modes = [phonon_coupling, *table]
     first_imag = across_groups(imag, first_pair)
     second_imag = across_groups(imag, second_pair)
-    reals = [real] + [across_seats(real, j) for j in range(1, GROUP)]
-
-    first_imag, reals[-1] = lax.optimization_barrier((first_imag, reals[-1]))
+    near = hop(real, False)
+    reals = [real, near, hop(real, True), hop(near, True)]
+
+    first_imag, reals[1], *table = lax.optimization_barrier((first_imag, reals[1], *table))
+    modes = [phonon_coupling, *table]
 
     group_sum, dos_first = call(
         functools.partial(column_sums, lax.axis_size("energy")), [line, line], [first_imag, dos]
@@ -433,25 +471,27 @@
         received.append(across_groups(group_sum, lambda a, step=step: a ^ step))
         step *= 2
 
+    heights = (m + EXTRA, m + EXTRA + EXTRA_B, m + EXTRA)
+    taller = [jax.ShapeDtypeStruct((h, m), jnp.bfloat16) for h in heights]
+    second_imag, reals[2] = lax.optimization_barrier((second_imag, reals[2]))
     sums = call(
         to_seats,
-        [taller] * (GROUP - 1),
+        taller,
         [imag, first_imag, second_imag, *modes],
-        [bank(3)],
+        [bank(3), bank(2)],
     )
     (imag_total,) = call(column_terms, [wide], [first_imag, second_imag, *modes])
+    received[-1], reals[3], *sums = lax.optimization_barrier((received[-1], reals[3], *sums))
     (before,) = call(sums_before, [line], received)
-    sums = call(
-        with_lines,
-        [taller] * (GROUP - 1),
-        [dos, before, *sums],
-        aliases={2 + i: i for i in range(GROUP - 1)},
-    )
-    seat_terms = [across_seats(value, j) for j, value in enumerate(sums, 1)]
+    sums = call(with_lines, taller, [dos, before, *sums], aliases={2: 0, 3: 1, 4: 2})
+    direct_term = hop(sums[1], False)
+    (merged,) = call(merge, taller[2:], [hop(sums[0], False), sums[2]])
+    seat_terms = [direct_term, hop(merged, True)]
 
     reals[0], _ = lax.optimization_barrier((reals[0], sums[0]))
+    for_groups = jax.ShapeDtypeStruct((m + EXTRA_C, m), jnp.bfloat16)
     first_out, second_out = call(
-        to_groups, [half, half], [*reals, *modes], [bank(GROUP), totals(2)]
+        to_groups, [for_groups] * 2, [*reals, *modes], [bank(GROUP), totals(2)]
     )
     first_term = across_groups(first_out, first_pair)
     second_term = across_groups(second_out, second_pair)

time: 40.3 us -> 38.2 us (0.948)
  the two profiles are of different devices: /device:TPU:0 before, /device:TPU:10 now
where the time goes in v5:
time: 38.2 us; the launch traced here: 37.6 us
  starting transfers between devices  20.8 us (54%)
  Pallas kernels  8.6 us (23%)
  waiting for transfers between devices  7.29 us (19%)
  between operations  0.82 us (2%)
    ppermute x5, starting transfers between devices, across_groups(): lax.ppermute(value, 'energy', [(GROUP * a + i, GROUP * b + i) for a, b in...  11.7 us
    pallas_call x13, Pallas kernels, call(): pl.pallas_call(kernel, out_shape=outs, in_specs=[SCALARS if i.ndim == 1 e...  8.6 us
    ppermute x6, starting transfers between devices, hop(): return lax.ppermute(value, ('energy', 'slab'), pairs)  6.6 us
    ppermute x5, waiting for transfers between devices, across_groups(): lax.ppermute(value, 'energy', [(GROUP * a + i, GROUP * b + i) for a, b in...  5.66 us
    ppermute x1, starting transfers between devices, greens_halves(): below = lax.ppermute(coupling, 'slab', up)  2.41 us
    ppermute x6, waiting for transfers between devices, hop(): return lax.ppermute(value, ('energy', 'slab'), pairs)  1.62 us
  transfers between devices with their start and end apart: 13, of which 6 were waited for; matrix products, arithmetic and copies ran while one was open for 0% of the time, Pallas kernels for 20%

profile of v5, /device:TPU:10, one launch (start us, length us, event | category | flops | bytes accessed | tf_op | source)
XLA Modules:
  0.0 37.6 jit_solution(1575801070838371530)
XLA Ops:
  0.6 0.1 collective-permute-start
  0.7 2.4 %collective-permute-start.1 = (bf16[384,384]{1,0:T(8,128)(2,1)}, bf16[384,384]{1,0:T(8,128)(2,1)S(1)}, u32[]{:S(2)}, u32[]{:S(2)}) collective-permute-start(bf16[384,384]{1,0:T(8,128)(2,1)} %own_ref.1), channel_id=1, source_target_pairs={{0,1},{2,3},{4,5},{6,7},{8,9},{10,11},{12,13},{14,15},{16,17},{18,... | collective-permute-start | bytes 884744 | tf_op jit(solution)/shard_map/ppermute | solution.py:161
  3.2 0.0 collective-permute-done.other_ref
  3.2 2.0 %shard_map.69 = (bf16[384,384]{1,0:T(8,128)(2,1)S(1)}, bf16[384,384]{1,0:T(8,128)(2,1)S(1)}, f32[1,384]{1,0:T(1,128)S(1)}) custom-call(bf16[384,768]{1,0:T(8,128)(2,1)S(1)} %bitcast.3, bf16[384,768]{1,0:T(8,128)(2,1)S(1)} %collective-permute-done.other_ref, bf16[384,384]{1,0:T(8,128)(2,1)S(1)} %copy-done.2, f32[1,384]{1,0:T(1,128)S(1)} %shard_map.68.holes_ref), custom_call_target="tpu_custom_call" | custom-call | tf_op jit(solution)/shard_map/pallas_call | solution.py:44
  5.2 0.0 collective-permute-done.1.below_ref
  5.2 0.0 copy-start
  5.2 0.0 copy-start.3
  5.2 0.0 copy-start.4
  5.2 1.6 %collective-permute-start.3 = (bf16[384,384]{1,0:T(8,128)(2,1)S(1)}, bf16[384,384]{1,0:T(8,128)(2,1)S(1)}, u32[]{:S(2)}, u32[]{:S(2)}) collective-permute-start(bf16[384,384]{1,0:T(8,128)(2,1)S(1)} %get-tuple-element.59.refs_0_), channel_id=1, source_target_pairs={{0,4},{1,3},{2,6},{3,1},{4,0},{5,7},{6,2},{7,5},{8,12},{9,11},{10,... | collective-permute-start | bytes 884744 | tf_op jit(solution)/shard_map/ppermute | solution.py:414
  6.8 0.4 %collective-permute-start.2 = (bf16[384,384]{1,0:T(8,128)(2,1)S(1)}, bf16[384,384]{1,0:T(8,128)(2,1)S(1)}, u32[]{:S(2)}, u32[]{:S(2)}) collective-permute-start(bf16[384,384]{1,0:T(8,128)(2,1)S(1)} %get-tuple-element.37.own_ref), channel_id=1, source_target_pairs={{0,8},{2,10},{4,12},{6,14},{8,0},{10,2},{12,4},{14,6},{16,24},{18,... | collective-permute-start | bytes 884744 | tf_op jit(solution)/shard_map/ppermute | solution.py:420
  7.3 4.6 %collective-permute-start.4 = (bf16[384,384]{1,0:T(8,128)(2,1)S(1)}, bf16[384,384]{1,0:T(8,128)(2,1)S(1)}, u32[]{:S(2)}, u32[]{:S(2)}) collective-permute-start(bf16[384,384]{1,0:T(8,128)(2,1)S(1)} %get-tuple-element.37.own_ref), channel_id=1, source_target_pairs={{8,16},{10,18},{12,20},{14,22},{16,8},{18,10},{20,12},{22,14},{9,1... | collective-permute-start | bytes 884744 | tf_op jit(solution)/shard_map/ppermute | solution.py:420
  11.9 0.6 %collective-permute-start.5 = (bf16[384,384]{1,0:T(8,128)(2,1)S(1)}, bf16[384,384]{1,0:T(8,128)(2,1)S(1)}, u32[]{:S(2)}, u32[]{:S(2)}) collective-permute-start(bf16[384,384]{1,0:T(8,128)(2,1)S(1)} %get-tuple-element.59.refs_0_), channel_id=1, source_target_pairs={{0,2},{1,5},{2,0},{3,7},{4,6},{5,1},{6,4},{7,3},{8,10},{9,13},{10,... | collective-permute-start | bytes 884744 | tf_op jit(solution)/shard_map/ppermute | solution.py:414
  12.5 1.5 %collective-permute-start.7 = (bf16[384,384]{1,0:T(8,128)(2,1)S(1)}, bf16[384,384]{1,0:T(8,128)(2,1)S(1)}, u32[]{:S(2)}, u32[]{:S(2)}) collective-permute-start(bf16[384,384]{1,0:T(8,128)(2,1)S(1)} %collective-permute-done.3.refs_0_.refs_1_), channel_id=1, source_target_pairs={{0,2},{1,5},{2,0},{3,7},{4,6},{5,1},{6,4},{7,3},{8,10},{9,13},{10,... | collective-permute-start | bytes 884744 | tf_op jit(solution)/shard_map/ppermute | solution.py:414
  14.0 0.6 %shard_map.71 = (s32[8,128]{1,0:T(8,128)S(1)}, f32[8,128]{1,0:T(8,128)S(1)}) custom-call(s32[3]{0:T(128)S(1)} %copy-done.3, f32[3]{0:T(128)S(1)} %copy-done.4), custom_call_target="tpu_custom_call" | custom-call | tf_op jit(solution)/shard_map/pallas_call | solution.py:44
  14.5 1.6 %collective-permute-done.2.first_ref = bf16[384,384]{1,0:T(8,128)(2,1)S(1)} collective-permute-done((bf16[384,384]{1,0:T(8,128)(2,1)S(1)}, bf16[384,384]{1,0:T(8,128)(2,1)S(1)}, u32[]{:S(2)}, u32[]{:S(2)}) %collective-permute-start.2) | collective-permute-done | bytes 294944 | tf_op jit(solution)/shard_map/ppermute | solution.py:420
  16.2 2.7 %collective-permute-start.6 = (f32[1,384]{1,0:T(1,128)S(1)}, f32[1,384]{1,0:T(1,128)S(1)}, u32[]{:S(2)}, u32[]{:S(2)}) collective-permute-start(f32[1,384]{1,0:T(1,128)S(1)} %get-tuple-element.45), channel_id=1, source_target_pairs={{0,16},{2,18},{4,20},{6,22},{8,24},{10,26},{12,28},{14,30},{16,0},... | collective-permute-start | bytes 4616 | tf_op jit(solution)/shard_map/ppermute | solution.py:420
  18.9 0.3 collective-permute-done.4.second_ref
  19.2 1.5 %shard_map.73 = (bf16[400,384]{1,0:T(8,128)(2,1)S(1)}, bf16[416,384]{1,0:T(8,128)(2,1)S(1)}, bf16[400,384]{1,0:T(8,128)(2,1)S(1)}) custom-call(bf16[384,384]{1,0:T(8,128)(2,1)S(1)} %get-tuple-element.37.own_ref, bf16[384,384]{1,0:T(8,128)(2,1)S(1)} %collective-permute-done.2.first_ref, bf16[384,384]{1,0:T(8,128)(2,1)S(1)} %collective-permute-done.4.second_ref, ...), custom_call_target="tpu_custom_call" | custom-call | tf_op jit(solution)/shard_map/pallas_call | solution.py:44
  20.8 1.1 %collective-permute-done.7.refs_2_.refs_3_ = bf16[384,384]{1,0:T(8,128)(2,1)S(1)} collective-permute-done((bf16[384,384]{1,0:T(8,128)(2,1)S(1)}, bf16[384,384]{1,0:T(8,128)(2,1)S(1)}, u32[]{:S(2)}, u32[]{:S(2)}) %collective-permute-start.7) | collective-permute-done | bytes 294944 | tf_op jit(solution)/shard_map/ppermute | solution.py:414
  21.9 0.6 %collective-permute-start.11 = (bf16[400,384]{1,0:T(8,128)(2,1)S(1)}, bf16[400,384]{1,0:T(8,128)(2,1)S(1)}, u32[]{:S(2)}, u32[]{:S(2)}) collective-permute-start(bf16[400,384]{1,0:T(8,128)(2,1)S(1)} %get-tuple-element.58), channel_id=1, source_target_pairs={{0,4},{1,3},{2,6},{3,1},{4,0},{5,7},{6,2},{7,5},{8,12},{9,11},{10,... | collective-permute-start | bytes 921608 | tf_op jit(solution)/shard_map/ppermute | solution.py:414
  22.5 1.5 %collective-permute-start.10 = (bf16[416,384]{1,0:T(8,128)(2,1)S(1)}, bf16[416,384]{1,0:T(8,128)(2,1)S(1)}, u32[]{:S(2)}, u32[]{:S(2)}) collective-permute-start(bf16[416,384]{1,0:T(8,128)(2,1)S(1)} %get-tuple-element.62), channel_id=1, source_target_pairs={{0,4},{1,3},{2,6},{3,1},{4,0},{5,7},{6,2},{7,5},{8,12},{9,11},{10,... | collective-permute-start | bytes 958472 | tf_op jit(solution)/shard_map/ppermute | solution.py:414
  24.0 1.6 %shard_map.78 = (bf16[400,384]{1,0:T(8,128)(2,1)S(1)}, bf16[400,384]{1,0:T(8,128)(2,1)S(1)}) custom-call(bf16[384,384]{1,0:T(8,128)(2,1)S(1)} %get-tuple-element.59.refs_0_, bf16[384,384]{1,0:T(8,128)(2,1)S(1)} %collective-permute-done.3.refs_0_.refs_1_, bf16[384,384]{1,0:T(8,128)(2,1)S(1)} %collective-permute-done.5.refs_1_.refs_2_, ...), custom_call_target="tpu_custom_call" | custom-call | tf_op jit(solution)/shard_map/pallas_call | solution.py:44
  25.6 0.1 collective-permute-start.8
  25.6 4.0 %collective-permute-start.9 = (bf16[400,384]{1,0:T(8,128)(2,1)S(1)}, bf16[400,384]{1,0:T(8,128)(2,1)S(1)}, u32[]{:S(2)}, u32[]{:S(2)}) collective-permute-start(bf16[400,384]{1,0:T(8,128)(2,1)S(1)} %get-tuple-element.61), channel_id=1, source_target_pairs={{8,16},{10,18},{12,20},{14,22},{16,8},{18,10},{20,12},{22,14},{9,1... | collective-permute-start | bytes 921608 | tf_op jit(solution)/shard_map/ppermute | solution.py:420
  29.6 0.1 shard_map.79
  29.7 0.8 %collective-permute-start.12 = (bf16[400,384]{1,0:T(8,128)(2,1)S(1)}, bf16[400,384]{1,0:T(8,128)(2,1)S(1)}, u32[]{:S(2)}, u32[]{:S(2)}) collective-permute-start(bf16[400,384]{1,0:T(8,128)(2,1)S(1)} %shard_map.79), channel_id=1, source_target_pairs={{0,2},{1,5},{2,0},{3,7},{4,6},{5,1},{6,4},{7,3},{8,10},{9,13},{10,... | collective-permute-start | bytes 921608 | tf_op jit(solution)/shard_map/ppermute | solution.py:414
  30.6 0.7 %shard_map.75.refs_1_ = f32[384,384]{1,0:T(8,128)S(1)} custom-call(bf16[384,384]{1,0:T(8,128)(2,1)S(1)} %collective-permute-done.2.first_ref, bf16[384,384]{1,0:T(8,128)(2,1)S(1)} %collective-permute-done.4.second_ref, bf16[3,384,384]{2,1,0:T(8,128)(2,1)S(1)} %copy-done, s32[8,128]{1,0:T(8,128)S(1)} %get-tuple-element.47.places_ref.refs_4_.refs_5_, ...), custom_call_target="tpu_custom_call" | custom-call | tf_op jit(solution)/shard_map/pallas_call | solution.py:44
  31.3 1.1 %shard_map.74.refs_0_ = f32[384,384]{1,0:T(8,128)S(1)} custom-call(bf16[384,384]{1,0:T(8,128)(2,1)S(1)} %collective-permute-done.3.refs_0_.refs_1_, bf16[384,384]{1,0:T(8,128)(2,1)S(1)} %collective-permute-done.5.refs_1_.refs_2_, bf16[384,384]{1,0:T(8,128)(2,1)S(1)} %collective-permute-done.7.refs_2_.refs_3_, bf16[3,384,384]{2,1,0:T(8,128)(2,1)S(1)} %copy-done, ...), custom_call_target="tpu_custom_call" | custom-call | tf_op jit(solution)/shard_map/pallas_call | solution.py:44
  32.4 0.9 %collective-permute-done.8.refs_2_ = bf16[400,384]{1,0:T(8,128)(2,1)S(1)} collective-permute-done((bf16[400,384]{1,0:T(8,128)(2,1)S(1)}, bf16[400,384]{1,0:T(8,128)(2,1)S(1)}, u32[]{:S(2)}, u32[]{:S(2)}) %collective-permute-start.8) | collective-permute-done | bytes 307232 | tf_op jit(solution)/shard_map/ppermute | solution.py:420
  33.3 2.8 %collective-permute-done.9.refs_3_ = bf16[400,384]{1,0:T(8,128)(2,1)S(1)} collective-permute-done((bf16[400,384]{1,0:T(8,128)(2,1)S(1)}, bf16[400,384]{1,0:T(8,128)(2,1)S(1)}, u32[]{:S(2)}, u32[]{:S(2)}) %collective-permute-start.9) | collective-permute-done | bytes 307232 | tf_op jit(solution)/shard_map/ppermute | solution.py:420
  36.1 0.6 %collective-permute-done.12.refs_7_ = bf16[400,384]{1,0:T(8,128)(2,1)S(1)} collective-permute-done((bf16[400,384]{1,0:T(8,128)(2,1)S(1)}, bf16[400,384]{1,0:T(8,128)(2,1)S(1)}, u32[]{:S(2)}, u32[]{:S(2)}) %collective-permute-start.12) | collective-permute-done | bytes 307232 | tf_op jit(solution)/shard_map/ppermute | solution.py:414
  36.7 0.9 %shard_map.80 = (bf16[384,768]{1,0:T(8,128)(2,1)}, f32[1,384]{1,0:T(1,128)}) custom-call(f32[384,384]{1,0:T(8,128)S(1)} %shard_map.74.refs_0_, f32[384,384]{1,0:T(8,128)S(1)} %shard_map.75.refs_1_, bf16[400,384]{1,0:T(8,128)(2,1)S(1)} %collective-permute-done.8.refs_2_, bf16[400,384]{1,0:T(8,128)(2,1)S(1)} %collective-permute-done.9.refs_3_, ...), custom_call_target="tpu_custom_call" | custom-call | tf_op jit(solution)/shard_map/pallas_call | solution.py:44
  (17 shorter events, 0.2 us)
Async XLA Ops:
  0.6 2.6 %copy-start.1 = (bf16[1,384,768]{2,1,0:T(8,128)(2,1)S(1)}, bf16[1,384,768]{2,1,0:T(8,128)(2,1)}, u32[]{:S(2)}) copy-start(bf16[1,384,768]{2,1,0:T(8,128)(2,1)} %param.5) | copy-start | bytes 1769476
  0.6 2.6 %copy-start.2 = (bf16[384,384]{1,0:T(8,128)(2,1)S(1)}, bf16[384,384]{1,0:T(8,128)(2,1)}, u32[]{:S(2)}) copy-start(bf16[384,384]{1,0:T(8,128)(2,1)} %own_ref.1) | copy-start | bytes 884740
  0.6 2.5 %collective-permute-start = (bf16[384,768]{1,0:T(8,128)(2,1)}, bf16[384,768]{1,0:T(8,128)(2,1)S(1)}, u32[]{:S(2)}, u32[]{:S(2)}) collective-permute-start(bf16[384,768]{1,0:T(8,128)(2,1)} %bitcast.2), channel_id=1, source_target_pairs={{0,1},{1,0},{2,3},{3,2},{4,5},{5,4},{6,7},{7,6},{8,9},{9,8},{10,11... | collective-permute-start | bytes 1769480 | tf_op jit(solution)/shard_map/ppermute | solution.py:165
  0.7 4.4 %collective-permute-start.1 = (bf16[384,384]{1,0:T(8,128)(2,1)}, bf16[384,384]{1,0:T(8,128)(2,1)S(1)}, u32[]{:S(2)}, u32[]{:S(2)}) collective-permute-start(bf16[384,384]{1,0:T(8,128)(2,1)} %own_ref.1), channel_id=1, source_target_pairs={{0,1},{2,3},{4,5},{6,7},{8,9},{10,11},{12,13},{14,15},{16,17},{18,... | collective-permute-start | bytes 884744 | tf_op jit(solution)/shard_map/ppermute | solution.py:161
  5.2 14.0 %copy-start = (bf16[3,384,384]{2,1,0:T(8,128)(2,1)S(1)}, bf16[3,384,384]{2,1,0:T(8,128)(2,1)}, u32[]{:S(2)}) copy-start(bf16[3,384,384]{2,1,0:T(8,128)(2,1)} %refs_4_.1) | copy-start | bytes 2654212
  5.2 8.8 %copy-start.3 = (s32[3]{0:T(128)S(1)}, s32[3]{0:T(128)}, u32[]{:S(2)}) copy-start(s32[3]{0:T(128)} %offsets_ref.1) | copy-start | bytes 40
  5.2 8.8 %copy-start.4 = (f32[3]{0:T(128)S(1)}, f32[3]{0:T(128)}, u32[]{:S(2)}) copy-start(f32[3]{0:T(128)} %bose_ref.1) | copy-start | bytes 40
  5.2 7.2 %collective-permute-start.3 = (bf16[384,384]{1,0:T(8,128)(2,1)S(1)}, bf16[384,384]{1,0:T(8,128)(2,1)S(1)}, u32[]{:S(2)}, u32[]{:S(2)}) collective-permute-start(bf16[384,384]{1,0:T(8,128)(2,1)S(1)} %get-tuple-element.59.refs_0_), channel_id=1, source_target_pairs={{0,4},{1,3},{2,6},{3,1},{4,0},{5,7},{6,2},{7,5},{8,12},{9,11},{10,... | collective-permute-start | bytes 884744 | tf_op jit(solution)/shard_map/ppermute | solution.py:414
  6.8 9.3 %collective-permute-start.2 = (bf16[384,384]{1,0:T(8,128)(2,1)S(1)}, bf16[384,384]{1,0:T(8,128)(2,1)S(1)}, u32[]{:S(2)}, u32[]{:S(2)}) collective-permute-start(bf16[384,384]{1,0:T(8,128)(2,1)S(1)} %get-tuple-element.37.own_ref), channel_id=1, source_target_pairs={{0,8},{2,10},{4,12},{6,14},{8,0},{10,2},{12,4},{14,6},{16,24},{18,... | collective-permute-start | bytes 884744 | tf_op jit(solution)/shard_map/ppermute | solution.py:420
  7.3 11.9 %collective-permute-start.4 = (bf16[384,384]{1,0:T(8,128)(2,1)S(1)}, bf16[384,384]{1,0:T(8,128)(2,1)S(1)}, u32[]{:S(2)}, u32[]{:S(2)}) collective-permute-start(bf16[384,384]{1,0:T(8,128)(2,1)S(1)} %get-tuple-element.37.own_ref), channel_id=1, source_target_pairs={{8,16},{10,18},{12,20},{14,22},{16,8},{18,10},{20,12},{22,14},{9,1... | collective-permute-start | bytes 884744 | tf_op jit(solution)/shard_map/ppermute | solution.py:420
  11.9 7.3 %collective-permute-start.5 = (bf16[384,384]{1,0:T(8,128)(2,1)S(1)}, bf16[384,384]{1,0:T(8,128)(2,1)S(1)}, u32[]{:S(2)}, u32[]{:S(2)}) collective-permute-start(bf16[384,384]{1,0:T(8,128)(2,1)S(1)} %get-tuple-element.59.refs_0_), channel_id=1, source_target_pairs={{0,2},{1,5},{2,0},{3,7},{4,6},{5,1},{6,4},{7,3},{8,10},{9,13},{10,... | collective-permute-start | bytes 884744 | tf_op jit(solution)/shard_map/ppermute | solution.py:414
  12.5 9.3 %collective-permute-start.7 = (bf16[384,384]{1,0:T(8,128)(2,1)S(1)}, bf16[384,384]{1,0:T(8,128)(2,1)S(1)}, u32[]{:S(2)}, u32[]{:S(2)}) collective-permute-start(bf16[384,384]{1,0:T(8,128)(2,1)S(1)} %collective-permute-done.3.refs_0_.refs_1_), channel_id=1, source_target_pairs={{0,2},{1,5},{2,0},{3,7},{4,6},{5,1},{6,4},{7,3},{8,10},{9,13},{10,... | collective-permute-start | bytes 884744 | tf_op jit(solution)/shard_map/ppermute | solution.py:414
  16.2 4.6 %collective-permute-start.6 = (f32[1,384]{1,0:T(1,128)S(1)}, f32[1,384]{1,0:T(1,128)S(1)}, u32[]{:S(2)}, u32[]{:S(2)}) collective-permute-start(f32[1,384]{1,0:T(1,128)S(1)} %get-tuple-element.45), channel_id=1, source_target_pairs={{0,16},{2,18},{4,20},{6,22},{8,24},{10,26},{12,28},{14,30},{16,0},... | collective-permute-start | bytes 4616 | tf_op jit(solution)/shard_map/ppermute | solution.py:420
  21.9 7.7 %collective-permute-start.11 = (bf16[400,384]{1,0:T(8,128)(2,1)S(1)}, bf16[400,384]{1,0:T(8,128)(2,1)S(1)}, u32[]{:S(2)}, u32[]{:S(2)}) collective-permute-start(bf16[400,384]{1,0:T(8,128)(2,1)S(1)} %get-tuple-element.58), channel_id=1, source_target_pairs={{0,4},{1,3},{2,6},{3,1},{4,0},{5,7},{6,2},{7,5},{8,12},{9,11},{10,... | collective-permute-start | bytes 921608 | tf_op jit(solution)/shard_map/ppermute | solution.py:414
  22.5 13.6 %collective-permute-start.10 = (bf16[416,384]{1,0:T(8,128)(2,1)S(1)}, bf16[416,384]{1,0:T(8,128)(2,1)S(1)}, u32[]{:S(2)}, u32[]{:S(2)}) collective-permute-start(bf16[416,384]{1,0:T(8,128)(2,1)S(1)} %get-tuple-element.62), channel_id=1, source_target_pairs={{0,4},{1,3},{2,6},{3,1},{4,0},{5,7},{6,2},{7,5},{8,12},{9,11},{10,... | collective-permute-start | bytes 958472 | tf_op jit(solution)/shard_map/ppermute | solution.py:414
  25.6 7.7 %collective-permute-start.8 = (bf16[400,384]{1,0:T(8,128)(2,1)S(1)}, bf16[400,384]{1,0:T(8,128)(2,1)S(1)}, u32[]{:S(2)}, u32[]{:S(2)}) collective-permute-start(bf16[400,384]{1,0:T(8,128)(2,1)S(1)} %get-tuple-element.60), channel_id=1, source_target_pairs={{0,8},{2,10},{4,12},{6,14},{8,0},{10,2},{12,4},{14,6},{16,24},{18,... | collective-permute-start | bytes 921608 | tf_op jit(solution)/shard_map/ppermute | solution.py:420
  25.6 10.5 %collective-permute-start.9 = (bf16[400,384]{1,0:T(8,128)(2,1)S(1)}, bf16[400,384]{1,0:T(8,128)(2,1)S(1)}, u32[]{:S(2)}, u32[]{:S(2)}) collective-permute-start(bf16[400,384]{1,0:T(8,128)(2,1)S(1)} %get-tuple-element.61), channel_id=1, source_target_pairs={{8,16},{10,18},{12,20},{14,22},{16,8},{18,10},{20,12},{22,14},{9,1... | collective-permute-start | bytes 921608 | tf_op jit(solution)/shard_map/ppermute | solution.py:420
  29.7 6.9 %collective-permute-start.12 = (bf16[400,384]{1,0:T(8,128)(2,1)S(1)}, bf16[400,384]{1,0:T(8,128)(2,1)S(1)}, u32[]{:S(2)}, u32[]{:S(2)}) collective-permute-start(bf16[400,384]{1,0:T(8,128)(2,1)S(1)} %shard_map.79), channel_id=1, source_target_pairs={{0,2},{1,5},{2,0},{3,7},{4,6},{5,1},{6,4},{7,3},{8,10},{9,13},{10,... | collective-permute-start | bytes 921608 | tf_op jit(solution)/shard_map/ppermute | solution.py:414

commit v6 on v5

--- a/solution.py
+++ b/solution.py
@@ -130,7 +130,12 @@
 
 
 def greens_of_second(g_ref, other_ref, below_ref, holes_ref, *rest):
-    *outs, couple = rest[3:]
+    kept, (*outs, couple) = rest[:3], rest[3:]
+
+    @pl.when(lax.axis_index("slab") == 0)
+    def _():
+        for out, value in zip(outs, kept):
+            out[...] = value[...]
 
     @pl.when(lax.axis_index("slab") != 0)
     def _():
@@ -267,7 +272,8 @@
     m = dos_ref.shape[1]
     _, _, seat = place()
     first, second = hops()
-    for out, j in zip(refs[3:], (GROUP - 1, first, second)):
+    for kept, out, j in zip(refs[:3], refs[3:], (GROUP - 1, first, second)):
+        out[...] = kept[...]
         counts = jnp.bitwise_xor(seat, j) > seat
         out[m : m + EXTRA] = split_rows(
             before_ref[...] + jnp.where(counts, dos_ref[...], 0.0)

time: 38.2 us -> 38.5 us (level); the launches traced: 37.6 us -> 38.3 us
  Pallas kernels: 8.6 us -> 9.73 us
  starting transfers between devices: 20.8 us -> 20.2 us
    pallas_call x13, Pallas kernels: 8.6 us -> 9.73 us  [call(): pl.pallas_call(kernel, out_shape=outs, in_specs=[SCALARS if i.ndim == 1 e...]
    ppermute x6, starting transfers between devices: 6.6 us -> 6.1 us  [hop(): return lax.ppermute(value, ('energy', 'slab'), pairs)]
  transfers between devices with their start and end apart: 13 -> 13, of which waited for: 6 -> 6; matrix products, arithmetic and copies ran while one was open for 0% -> 0% of each run, Pallas kernels for 20% -> 22%
where the time goes in v6:
time: 38.5 us; the launch traced here: 38.3 us
  starting transfers between devices  20.2 us (52%)
  Pallas kernels  9.73 us (25%)
  waiting for transfers between devices  7.52 us (20%)
  between operations  0.82 us (2%)
    ppermute x5, starting transfers between devices, across_groups(): lax.ppermute(value, 'energy', [(GROUP * a + i, GROUP * b + i) for a, b in...  11.6 us
    pallas_call x13, Pallas kernels, call(): pl.pallas_call(kernel, out_shape=outs, in_specs=[SCALARS if i.ndim == 1 e...  9.73 us
    ppermute x6, starting transfers between devices, hop(): return lax.ppermute(value, ('energy', 'slab'), pairs)  6.1 us
    ppermute x5, waiting for transfers between devices, across_groups(): lax.ppermute(value, 'energy', [(GROUP * a + i, GROUP * b + i) for a, b in...  5.97 us
    ppermute x1, starting transfers between devices, greens_halves(): below = lax.ppermute(coupling, 'slab', up)  2.41 us
    ppermute x6, waiting for transfers between devices, hop(): return lax.ppermute(value, ('energy', 'slab'), pairs)  1.55 us
  transfers between devices with their start and end apart: 13, of which 6 were waited for; matrix products, arithmetic and copies ran while one was open for 0% of the time, Pallas kernels for 22%

profile of v6, /device:TPU:10, one launch (start us, length us, event | category | flops | bytes accessed | tf_op | source)
XLA Modules:
  0.0 38.3 jit_solution(2252549619715836986)
XLA Ops:
  0.6 0.1 collective-permute-start
  0.7 2.4 %collective-permute-start.1 = (bf16[384,384]{1,0:T(8,128)(2,1)}, bf16[384,384]{1,0:T(8,128)(2,1)S(1)}, u32[]{:S(2)}, u32[]{:S(2)}) collective-permute-start(bf16[384,384]{1,0:T(8,128)(2,1)} %own_ref.1), channel_id=1, source_target_pairs={{0,1},{2,3},{4,5},{6,7},{8,9},{10,11},{12,13},{14,15},{16,17},{18,... | collective-permute-start | bytes 884744 | tf_op jit(solution)/shard_map/ppermute | solution.py:166
  3.2 2.0 %shard_map.69 = (bf16[384,384]{1,0:T(8,128)(2,1)S(1)}, bf16[384,384]{1,0:T(8,128)(2,1)S(1)}, f32[1,384]{1,0:T(1,128)S(1)}) custom-call(bf16[384,768]{1,0:T(8,128)(2,1)S(1)} %bitcast.3, bf16[384,768]{1,0:T(8,128)(2,1)S(1)} %collective-permute-done.other_ref, bf16[384,384]{1,0:T(8,128)(2,1)S(1)} %copy-done.2, f32[1,384]{1,0:T(1,128)S(1)} %shard_map.68.holes_ref), custom_call_target="tpu_custom_call" | custom-call | tf_op jit(solution)/shard_map/pallas_call | solution.py:44
  5.2 0.0 copy-start
  5.2 0.1 shard_map.70
  5.3 0.0 copy-start.3
  5.3 0.0 copy-start.4
  5.3 1.6 %collective-permute-start.3 = (bf16[384,384]{1,0:T(8,128)(2,1)S(1)}, bf16[384,384]{1,0:T(8,128)(2,1)S(1)}, u32[]{:S(2)}, u32[]{:S(2)}) collective-permute-start(bf16[384,384]{1,0:T(8,128)(2,1)S(1)} %get-tuple-element.59.refs_0_), channel_id=1, source_target_pairs={{0,4},{1,3},{2,6},{3,1},{4,0},{5,7},{6,2},{7,5},{8,12},{9,11},{10,... | collective-permute-start | bytes 884744 | tf_op jit(solution)/shard_map/ppermute | solution.py:420
  6.9 0.4 %collective-permute-start.2 = (bf16[384,384]{1,0:T(8,128)(2,1)S(1)}, bf16[384,384]{1,0:T(8,128)(2,1)S(1)}, u32[]{:S(2)}, u32[]{:S(2)}) collective-permute-start(bf16[384,384]{1,0:T(8,128)(2,1)S(1)} %get-tuple-element.37.own_ref), channel_id=1, source_target_pairs={{0,8},{2,10},{4,12},{6,14},{8,0},{10,2},{12,4},{14,6},{16,24},{18,... | collective-permute-start | bytes 884744 | tf_op jit(solution)/shard_map/ppermute | solution.py:426
  7.4 4.6 %collective-permute-start.4 = (bf16[384,384]{1,0:T(8,128)(2,1)S(1)}, bf16[384,384]{1,0:T(8,128)(2,1)S(1)}, u32[]{:S(2)}, u32[]{:S(2)}) collective-permute-start(bf16[384,384]{1,0:T(8,128)(2,1)S(1)} %get-tuple-element.37.own_ref), channel_id=1, source_target_pairs={{8,16},{10,18},{12,20},{14,22},{16,8},{18,10},{20,12},{22,14},{9,1... | collective-permute-start | bytes 884744 | tf_op jit(solution)/shard_map/ppermute | solution.py:426
  12.0 0.6 %collective-permute-start.5 = (bf16[384,384]{1,0:T(8,128)(2,1)S(1)}, bf16[384,384]{1,0:T(8,128)(2,1)S(1)}, u32[]{:S(2)}, u32[]{:S(2)}) collective-permute-start(bf16[384,384]{1,0:T(8,128)(2,1)S(1)} %get-tuple-element.59.refs_0_), channel_id=1, source_target_pairs={{0,2},{1,5},{2,0},{3,7},{4,6},{5,1},{6,4},{7,3},{8,10},{9,13},{10,... | collective-permute-start | bytes 884744 | tf_op jit(solution)/shard_map/ppermute | solution.py:420
  12.6 1.5 %collective-permute-start.7 = (bf16[384,384]{1,0:T(8,128)(2,1)S(1)}, bf16[384,384]{1,0:T(8,128)(2,1)S(1)}, u32[]{:S(2)}, u32[]{:S(2)}) collective-permute-start(bf16[384,384]{1,0:T(8,128)(2,1)S(1)} %collective-permute-done.3.refs_0_.refs_1_), channel_id=1, source_target_pairs={{0,2},{1,5},{2,0},{3,7},{4,6},{5,1},{6,4},{7,3},{8,10},{9,13},{10,... | collective-permute-start | bytes 884744 | tf_op jit(solution)/shard_map/ppermute | solution.py:420
  14.1 0.6 %shard_map.71 = (s32[8,128]{1,0:T(8,128)S(1)}, f32[8,128]{1,0:T(8,128)S(1)}) custom-call(s32[3]{0:T(128)S(1)} %copy-done.3, f32[3]{0:T(128)S(1)} %copy-done.4), custom_call_target="tpu_custom_call" | custom-call | tf_op jit(solution)/shard_map/pallas_call | solution.py:44
  14.6 1.5 %collective-permute-done.2.first_ref = bf16[384,384]{1,0:T(8,128)(2,1)S(1)} collective-permute-done((bf16[384,384]{1,0:T(8,128)(2,1)S(1)}, bf16[384,384]{1,0:T(8,128)(2,1)S(1)}, u32[]{:S(2)}, u32[]{:S(2)}) %collective-permute-start.2) | collective-permute-done | bytes 294944 | tf_op jit(solution)/shard_map/ppermute | solution.py:426
  16.2 2.7 %collective-permute-start.6 = (f32[1,384]{1,0:T(1,128)S(1)}, f32[1,384]{1,0:T(1,128)S(1)}, u32[]{:S(2)}, u32[]{:S(2)}) collective-permute-start(f32[1,384]{1,0:T(1,128)S(1)} %get-tuple-element.45), channel_id=1, source_target_pairs={{0,16},{2,18},{4,20},{6,22},{8,24},{10,26},{12,28},{14,30},{16,0},... | collective-permute-start | bytes 4616 | tf_op jit(solution)/shard_map/ppermute | solution.py:426
  18.8 0.3 collective-permute-done.4.second_ref
  19.2 1.8 %shard_map.73 = (bf16[400,384]{1,0:T(8,128)(2,1)S(1)}, bf16[416,384]{1,0:T(8,128)(2,1)S(1)}, bf16[400,384]{1,0:T(8,128)(2,1)S(1)}) custom-call(bf16[384,384]{1,0:T(8,128)(2,1)S(1)} %get-tuple-element.37.own_ref, bf16[384,384]{1,0:T(8,128)(2,1)S(1)} %collective-permute-done.2.first_ref, bf16[384,384]{1,0:T(8,128)(2,1)S(1)} %collective-permute-done.4.second_ref, ...), custom_call_target="tpu_custom_call" | custom-call | tf_op jit(solution)/shard_map/pallas_call | solution.py:44
  21.0 0.9 %collective-permute-done.7.refs_2_.refs_3_ = bf16[384,384]{1,0:T(8,128)(2,1)S(1)} collective-permute-done((bf16[384,384]{1,0:T(8,128)(2,1)S(1)}, bf16[384,384]{1,0:T(8,128)(2,1)S(1)}, u32[]{:S(2)}, u32[]{:S(2)}) %collective-permute-start.7) | collective-permute-done | bytes 294944 | tf_op jit(solution)/shard_map/ppermute | solution.py:420
  21.9 0.2 shard_map.77
  22.1 0.6 %collective-permute-start.11 = (bf16[400,384]{1,0:T(8,128)(2,1)S(1)}, bf16[400,384]{1,0:T(8,128)(2,1)S(1)}, u32[]{:S(2)}, u32[]{:S(2)}) collective-permute-start(bf16[400,384]{1,0:T(8,128)(2,1)S(1)} %get-tuple-element.58), channel_id=1, source_target_pairs={{0,4},{1,3},{2,6},{3,1},{4,0},{5,7},{6,2},{7,5},{8,12},{9,11},{10,... | collective-permute-start | bytes 921608 | tf_op jit(solution)/shard_map/ppermute | solution.py:420
  22.7 1.5 %collective-permute-start.10 = (bf16[416,384]{1,0:T(8,128)(2,1)S(1)}, bf16[416,384]{1,0:T(8,128)(2,1)S(1)}, u32[]{:S(2)}, u32[]{:S(2)}) collective-permute-start(bf16[416,384]{1,0:T(8,128)(2,1)S(1)} %get-tuple-element.62), channel_id=1, source_target_pairs={{0,4},{1,3},{2,6},{3,1},{4,0},{5,7},{6,2},{7,5},{8,12},{9,11},{10,... | collective-permute-start | bytes 958472 | tf_op jit(solution)/shard_map/ppermute | solution.py:420
  24.2 2.2 %shard_map.78 = (bf16[400,384]{1,0:T(8,128)(2,1)S(1)}, bf16[400,384]{1,0:T(8,128)(2,1)S(1)}) custom-call(bf16[384,384]{1,0:T(8,128)(2,1)S(1)} %get-tuple-element.59.refs_0_, bf16[384,384]{1,0:T(8,128)(2,1)S(1)} %collective-permute-done.3.refs_0_.refs_1_, bf16[384,384]{1,0:T(8,128)(2,1)S(1)} %collective-permute-done.5.refs_1_.refs_2_, ...), custom_call_target="tpu_custom_call" | custom-call | tf_op jit(solution)/shard_map/pallas_call | solution.py:44
  26.4 0.1 collective-permute-start.8
  26.5 3.9 %collective-permute-start.9 = (bf16[400,384]{1,0:T(8,128)(2,1)S(1)}, bf16[400,384]{1,0:T(8,128)(2,1)S(1)}, u32[]{:S(2)}, u32[]{:S(2)}) collective-permute-start(bf16[400,384]{1,0:T(8,128)(2,1)S(1)} %get-tuple-element.61), channel_id=1, source_target_pairs={{8,16},{10,18},{12,20},{14,22},{16,8},{18,10},{20,12},{22,14},{9,1... | collective-permute-start | bytes 921608 | tf_op jit(solution)/shard_map/ppermute | solution.py:426
  30.4 0.1 shard_map.79
  30.5 0.3 collective-permute-start.12
  30.8 0.7 %shard_map.75.refs_1_ = f32[384,384]{1,0:T(8,128)S(1)} custom-call(bf16[384,384]{1,0:T(8,128)(2,1)S(1)} %collective-permute-done.2.first_ref, bf16[384,384]{1,0:T(8,128)(2,1)S(1)} %collective-permute-done.4.second_ref, bf16[3,384,384]{2,1,0:T(8,128)(2,1)S(1)} %copy-done, s32[8,128]{1,0:T(8,128)S(1)} %get-tuple-element.47.places_ref.refs_4_.refs_5_, ...), custom_call_target="tpu_custom_call" | custom-call | tf_op jit(solution)/shard_map/pallas_call | solution.py:44
  31.5 1.1 %shard_map.74.refs_0_ = f32[384,384]{1,0:T(8,128)S(1)} custom-call(bf16[384,384]{1,0:T(8,128)(2,1)S(1)} %collective-permute-done.3.refs_0_.refs_1_, bf16[384,384]{1,0:T(8,128)(2,1)S(1)} %collective-permute-done.5.refs_1_.refs_2_, bf16[384,384]{1,0:T(8,128)(2,1)S(1)} %collective-permute-done.7.refs_2_.refs_3_, bf16[3,384,384]{2,1,0:T(8,128)(2,1)S(1)} %copy-done, ...), custom_call_target="tpu_custom_call" | custom-call | tf_op jit(solution)/shard_map/pallas_call | solution.py:44
  32.6 1.6 %collective-permute-done.8.refs_2_ = bf16[400,384]{1,0:T(8,128)(2,1)S(1)} collective-permute-done((bf16[400,384]{1,0:T(8,128)(2,1)S(1)}, bf16[400,384]{1,0:T(8,128)(2,1)S(1)}, u32[]{:S(2)}, u32[]{:S(2)}) %collective-permute-start.8) | collective-permute-done | bytes 307232 | tf_op jit(solution)/shard_map/ppermute | solution.py:426
  34.2 2.5 %collective-permute-done.9.refs_3_ = bf16[400,384]{1,0:T(8,128)(2,1)S(1)} collective-permute-done((bf16[400,384]{1,0:T(8,128)(2,1)S(1)}, bf16[400,384]{1,0:T(8,128)(2,1)S(1)}, u32[]{:S(2)}, u32[]{:S(2)}) %collective-permute-start.9) | collective-permute-done | bytes 307232 | tf_op jit(solution)/shard_map/ppermute | solution.py:426
  36.8 0.6 %collective-permute-done.12.refs_7_ = bf16[400,384]{1,0:T(8,128)(2,1)S(1)} collective-permute-done((bf16[400,384]{1,0:T(8,128)(2,1)S(1)}, bf16[400,384]{1,0:T(8,128)(2,1)S(1)}, u32[]{:S(2)}, u32[]{:S(2)}) %collective-permute-start.12) | collective-permute-done | bytes 307232 | tf_op jit(solution)/shard_map/ppermute | solution.py:420
  37.4 0.9 %shard_map.80 = (bf16[384,768]{1,0:T(8,128)(2,1)}, f32[1,384]{1,0:T(1,128)}) custom-call(f32[384,384]{1,0:T(8,128)S(1)} %shard_map.74.refs_0_, f32[384,384]{1,0:T(8,128)S(1)} %shard_map.75.refs_1_, bf16[400,384]{1,0:T(8,128)(2,1)S(1)} %collective-permute-done.8.refs_2_, bf16[400,384]{1,0:T(8,128)(2,1)S(1)} %collective-permute-done.9.refs_3_, ...), custom_call_target="tpu_custom_call" | custom-call | tf_op jit(solution)/shard_map/pallas_call | solution.py:44
  (17 shorter events, 0.1 us)
Async XLA Ops:
  0.6 2.6 %copy-start.1 = (bf16[1,384,768]{2,1,0:T(8,128)(2,1)S(1)}, bf16[1,384,768]{2,1,0:T(8,128)(2,1)}, u32[]{:S(2)}) copy-start(bf16[1,384,768]{2,1,0:T(8,128)(2,1)} %param.5) | copy-start | bytes 1769476
  0.6 2.6 %copy-start.2 = (bf16[384,384]{1,0:T(8,128)(2,1)S(1)}, bf16[384,384]{1,0:T(8,128)(2,1)}, u32[]{:S(2)}) copy-start(bf16[384,384]{1,0:T(8,128)(2,1)} %own_ref.1) | copy-start | bytes 884740
  0.6 2.5 %collective-permute-start = (bf16[384,768]{1,0:T(8,128)(2,1)}, bf16[384,768]{1,0:T(8,128)(2,1)S(1)}, u32[]{:S(2)}, u32[]{:S(2)}) collective-permute-start(bf16[384,768]{1,0:T(8,128)(2,1)} %bitcast.2), channel_id=1, source_target_pairs={{0,1},{1,0},{2,3},{3,2},{4,5},{5,4},{6,7},{7,6},{8,9},{9,8},{10,11... | collective-permute-start | bytes 1769480 | tf_op jit(solution)/shard_map/ppermute | solution.py:170
  0.7 4.4 %collective-permute-start.1 = (bf16[384,384]{1,0:T(8,128)(2,1)}, bf16[384,384]{1,0:T(8,128)(2,1)S(1)}, u32[]{:S(2)}, u32[]{:S(2)}) collective-permute-start(bf16[384,384]{1,0:T(8,128)(2,1)} %own_ref.1), channel_id=1, source_target_pairs={{0,1},{2,3},{4,5},{6,7},{8,9},{10,11},{12,13},{14,15},{16,17},{18,... | collective-permute-start | bytes 884744 | tf_op jit(solution)/shard_map/ppermute | solution.py:166
  5.2 14.0 %copy-start = (bf16[3,384,384]{2,1,0:T(8,128)(2,1)S(1)}, bf16[3,384,384]{2,1,0:T(8,128)(2,1)}, u32[]{:S(2)}) copy-start(bf16[3,384,384]{2,1,0:T(8,128)(2,1)} %refs_4_.1) | copy-start | bytes 2654212
  5.3 8.8 %copy-start.3 = (s32[3]{0:T(128)S(1)}, s32[3]{0:T(128)}, u32[]{:S(2)}) copy-start(s32[3]{0:T(128)} %offsets_ref.1) | copy-start | bytes 40
  5.3 8.8 %copy-start.4 = (f32[3]{0:T(128)S(1)}, f32[3]{0:T(128)}, u32[]{:S(2)}) copy-start(f32[3]{0:T(128)} %bose_ref.1) | copy-start | bytes 40
  5.3 7.2 %collective-permute-start.3 = (bf16[384,384]{1,0:T(8,128)(2,1)S(1)}, bf16[384,384]{1,0:T(8,128)(2,1)S(1)}, u32[]{:S(2)}, u32[]{:S(2)}) collective-permute-start(bf16[384,384]{1,0:T(8,128)(2,1)S(1)} %get-tuple-element.59.refs_0_), channel_id=1, source_target_pairs={{0,4},{1,3},{2,6},{3,1},{4,0},{5,7},{6,2},{7,5},{8,12},{9,11},{10,... | collective-permute-start | bytes 884744 | tf_op jit(solution)/shard_map/ppermute | solution.py:420
  6.9 9.2 %collective-permute-start.2 = (bf16[384,384]{1,0:T(8,128)(2,1)S(1)}, bf16[384,384]{1,0:T(8,128)(2,1)S(1)}, u32[]{:S(2)}, u32[]{:S(2)}) collective-permute-start(bf16[384,384]{1,0:T(8,128)(2,1)S(1)} %get-tuple-element.37.own_ref), channel_id=1, source_target_pairs={{0,8},{2,10},{4,12},{6,14},{8,0},{10,2},{12,4},{14,6},{16,24},{18,... | collective-permute-start | bytes 884744 | tf_op jit(solution)/shard_map/ppermute | solution.py:426
  7.4 11.8 %collective-permute-start.4 = (bf16[384,384]{1,0:T(8,128)(2,1)S(1)}, bf16[384,384]{1,0:T(8,128)(2,1)S(1)}, u32[]{:S(2)}, u32[]{:S(2)}) collective-permute-start(bf16[384,384]{1,0:T(8,128)(2,1)S(1)} %get-tuple-element.37.own_ref), channel_id=1, source_target_pairs={{8,16},{10,18},{12,20},{14,22},{16,8},{18,10},{20,12},{22,14},{9,1... | collective-permute-start | bytes 884744 | tf_op jit(solution)/shard_map/ppermute | solution.py:426
  12.0 7.2 %collective-permute-start.5 = (bf16[384,384]{1,0:T(8,128)(2,1)S(1)}, bf16[384,384]{1,0:T(8,128)(2,1)S(1)}, u32[]{:S(2)}, u32[]{:S(2)}) collective-permute-start(bf16[384,384]{1,0:T(8,128)(2,1)S(1)} %get-tuple-element.59.refs_0_), channel_id=1, source_target_pairs={{0,2},{1,5},{2,0},{3,7},{4,6},{5,1},{6,4},{7,3},{8,10},{9,13},{10,... | collective-permute-start | bytes 884744 | tf_op jit(solution)/shard_map/ppermute | solution.py:420
  12.6 9.3 %collective-permute-start.7 = (bf16[384,384]{1,0:T(8,128)(2,1)S(1)}, bf16[384,384]{1,0:T(8,128)(2,1)S(1)}, u32[]{:S(2)}, u32[]{:S(2)}) collective-permute-start(bf16[384,384]{1,0:T(8,128)(2,1)S(1)} %collective-permute-done.3.refs_0_.refs_1_), channel_id=1, source_target_pairs={{0,2},{1,5},{2,0},{3,7},{4,6},{5,1},{6,4},{7,3},{8,10},{9,13},{10,... | collective-permute-start | bytes 884744 | tf_op jit(solution)/shard_map/ppermute | solution.py:420
  16.2 4.8 %collective-permute-start.6 = (f32[1,384]{1,0:T(1,128)S(1)}, f32[1,384]{1,0:T(1,128)S(1)}, u32[]{:S(2)}, u32[]{:S(2)}) collective-permute-start(f32[1,384]{1,0:T(1,128)S(1)} %get-tuple-element.45), channel_id=1, source_target_pairs={{0,16},{2,18},{4,20},{6,22},{8,24},{10,26},{12,28},{14,30},{16,0},... | collective-permute-start | bytes 4616 | tf_op jit(solution)/shard_map/ppermute | solution.py:426
  22.1 8.3 %collective-permute-start.11 = (bf16[400,384]{1,0:T(8,128)(2,1)S(1)}, bf16[400,384]{1,0:T(8,128)(2,1)S(1)}, u32[]{:S(2)}, u32[]{:S(2)}) collective-permute-start(bf16[400,384]{1,0:T(8,128)(2,1)S(1)} %get-tuple-element.58), channel_id=1, source_target_pairs={{0,4},{1,3},{2,6},{3,1},{4,0},{5,7},{6,2},{7,5},{8,12},{9,11},{10,... | collective-permute-start | bytes 921608 | tf_op jit(solution)/shard_map/ppermute | solution.py:420
  22.7 14.1 %collective-permute-start.10 = (bf16[416,384]{1,0:T(8,128)(2,1)S(1)}, bf16[416,384]{1,0:T(8,128)(2,1)S(1)}, u32[]{:S(2)}, u32[]{:S(2)}) collective-permute-start(bf16[416,384]{1,0:T(8,128)(2,1)S(1)} %get-tuple-element.62), channel_id=1, source_target_pairs={{0,4},{1,3},{2,6},{3,1},{4,0},{5,7},{6,2},{7,5},{8,12},{9,11},{10,... | collective-permute-start | bytes 958472 | tf_op jit(solution)/shard_map/ppermute | solution.py:420
  26.4 7.8 %collective-permute-start.8 = (bf16[400,384]{1,0:T(8,128)(2,1)S(1)}, bf16[400,384]{1,0:T(8,128)(2,1)S(1)}, u32[]{:S(2)}, u32[]{:S(2)}) collective-permute-start(bf16[400,384]{1,0:T(8,128)(2,1)S(1)} %get-tuple-element.60), channel_id=1, source_target_pairs={{0,8},{2,10},{4,12},{6,14},{8,0},{10,2},{12,4},{14,6},{16,24},{18,... | collective-permute-start | bytes 921608 | tf_op jit(solution)/shard_map/ppermute | solution.py:426
  26.5 10.3 %collective-permute-start.9 = (bf16[400,384]{1,0:T(8,128)(2,1)S(1)}, bf16[400,384]{1,0:T(8,128)(2,1)S(1)}, u32[]{:S(2)}, u32[]{:S(2)}) collective-permute-start(bf16[400,384]{1,0:T(8,128)(2,1)S(1)} %get-tuple-element.61), channel_id=1, source_target_pairs={{8,16},{10,18},{12,20},{14,22},{16,8},{18,10},{20,12},{22,14},{9,1... | collective-permute-start | bytes 921608 | tf_op jit(solution)/shard_map/ppermute | solution.py:426
  30.5 6.9 %collective-permute-start.12 = (bf16[400,384]{1,0:T(8,128)(2,1)S(1)}, bf16[400,384]{1,0:T(8,128)(2,1)S(1)}, u32[]{:S(2)}, u32[]{:S(2)}) collective-permute-start(bf16[400,384]{1,0:T(8,128)(2,1)S(1)} %shard_map.79), channel_id=1, source_target_pairs={{0,2},{1,5},{2,0},{3,7},{4,6},{5,1},{6,4},{7,3},{8,10},{9,13},{10,... | collective-permute-start | bytes 921608 | tf_op jit(solution)/shard_map/ppermute | solution.py:420

commit v7 on v6

--- a/solution.py
+++ b/solution.py
@@ -264,8 +264,6 @@
     first, second = hops()
     direct[:m] = sums[first - 1]
     merged[:m] = sums[second - 1]
-    for out in (across, direct, merged):
-        out[m:] = jnp.zeros((out.shape[0] - m, m), jnp.bfloat16)
 
 
 def with_lines(dos_ref, before_ref, *refs):
@@ -273,11 +271,13 @@
     _, _, seat = place()
     first, second = hops()
     for kept, out, j in zip(refs[:3], refs[3:], (GROUP - 1, first, second)):
-        out[...] = kept[...]
+        out[:m] = kept[:m]
         counts = jnp.bitwise_xor(seat, j) > seat
         out[m : m + EXTRA] = split_rows(
             before_ref[...] + jnp.where(counts, dos_ref[...], 0.0)
         )
+        if out.shape[0] > m + EXTRA:
+            out[m + EXTRA :] = jnp.zeros((out.shape[0] - m - EXTRA, m), jnp.bfloat16)
 
 
 def merge(received_ref, merged_ref, out):

time: 38.5 us -> 38.5 us (level)
  no operation moved by 1% of the time
where the time goes in v7:
time: 38.5 us; the launch traced here: 38.3 us
  starting transfers between devices  20.2 us (52%)
  Pallas kernels  9.73 us (25%)
  waiting for transfers between devices  7.54 us (20%)
  between operations  0.82 us (2%)
    ppermute x5, starting transfers between devices, across_groups(): lax.ppermute(value, 'energy', [(GROUP * a + i, GROUP * b + i) for a, b in...  11.6 us
    pallas_call x13, Pallas kernels, call(): pl.pallas_call(kernel, out_shape=outs, in_specs=[SCALARS if i.ndim == 1 e...  9.73 us
    ppermute x6, starting transfers between devices, hop(): return lax.ppermute(value, ('energy', 'slab'), pairs)  6.08 us
    ppermute x5, waiting for transfers between devices, across_groups(): lax.ppermute(value, 'energy', [(GROUP * a + i, GROUP * b + i) for a, b in...  5.98 us
    ppermute x1, starting transfers between devices, greens_halves(): below = lax.ppermute(coupling, 'slab', up)  2.41 us
    ppermute x6, waiting for transfers between devices, hop(): return lax.ppermute(value, ('energy', 'slab'), pairs)  1.56 us
  transfers between devices with their start and end apart: 13, of which 6 were waited for; matrix products, arithmetic and copies ran while one was open for 0% of the time, Pallas kernels for 22%

profile of v7, /device:TPU:10, one launch (start us, length us, event | category | flops | bytes accessed | tf_op | source)
XLA Modules:
  0.0 38.3 jit_solution(8652408719190665128)
XLA Ops:
  0.6 0.1 collective-permute-start
  0.7 2.4 %collective-permute-start.1 = (bf16[384,384]{1,0:T(8,128)(2,1)}, bf16[384,384]{1,0:T(8,128)(2,1)S(1)}, u32[]{:S(2)}, u32[]{:S(2)}) collective-permute-start(bf16[384,384]{1,0:T(8,128)(2,1)} %own_ref.1), channel_id=1, source_target_pairs={{0,1},{2,3},{4,5},{6,7},{8,9},{10,11},{12,13},{14,15},{16,17},{18,... | collective-permute-start | bytes 884744 | tf_op jit(solution)/shard_map/ppermute | solution.py:166
  3.2 2.0 %shard_map.69 = (bf16[384,384]{1,0:T(8,128)(2,1)S(1)}, bf16[384,384]{1,0:T(8,128)(2,1)S(1)}, f32[1,384]{1,0:T(1,128)S(1)}) custom-call(bf16[384,768]{1,0:T(8,128)(2,1)S(1)} %bitcast.3, bf16[384,768]{1,0:T(8,128)(2,1)S(1)} %collective-permute-done.other_ref, bf16[384,384]{1,0:T(8,128)(2,1)S(1)} %copy-done.2, f32[1,384]{1,0:T(1,128)S(1)} %shard_map.68.holes_ref), custom_call_target="tpu_custom_call" | custom-call | tf_op jit(solution)/shard_map/pallas_call | solution.py:44
  5.2 0.0 copy-start
  5.2 0.1 shard_map.70
  5.3 0.0 copy-start.3
  5.3 0.0 copy-start.4
  5.3 1.6 %collective-permute-start.3 = (bf16[384,384]{1,0:T(8,128)(2,1)S(1)}, bf16[384,384]{1,0:T(8,128)(2,1)S(1)}, u32[]{:S(2)}, u32[]{:S(2)}) collective-permute-start(bf16[384,384]{1,0:T(8,128)(2,1)S(1)} %get-tuple-element.59.refs_0_), channel_id=1, source_target_pairs={{0,4},{1,3},{2,6},{3,1},{4,0},{5,7},{6,2},{7,5},{8,12},{9,11},{10,... | collective-permute-start | bytes 884744 | tf_op jit(solution)/shard_map/ppermute | solution.py:420
  6.9 0.4 %collective-permute-start.2 = (bf16[384,384]{1,0:T(8,128)(2,1)S(1)}, bf16[384,384]{1,0:T(8,128)(2,1)S(1)}, u32[]{:S(2)}, u32[]{:S(2)}) collective-permute-start(bf16[384,384]{1,0:T(8,128)(2,1)S(1)} %get-tuple-element.37.own_ref), channel_id=1, source_target_pairs={{0,8},{2,10},{4,12},{6,14},{8,0},{10,2},{12,4},{14,6},{16,24},{18,... | collective-permute-start | bytes 884744 | tf_op jit(solution)/shard_map/ppermute | solution.py:426
  7.4 4.6 %collective-permute-start.4 = (bf16[384,384]{1,0:T(8,128)(2,1)S(1)}, bf16[384,384]{1,0:T(8,128)(2,1)S(1)}, u32[]{:S(2)}, u32[]{:S(2)}) collective-permute-start(bf16[384,384]{1,0:T(8,128)(2,1)S(1)} %get-tuple-element.37.own_ref), channel_id=1, source_target_pairs={{8,16},{10,18},{12,20},{14,22},{16,8},{18,10},{20,12},{22,14},{9,1... | collective-permute-start | bytes 884744 | tf_op jit(solution)/shard_map/ppermute | solution.py:426
  12.0 0.6 %collective-permute-start.5 = (bf16[384,384]{1,0:T(8,128)(2,1)S(1)}, bf16[384,384]{1,0:T(8,128)(2,1)S(1)}, u32[]{:S(2)}, u32[]{:S(2)}) collective-permute-start(bf16[384,384]{1,0:T(8,128)(2,1)S(1)} %get-tuple-element.59.refs_0_), channel_id=1, source_target_pairs={{0,2},{1,5},{2,0},{3,7},{4,6},{5,1},{6,4},{7,3},{8,10},{9,13},{10,... | collective-permute-start | bytes 884744 | tf_op jit(solution)/shard_map/ppermute | solution.py:420
  12.6 1.5 %collective-permute-start.7 = (bf16[384,384]{1,0:T(8,128)(2,1)S(1)}, bf16[384,384]{1,0:T(8,128)(2,1)S(1)}, u32[]{:S(2)}, u32[]{:S(2)}) collective-permute-start(bf16[384,384]{1,0:T(8,128)(2,1)S(1)} %collective-permute-done.3.refs_0_.refs_1_), channel_id=1, source_target_pairs={{0,2},{1,5},{2,0},{3,7},{4,6},{5,1},{6,4},{7,3},{8,10},{9,13},{10,... | collective-permute-start | bytes 884744 | tf_op jit(solution)/shard_map/ppermute | solution.py:420
  14.1 0.6 %shard_map.71 = (s32[8,128]{1,0:T(8,128)S(1)}, f32[8,128]{1,0:T(8,128)S(1)}) custom-call(s32[3]{0:T(128)S(1)} %copy-done.3, f32[3]{0:T(128)S(1)} %copy-done.4), custom_call_target="tpu_custom_call" | custom-call | tf_op jit(solution)/shard_map/pallas_call | solution.py:44
  14.6 1.5 %collective-permute-done.2.first_ref = bf16[384,384]{1,0:T(8,128)(2,1)S(1)} collective-permute-done((bf16[384,384]{1,0:T(8,128)(2,1)S(1)}, bf16[384,384]{1,0:T(8,128)(2,1)S(1)}, u32[]{:S(2)}, u32[]{:S(2)}) %collective-permute-start.2) | collective-permute-done | bytes 294944 | tf_op jit(solution)/shard_map/ppermute | solution.py:426
  16.2 2.7 %collective-permute-start.6 = (f32[1,384]{1,0:T(1,128)S(1)}, f32[1,384]{1,0:T(1,128)S(1)}, u32[]{:S(2)}, u32[]{:S(2)}) collective-permute-start(f32[1,384]{1,0:T(1,128)S(1)} %get-tuple-element.45), channel_id=1, source_target_pairs={{0,16},{2,18},{4,20},{6,22},{8,24},{10,26},{12,28},{14,30},{16,0},... | collective-permute-start | bytes 4616 | tf_op jit(solution)/shard_map/ppermute | solution.py:426
  18.8 0.3 collective-permute-done.4.second_ref
  19.2 1.8 %shard_map.73 = (bf16[400,384]{1,0:T(8,128)(2,1)S(1)}, bf16[416,384]{1,0:T(8,128)(2,1)S(1)}, bf16[400,384]{1,0:T(8,128)(2,1)S(1)}) custom-call(bf16[384,384]{1,0:T(8,128)(2,1)S(1)} %get-tuple-element.37.own_ref, bf16[384,384]{1,0:T(8,128)(2,1)S(1)} %collective-permute-done.2.first_ref, bf16[384,384]{1,0:T(8,128)(2,1)S(1)} %collective-permute-done.4.second_ref, ...), custom_call_target="tpu_custom_call" | custom-call | tf_op jit(solution)/shard_map/pallas_call | solution.py:44
  21.0 0.9 %collective-permute-done.7.refs_2_.refs_3_ = bf16[384,384]{1,0:T(8,128)(2,1)S(1)} collective-permute-done((bf16[384,384]{1,0:T(8,128)(2,1)S(1)}, bf16[384,384]{1,0:T(8,128)(2,1)S(1)}, u32[]{:S(2)}, u32[]{:S(2)}) %collective-permute-start.7) | collective-permute-done | bytes 294944 | tf_op jit(solution)/shard_map/ppermute | solution.py:420
  21.9 0.2 shard_map.77
  22.1 0.6 %collective-permute-start.11 = (bf16[400,384]{1,0:T(8,128)(2,1)S(1)}, bf16[400,384]{1,0:T(8,128)(2,1)S(1)}, u32[]{:S(2)}, u32[]{:S(2)}) collective-permute-start(bf16[400,384]{1,0:T(8,128)(2,1)S(1)} %get-tuple-element.58), channel_id=1, source_target_pairs={{0,4},{1,3},{2,6},{3,1},{4,0},{5,7},{6,2},{7,5},{8,12},{9,11},{10,... | collective-permute-start | bytes 921608 | tf_op jit(solution)/shard_map/ppermute | solution.py:420
  22.7 1.5 %collective-permute-start.10 = (bf16[416,384]{1,0:T(8,128)(2,1)S(1)}, bf16[416,384]{1,0:T(8,128)(2,1)S(1)}, u32[]{:S(2)}, u32[]{:S(2)}) collective-permute-start(bf16[416,384]{1,0:T(8,128)(2,1)S(1)} %get-tuple-element.62), channel_id=1, source_target_pairs={{0,4},{1,3},{2,6},{3,1},{4,0},{5,7},{6,2},{7,5},{8,12},{9,11},{10,... | collective-permute-start | bytes 958472 | tf_op jit(solution)/shard_map/ppermute | solution.py:420
  24.2 2.2 %shard_map.78 = (bf16[400,384]{1,0:T(8,128)(2,1)S(1)}, bf16[400,384]{1,0:T(8,128)(2,1)S(1)}) custom-call(bf16[384,384]{1,0:T(8,128)(2,1)S(1)} %get-tuple-element.59.refs_0_, bf16[384,384]{1,0:T(8,128)(2,1)S(1)} %collective-permute-done.3.refs_0_.refs_1_, bf16[384,384]{1,0:T(8,128)(2,1)S(1)} %collective-permute-done.5.refs_1_.refs_2_, ...), custom_call_target="tpu_custom_call" | custom-call | tf_op jit(solution)/shard_map/pallas_call | solution.py:44
  26.4 0.1 collective-permute-start.8
  26.5 3.9 %collective-permute-start.9 = (bf16[400,384]{1,0:T(8,128)(2,1)S(1)}, bf16[400,384]{1,0:T(8,128)(2,1)S(1)}, u32[]{:S(2)}, u32[]{:S(2)}) collective-permute-start(bf16[400,384]{1,0:T(8,128)(2,1)S(1)} %get-tuple-element.61), channel_id=1, source_target_pairs={{8,16},{10,18},{12,20},{14,22},{16,8},{18,10},{20,12},{22,14},{9,1... | collective-permute-start | bytes 921608 | tf_op jit(solution)/shard_map/ppermute | solution.py:426
  30.4 0.1 shard_map.79
  30.5 0.3 collective-permute-start.12
  30.8 0.7 %shard_map.75.refs_1_ = f32[384,384]{1,0:T(8,128)S(1)} custom-call(bf16[384,384]{1,0:T(8,128)(2,1)S(1)} %collective-permute-done.2.first_ref, bf16[384,384]{1,0:T(8,128)(2,1)S(1)} %collective-permute-done.4.second_ref, bf16[3,384,384]{2,1,0:T(8,128)(2,1)S(1)} %copy-done, s32[8,128]{1,0:T(8,128)S(1)} %get-tuple-element.47.places_ref.refs_4_.refs_5_, ...), custom_call_target="tpu_custom_call" | custom-call | tf_op jit(solution)/shard_map/pallas_call | solution.py:44
  31.5 1.1 %shard_map.74.refs_0_ = f32[384,384]{1,0:T(8,128)S(1)} custom-call(bf16[384,384]{1,0:T(8,128)(2,1)S(1)} %collective-permute-done.3.refs_0_.refs_1_, bf16[384,384]{1,0:T(8,128)(2,1)S(1)} %collective-permute-done.5.refs_1_.refs_2_, bf16[384,384]{1,0:T(8,128)(2,1)S(1)} %collective-permute-done.7.refs_2_.refs_3_, bf16[3,384,384]{2,1,0:T(8,128)(2,1)S(1)} %copy-done, ...), custom_call_target="tpu_custom_call" | custom-call | tf_op jit(solution)/shard_map/pallas_call | solution.py:44
  32.6 1.6 %collective-permute-done.8.refs_2_ = bf16[400,384]{1,0:T(8,128)(2,1)S(1)} collective-permute-done((bf16[400,384]{1,0:T(8,128)(2,1)S(1)}, bf16[400,384]{1,0:T(8,128)(2,1)S(1)}, u32[]{:S(2)}, u32[]{:S(2)}) %collective-permute-start.8) | collective-permute-done | bytes 307232 | tf_op jit(solution)/shard_map/ppermute | solution.py:426
  34.2 2.5 %collective-permute-done.9.refs_3_ = bf16[400,384]{1,0:T(8,128)(2,1)S(1)} collective-permute-done((bf16[400,384]{1,0:T(8,128)(2,1)S(1)}, bf16[400,384]{1,0:T(8,128)(2,1)S(1)}, u32[]{:S(2)}, u32[]{:S(2)}) %collective-permute-start.9) | collective-permute-done | bytes 307232 | tf_op jit(solution)/shard_map/ppermute | solution.py:426
  36.8 0.6 %collective-permute-done.12.refs_7_ = bf16[400,384]{1,0:T(8,128)(2,1)S(1)} collective-permute-done((bf16[400,384]{1,0:T(8,128)(2,1)S(1)}, bf16[400,384]{1,0:T(8,128)(2,1)S(1)}, u32[]{:S(2)}, u32[]{:S(2)}) %collective-permute-start.12) | collective-permute-done | bytes 307232 | tf_op jit(solution)/shard_map/ppermute | solution.py:420
  37.4 0.9 %shard_map.80 = (bf16[384,768]{1,0:T(8,128)(2,1)}, f32[1,384]{1,0:T(1,128)}) custom-call(f32[384,384]{1,0:T(8,128)S(1)} %shard_map.74.refs_0_, f32[384,384]{1,0:T(8,128)S(1)} %shard_map.75.refs_1_, bf16[400,384]{1,0:T(8,128)(2,1)S(1)} %collective-permute-done.8.refs_2_, bf16[400,384]{1,0:T(8,128)(2,1)S(1)} %collective-permute-done.9.refs_3_, ...), custom_call_target="tpu_custom_call" | custom-call | tf_op jit(solution)/shard_map/pallas_call | solution.py:44
  (17 shorter events, 0.1 us)
Async XLA Ops:
  0.6 2.6 %copy-start.1 = (bf16[1,384,768]{2,1,0:T(8,128)(2,1)S(1)}, bf16[1,384,768]{2,1,0:T(8,128)(2,1)}, u32[]{:S(2)}) copy-start(bf16[1,384,768]{2,1,0:T(8,128)(2,1)} %param.5) | copy-start | bytes 1769476
  0.6 2.6 %copy-start.2 = (bf16[384,384]{1,0:T(8,128)(2,1)S(1)}, bf16[384,384]{1,0:T(8,128)(2,1)}, u32[]{:S(2)}) copy-start(bf16[384,384]{1,0:T(8,128)(2,1)} %own_ref.1) | copy-start | bytes 884740
  0.6 2.5 %collective-permute-start = (bf16[384,768]{1,0:T(8,128)(2,1)}, bf16[384,768]{1,0:T(8,128)(2,1)S(1)}, u32[]{:S(2)}, u32[]{:S(2)}) collective-permute-start(bf16[384,768]{1,0:T(8,128)(2,1)} %bitcast.2), channel_id=1, source_target_pairs={{0,1},{1,0},{2,3},{3,2},{4,5},{5,4},{6,7},{7,6},{8,9},{9,8},{10,11... | collective-permute-start | bytes 1769480 | tf_op jit(solution)/shard_map/ppermute | solution.py:170
  0.7 4.4 %collective-permute-start.1 = (bf16[384,384]{1,0:T(8,128)(2,1)}, bf16[384,384]{1,0:T(8,128)(2,1)S(1)}, u32[]{:S(2)}, u32[]{:S(2)}) collective-permute-start(bf16[384,384]{1,0:T(8,128)(2,1)} %own_ref.1), channel_id=1, source_target_pairs={{0,1},{2,3},{4,5},{6,7},{8,9},{10,11},{12,13},{14,15},{16,17},{18,... | collective-permute-start | bytes 884744 | tf_op jit(solution)/shard_map/ppermute | solution.py:166
  5.2 14.0 %copy-start = (bf16[3,384,384]{2,1,0:T(8,128)(2,1)S(1)}, bf16[3,384,384]{2,1,0:T(8,128)(2,1)}, u32[]{:S(2)}) copy-start(bf16[3,384,384]{2,1,0:T(8,128)(2,1)} %refs_4_.1) | copy-start | bytes 2654212
  5.3 8.8 %copy-start.3 = (s32[3]{0:T(128)S(1)}, s32[3]{0:T(128)}, u32[]{:S(2)}) copy-start(s32[3]{0:T(128)} %offsets_ref.1) | copy-start | bytes 40
  5.3 8.8 %copy-start.4 = (f32[3]{0:T(128)S(1)}, f32[3]{0:T(128)}, u32[]{:S(2)}) copy-start(f32[3]{0:T(128)} %bose_ref.1) | copy-start | bytes 40
  5.3 7.2 %collective-permute-start.3 = (bf16[384,384]{1,0:T(8,128)(2,1)S(1)}, bf16[384,384]{1,0:T(8,128)(2,1)S(1)}, u32[]{:S(2)}, u32[]{:S(2)}) collective-permute-start(bf16[384,384]{1,0:T(8,128)(2,1)S(1)} %get-tuple-element.59.refs_0_), channel_id=1, source_target_pairs={{0,4},{1,3},{2,6},{3,1},{4,0},{5,7},{6,2},{7,5},{8,12},{9,11},{10,... | collective-permute-start | bytes 884744 | tf_op jit(solution)/shard_map/ppermute | solution.py:420
  6.9 9.2 %collective-permute-start.2 = (bf16[384,384]{1,0:T(8,128)(2,1)S(1)}, bf16[384,384]{1,0:T(8,128)(2,1)S(1)}, u32[]{:S(2)}, u32[]{:S(2)}) collective-permute-start(bf16[384,384]{1,0:T(8,128)(2,1)S(1)} %get-tuple-element.37.own_ref), channel_id=1, source_target_pairs={{0,8},{2,10},{4,12},{6,14},{8,0},{10,2},{12,4},{14,6},{16,24},{18,... | collective-permute-start | bytes 884744 | tf_op jit(solution)/shard_map/ppermute | solution.py:426
  7.4 11.8 %collective-permute-start.4 = (bf16[384,384]{1,0:T(8,128)(2,1)S(1)}, bf16[384,384]{1,0:T(8,128)(2,1)S(1)}, u32[]{:S(2)}, u32[]{:S(2)}) collective-permute-start(bf16[384,384]{1,0:T(8,128)(2,1)S(1)} %get-tuple-element.37.own_ref), channel_id=1, source_target_pairs={{8,16},{10,18},{12,20},{14,22},{16,8},{18,10},{20,12},{22,14},{9,1... | collective-permute-start | bytes 884744 | tf_op jit(solution)/shard_map/ppermute | solution.py:426
  12.0 7.2 %collective-permute-start.5 = (bf16[384,384]{1,0:T(8,128)(2,1)S(1)}, bf16[384,384]{1,0:T(8,128)(2,1)S(1)}, u32[]{:S(2)}, u32[]{:S(2)}) collective-permute-start(bf16[384,384]{1,0:T(8,128)(2,1)S(1)} %get-tuple-element.59.refs_0_), channel_id=1, source_target_pairs={{0,2},{1,5},{2,0},{3,7},{4,6},{5,1},{6,4},{7,3},{8,10},{9,13},{10,... | collective-permute-start | bytes 884744 | tf_op jit(solution)/shard_map/ppermute | solution.py:420
  12.6 9.3 %collective-permute-start.7 = (bf16[384,384]{1,0:T(8,128)(2,1)S(1)}, bf16[384,384]{1,0:T(8,128)(2,1)S(1)}, u32[]{:S(2)}, u32[]{:S(2)}) collective-permute-start(bf16[384,384]{1,0:T(8,128)(2,1)S(1)} %collective-permute-done.3.refs_0_.refs_1_), channel_id=1, source_target_pairs={{0,2},{1,5},{2,0},{3,7},{4,6},{5,1},{6,4},{7,3},{8,10},{9,13},{10,... | collective-permute-start | bytes 884744 | tf_op jit(solution)/shard_map/ppermute | solution.py:420
  16.2 4.8 %collective-permute-start.6 = (f32[1,384]{1,0:T(1,128)S(1)}, f32[1,384]{1,0:T(1,128)S(1)}, u32[]{:S(2)}, u32[]{:S(2)}) collective-permute-start(f32[1,384]{1,0:T(1,128)S(1)} %get-tuple-element.45), channel_id=1, source_target_pairs={{0,16},{2,18},{4,20},{6,22},{8,24},{10,26},{12,28},{14,30},{16,0},... | collective-permute-start | bytes 4616 | tf_op jit(solution)/shard_map/ppermute | solution.py:426
  22.1 8.3 %collective-permute-start.11 = (bf16[400,384]{1,0:T(8,128)(2,1)S(1)}, bf16[400,384]{1,0:T(8,128)(2,1)S(1)}, u32[]{:S(2)}, u32[]{:S(2)}) collective-permute-start(bf16[400,384]{1,0:T(8,128)(2,1)S(1)} %get-tuple-element.58), channel_id=1, source_target_pairs={{0,4},{1,3},{2,6},{3,1},{4,0},{5,7},{6,2},{7,5},{8,12},{9,11},{10,... | collective-permute-start | bytes 921608 | tf_op jit(solution)/shard_map/ppermute | solution.py:420
  22.7 14.1 %collective-permute-start.10 = (bf16[416,384]{1,0:T(8,128)(2,1)S(1)}, bf16[416,384]{1,0:T(8,128)(2,1)S(1)}, u32[]{:S(2)}, u32[]{:S(2)}) collective-permute-start(bf16[416,384]{1,0:T(8,128)(2,1)S(1)} %get-tuple-element.62), channel_id=1, source_target_pairs={{0,4},{1,3},{2,6},{3,1},{4,0},{5,7},{6,2},{7,5},{8,12},{9,11},{10,... | collective-permute-start | bytes 958472 | tf_op jit(solution)/shard_map/ppermute | solution.py:420
  26.4 7.8 %collective-permute-start.8 = (bf16[400,384]{1,0:T(8,128)(2,1)S(1)}, bf16[400,384]{1,0:T(8,128)(2,1)S(1)}, u32[]{:S(2)}, u32[]{:S(2)}) collective-permute-start(bf16[400,384]{1,0:T(8,128)(2,1)S(1)} %get-tuple-element.60), channel_id=1, source_target_pairs={{0,8},{2,10},{4,12},{6,14},{8,0},{10,2},{12,4},{14,6},{16,24},{18,... | collective-permute-start | bytes 921608 | tf_op jit(solution)/shard_map/ppermute | solution.py:426
  26.5 10.3 %collective-permute-start.9 = (bf16[400,384]{1,0:T(8,128)(2,1)S(1)}, bf16[400,384]{1,0:T(8,128)(2,1)S(1)}, u32[]{:S(2)}, u32[]{:S(2)}) collective-permute-start(bf16[400,384]{1,0:T(8,128)(2,1)S(1)} %get-tuple-element.61), channel_id=1, source_target_pairs={{8,16},{10,18},{12,20},{14,22},{16,8},{18,10},{20,12},{22,14},{9,1... | collective-permute-start | bytes 921608 | tf_op jit(solution)/shard_map/ppermute | solution.py:426
  30.5 6.9 %collective-permute-start.12 = (bf16[400,384]{1,0:T(8,128)(2,1)S(1)}, bf16[400,384]{1,0:T(8,128)(2,1)S(1)}, u32[]{:S(2)}, u32[]{:S(2)}) collective-permute-start(bf16[400,384]{1,0:T(8,128)(2,1)S(1)} %shard_map.79), channel_id=1, source_target_pairs={{0,2},{1,5},{2,0},{3,7},{4,6},{5,1},{6,4},{7,3},{8,10},{9,13},{10,... | collective-permute-start | bytes 921608 | tf_op jit(solution)/shard_map/ppermute | solution.py:420

commit v8 on v7

--- a/solution.py
+++ b/solution.py
@@ -293,20 +293,21 @@
     _, group, seat = place()
     upward = seat < GROUP // 2
     first, second = hops()
-    for j, part in zip((0, first, second, GROUP - 1), parts):
-        bank[j] = part[...]
+    for j, part in zip((first, second, GROUP - 1), parts[1:]):
+        bank[j - 1] = part[...]
     modes = modes_of(phonon_ref, places_ref, factors_ref)
 
     def gives(shift, factor, up):
         source = seat + jnp.where(up, GROUP - shift, shift - GROUP)
         inside = jnp.logical_and(source >= 0, source < GROUP)
-        place_of = jnp.where(inside, jnp.bitwise_xor(seat, source), 0)
+        place_of = jnp.where(inside, jnp.bitwise_xor(seat, source) - 1, 0)
         return inside, place_of, jnp.where(up, factor + 1.0, factor)
 
     most = less = None
     for index, shift, factor in modes:
         inside, place_of, weight = gives(shift, factor, upward)
-        whole = product(phonon_ref[index], bank[place_of])
+        block = parts[0][...] if most is None else bank[place_of]
+        whole = product(phonon_ref[index], block)
         term = jnp.where(inside, weight, 0.0) * whole
         if most is None:
             most, less = term, gives(shift, factor, jnp.logical_not(upward))[2] * whole
@@ -497,7 +498,7 @@
     reals[0], _ = lax.optimization_barrier((reals[0], sums[0]))
     for_groups = jax.ShapeDtypeStruct((m + EXTRA_C, m), jnp.bfloat16)
     first_out, second_out = call(
-        to_groups, [for_groups] * 2, [*reals, *modes], [bank(GROUP), totals(2)]
+        to_groups, [for_groups] * 2, [*reals, *modes], [bank(GROUP - 1), totals(2)]
     )
     first_term = across_groups(first_out, first_pair)
     second_term = across_groups(second_out, second_pair)

time: 38.5 us -> 38.4 us (level)
  no operation moved by 1% of the time
where the time goes in v8:
time: 38.4 us; the launch traced here: 38.2 us
  starting transfers between devices  20.2 us (53%)
  Pallas kernels  9.65 us (25%)
  waiting for transfers between devices  7.52 us (20%)
  between operations  0.82 us (2%)
    ppermute x5, starting transfers between devices, across_groups(): lax.ppermute(value, 'energy', [(GROUP * a + i, GROUP * b + i) for a, b in...  11.6 us
    pallas_call x13, Pallas kernels, call(): pl.pallas_call(kernel, out_shape=outs, in_specs=[SCALARS if i.ndim == 1 e...  9.65 us
    ppermute x6, starting transfers between devices, hop(): return lax.ppermute(value, ('energy', 'slab'), pairs)  6.1 us
    ppermute x5, waiting for transfers between devices, across_groups(): lax.ppermute(value, 'energy', [(GROUP * a + i, GROUP * b + i) for a, b in...  5.97 us
    ppermute x1, starting transfers between devices, greens_halves(): below = lax.ppermute(coupling, 'slab', up)  2.41 us
    ppermute x6, waiting for transfers between devices, hop(): return lax.ppermute(value, ('energy', 'slab'), pairs)  1.55 us
  transfers between devices with their start and end apart: 13, of which 6 were waited for; matrix products, arithmetic and copies ran while one was open for 0% of the time, Pallas kernels for 22%

profile of v8, /device:TPU:10, one launch (start us, length us, event | category | flops | bytes accessed | tf_op | source)
XLA Modules:
  0.0 38.2 jit_solution(1939490581900483958)
XLA Ops:
  0.6 0.1 collective-permute-start
  0.7 2.4 %collective-permute-start.1 = (bf16[384,384]{1,0:T(8,128)(2,1)}, bf16[384,384]{1,0:T(8,128)(2,1)S(1)}, u32[]{:S(2)}, u32[]{:S(2)}) collective-permute-start(bf16[384,384]{1,0:T(8,128)(2,1)} %own_ref.1), channel_id=1, source_target_pairs={{0,1},{2,3},{4,5},{6,7},{8,9},{10,11},{12,13},{14,15},{16,17},{18,... | collective-permute-start | bytes 884744 | tf_op jit(solution)/shard_map/ppermute | solution.py:166
  3.2 2.0 %shard_map.69 = (bf16[384,384]{1,0:T(8,128)(2,1)S(1)}, bf16[384,384]{1,0:T(8,128)(2,1)S(1)}, f32[1,384]{1,0:T(1,128)S(1)}) custom-call(bf16[384,768]{1,0:T(8,128)(2,1)S(1)} %bitcast.3, bf16[384,768]{1,0:T(8,128)(2,1)S(1)} %collective-permute-done.other_ref, bf16[384,384]{1,0:T(8,128)(2,1)S(1)} %copy-done.2, f32[1,384]{1,0:T(1,128)S(1)} %shard_map.68.holes_ref), custom_call_target="tpu_custom_call" | custom-call | tf_op jit(solution)/shard_map/pallas_call | solution.py:44
  5.2 0.0 copy-start
  5.2 0.1 shard_map.70
  5.3 0.0 copy-start.3
  5.3 0.0 copy-start.4
  5.3 1.6 %collective-permute-start.3 = (bf16[384,384]{1,0:T(8,128)(2,1)S(1)}, bf16[384,384]{1,0:T(8,128)(2,1)S(1)}, u32[]{:S(2)}, u32[]{:S(2)}) collective-permute-start(bf16[384,384]{1,0:T(8,128)(2,1)S(1)} %get-tuple-element.59.refs_0_), channel_id=1, source_target_pairs={{0,4},{1,3},{2,6},{3,1},{4,0},{5,7},{6,2},{7,5},{8,12},{9,11},{10,... | collective-permute-start | bytes 884744 | tf_op jit(solution)/shard_map/ppermute | solution.py:421
  6.9 0.4 %collective-permute-start.2 = (bf16[384,384]{1,0:T(8,128)(2,1)S(1)}, bf16[384,384]{1,0:T(8,128)(2,1)S(1)}, u32[]{:S(2)}, u32[]{:S(2)}) collective-permute-start(bf16[384,384]{1,0:T(8,128)(2,1)S(1)} %get-tuple-element.37.own_ref), channel_id=1, source_target_pairs={{0,8},{2,10},{4,12},{6,14},{8,0},{10,2},{12,4},{14,6},{16,24},{18,... | collective-permute-start | bytes 884744 | tf_op jit(solution)/shard_map/ppermute | solution.py:427
  7.4 4.6 %collective-permute-start.4 = (bf16[384,384]{1,0:T(8,128)(2,1)S(1)}, bf16[384,384]{1,0:T(8,128)(2,1)S(1)}, u32[]{:S(2)}, u32[]{:S(2)}) collective-permute-start(bf16[384,384]{1,0:T(8,128)(2,1)S(1)} %get-tuple-element.37.own_ref), channel_id=1, source_target_pairs={{8,16},{10,18},{12,20},{14,22},{16,8},{18,10},{20,12},{22,14},{9,1... | collective-permute-start | bytes 884744 | tf_op jit(solution)/shard_map/ppermute | solution.py:427
  12.0 0.6 %collective-permute-start.5 = (bf16[384,384]{1,0:T(8,128)(2,1)S(1)}, bf16[384,384]{1,0:T(8,128)(2,1)S(1)}, u32[]{:S(2)}, u32[]{:S(2)}) collective-permute-start(bf16[384,384]{1,0:T(8,128)(2,1)S(1)} %get-tuple-element.59.refs_0_), channel_id=1, source_target_pairs={{0,2},{1,5},{2,0},{3,7},{4,6},{5,1},{6,4},{7,3},{8,10},{9,13},{10,... | collective-permute-start | bytes 884744 | tf_op jit(solution)/shard_map/ppermute | solution.py:421
  12.6 1.5 %collective-permute-start.7 = (bf16[384,384]{1,0:T(8,128)(2,1)S(1)}, bf16[384,384]{1,0:T(8,128)(2,1)S(1)}, u32[]{:S(2)}, u32[]{:S(2)}) collective-permute-start(bf16[384,384]{1,0:T(8,128)(2,1)S(1)} %collective-permute-done.3.refs_0_.refs_1_), channel_id=1, source_target_pairs={{0,2},{1,5},{2,0},{3,7},{4,6},{5,1},{6,4},{7,3},{8,10},{9,13},{10,... | collective-permute-start | bytes 884744 | tf_op jit(solution)/shard_map/ppermute | solution.py:421
  14.1 0.6 %shard_map.71 = (s32[8,128]{1,0:T(8,128)S(1)}, f32[8,128]{1,0:T(8,128)S(1)}) custom-call(s32[3]{0:T(128)S(1)} %copy-done.3, f32[3]{0:T(128)S(1)} %copy-done.4), custom_call_target="tpu_custom_call" | custom-call | tf_op jit(solution)/shard_map/pallas_call | solution.py:44
  14.6 1.5 %collective-permute-done.2.first_ref = bf16[384,384]{1,0:T(8,128)(2,1)S(1)} collective-permute-done((bf16[384,384]{1,0:T(8,128)(2,1)S(1)}, bf16[384,384]{1,0:T(8,128)(2,1)S(1)}, u32[]{:S(2)}, u32[]{:S(2)}) %collective-permute-start.2) | collective-permute-done | bytes 294944 | tf_op jit(solution)/shard_map/ppermute | solution.py:427
  16.2 2.7 %collective-permute-start.6 = (f32[1,384]{1,0:T(1,128)S(1)}, f32[1,384]{1,0:T(1,128)S(1)}, u32[]{:S(2)}, u32[]{:S(2)}) collective-permute-start(f32[1,384]{1,0:T(1,128)S(1)} %get-tuple-element.45), channel_id=1, source_target_pairs={{0,16},{2,18},{4,20},{6,22},{8,24},{10,26},{12,28},{14,30},{16,0},... | collective-permute-start | bytes 4616 | tf_op jit(solution)/shard_map/ppermute | solution.py:427
  18.8 0.3 collective-permute-done.4.second_ref
  19.2 1.8 %shard_map.73 = (bf16[400,384]{1,0:T(8,128)(2,1)S(1)}, bf16[416,384]{1,0:T(8,128)(2,1)S(1)}, bf16[400,384]{1,0:T(8,128)(2,1)S(1)}) custom-call(bf16[384,384]{1,0:T(8,128)(2,1)S(1)} %get-tuple-element.37.own_ref, bf16[384,384]{1,0:T(8,128)(2,1)S(1)} %collective-permute-done.2.first_ref, bf16[384,384]{1,0:T(8,128)(2,1)S(1)} %collective-permute-done.4.second_ref, ...), custom_call_target="tpu_custom_call" | custom-call | tf_op jit(solution)/shard_map/pallas_call | solution.py:44
  21.0 0.9 %collective-permute-done.7.refs_2_.refs_3_ = bf16[384,384]{1,0:T(8,128)(2,1)S(1)} collective-permute-done((bf16[384,384]{1,0:T(8,128)(2,1)S(1)}, bf16[384,384]{1,0:T(8,128)(2,1)S(1)}, u32[]{:S(2)}, u32[]{:S(2)}) %collective-permute-start.7) | collective-permute-done | bytes 294944 | tf_op jit(solution)/shard_map/ppermute | solution.py:421
  21.9 0.2 shard_map.77
  22.1 0.6 %collective-permute-start.11 = (bf16[400,384]{1,0:T(8,128)(2,1)S(1)}, bf16[400,384]{1,0:T(8,128)(2,1)S(1)}, u32[]{:S(2)}, u32[]{:S(2)}) collective-permute-start(bf16[400,384]{1,0:T(8,128)(2,1)S(1)} %get-tuple-element.58), channel_id=1, source_target_pairs={{0,4},{1,3},{2,6},{3,1},{4,0},{5,7},{6,2},{7,5},{8,12},{9,11},{10,... | collective-permute-start | bytes 921608 | tf_op jit(solution)/shard_map/ppermute | solution.py:421
  22.7 1.5 %collective-permute-start.10 = (bf16[416,384]{1,0:T(8,128)(2,1)S(1)}, bf16[416,384]{1,0:T(8,128)(2,1)S(1)}, u32[]{:S(2)}, u32[]{:S(2)}) collective-permute-start(bf16[416,384]{1,0:T(8,128)(2,1)S(1)} %get-tuple-element.62), channel_id=1, source_target_pairs={{0,4},{1,3},{2,6},{3,1},{4,0},{5,7},{6,2},{7,5},{8,12},{9,11},{10,... | collective-permute-start | bytes 958472 | tf_op jit(solution)/shard_map/ppermute | solution.py:421
  24.2 2.1 %shard_map.78 = (bf16[400,384]{1,0:T(8,128)(2,1)S(1)}, bf16[400,384]{1,0:T(8,128)(2,1)S(1)}) custom-call(bf16[384,384]{1,0:T(8,128)(2,1)S(1)} %get-tuple-element.59.refs_0_, bf16[384,384]{1,0:T(8,128)(2,1)S(1)} %collective-permute-done.3.refs_0_.refs_1_, bf16[384,384]{1,0:T(8,128)(2,1)S(1)} %collective-permute-done.5.refs_1_.refs_2_, ...), custom_call_target="tpu_custom_call" | custom-call | tf_op jit(solution)/shard_map/pallas_call | solution.py:44
  26.3 0.1 collective-permute-start.8
  26.4 3.9 %collective-permute-start.9 = (bf16[400,384]{1,0:T(8,128)(2,1)S(1)}, bf16[400,384]{1,0:T(8,128)(2,1)S(1)}, u32[]{:S(2)}, u32[]{:S(2)}) collective-permute-start(bf16[400,384]{1,0:T(8,128)(2,1)S(1)} %get-tuple-element.61), channel_id=1, source_target_pairs={{8,16},{10,18},{12,20},{14,22},{16,8},{18,10},{20,12},{22,14},{9,1... | collective-permute-start | bytes 921608 | tf_op jit(solution)/shard_map/ppermute | solution.py:427
  30.3 0.1 shard_map.79
  30.4 0.3 collective-permute-start.12
  30.7 0.7 %shard_map.75.refs_1_ = f32[384,384]{1,0:T(8,128)S(1)} custom-call(bf16[384,384]{1,0:T(8,128)(2,1)S(1)} %collective-permute-done.2.first_ref, bf16[384,384]{1,0:T(8,128)(2,1)S(1)} %collective-permute-done.4.second_ref, bf16[3,384,384]{2,1,0:T(8,128)(2,1)S(1)} %copy-done, s32[8,128]{1,0:T(8,128)S(1)} %get-tuple-element.47.places_ref.refs_4_.refs_5_, ...), custom_call_target="tpu_custom_call" | custom-call | tf_op jit(solution)/shard_map/pallas_call | solution.py:44
  31.4 1.1 %shard_map.74.refs_0_ = f32[384,384]{1,0:T(8,128)S(1)} custom-call(bf16[384,384]{1,0:T(8,128)(2,1)S(1)} %collective-permute-done.3.refs_0_.refs_1_, bf16[384,384]{1,0:T(8,128)(2,1)S(1)} %collective-permute-done.5.refs_1_.refs_2_, bf16[384,384]{1,0:T(8,128)(2,1)S(1)} %collective-permute-done.7.refs_2_.refs_3_, bf16[3,384,384]{2,1,0:T(8,128)(2,1)S(1)} %copy-done, ...), custom_call_target="tpu_custom_call" | custom-call | tf_op jit(solution)/shard_map/pallas_call | solution.py:44
  32.5 1.6 %collective-permute-done.8.refs_2_ = bf16[400,384]{1,0:T(8,128)(2,1)S(1)} collective-permute-done((bf16[400,384]{1,0:T(8,128)(2,1)S(1)}, bf16[400,384]{1,0:T(8,128)(2,1)S(1)}, u32[]{:S(2)}, u32[]{:S(2)}) %collective-permute-start.8) | collective-permute-done | bytes 307232 | tf_op jit(solution)/shard_map/ppermute | solution.py:427
  34.1 2.5 %collective-permute-done.9.refs_3_ = bf16[400,384]{1,0:T(8,128)(2,1)S(1)} collective-permute-done((bf16[400,384]{1,0:T(8,128)(2,1)S(1)}, bf16[400,384]{1,0:T(8,128)(2,1)S(1)}, u32[]{:S(2)}, u32[]{:S(2)}) %collective-permute-start.9) | collective-permute-done | bytes 307232 | tf_op jit(solution)/shard_map/ppermute | solution.py:427
  36.7 0.6 %collective-permute-done.12.refs_7_ = bf16[400,384]{1,0:T(8,128)(2,1)S(1)} collective-permute-done((bf16[400,384]{1,0:T(8,128)(2,1)S(1)}, bf16[400,384]{1,0:T(8,128)(2,1)S(1)}, u32[]{:S(2)}, u32[]{:S(2)}) %collective-permute-start.12) | collective-permute-done | bytes 307232 | tf_op jit(solution)/shard_map/ppermute | solution.py:421
  37.3 0.9 %shard_map.80 = (bf16[384,768]{1,0:T(8,128)(2,1)}, f32[1,384]{1,0:T(1,128)}) custom-call(f32[384,384]{1,0:T(8,128)S(1)} %shard_map.74.refs_0_, f32[384,384]{1,0:T(8,128)S(1)} %shard_map.75.refs_1_, bf16[400,384]{1,0:T(8,128)(2,1)S(1)} %collective-permute-done.8.refs_2_, bf16[400,384]{1,0:T(8,128)(2,1)S(1)} %collective-permute-done.9.refs_3_, ...), custom_call_target="tpu_custom_call" | custom-call | tf_op jit(solution)/shard_map/pallas_call | solution.py:44
  (17 shorter events, 0.1 us)
Async XLA Ops:
  0.6 2.6 %copy-start.1 = (bf16[1,384,768]{2,1,0:T(8,128)(2,1)S(1)}, bf16[1,384,768]{2,1,0:T(8,128)(2,1)}, u32[]{:S(2)}) copy-start(bf16[1,384,768]{2,1,0:T(8,128)(2,1)} %param.5) | copy-start | bytes 1769476
  0.6 2.6 %copy-start.2 = (bf16[384,384]{1,0:T(8,128)(2,1)S(1)}, bf16[384,384]{1,0:T(8,128)(2,1)}, u32[]{:S(2)}) copy-start(bf16[384,384]{1,0:T(8,128)(2,1)} %own_ref.1) | copy-start | bytes 884740
  0.6 2.5 %collective-permute-start = (bf16[384,768]{1,0:T(8,128)(2,1)}, bf16[384,768]{1,0:T(8,128)(2,1)S(1)}, u32[]{:S(2)}, u32[]{:S(2)}) collective-permute-start(bf16[384,768]{1,0:T(8,128)(2,1)} %bitcast.2), channel_id=1, source_target_pairs={{0,1},{1,0},{2,3},{3,2},{4,5},{5,4},{6,7},{7,6},{8,9},{9,8},{10,11... | collective-permute-start | bytes 1769480 | tf_op jit(solution)/shard_map/ppermute | solution.py:170
  0.7 4.4 %collective-permute-start.1 = (bf16[384,384]{1,0:T(8,128)(2,1)}, bf16[384,384]{1,0:T(8,128)(2,1)S(1)}, u32[]{:S(2)}, u32[]{:S(2)}) collective-permute-start(bf16[384,384]{1,0:T(8,128)(2,1)} %own_ref.1), channel_id=1, source_target_pairs={{0,1},{2,3},{4,5},{6,7},{8,9},{10,11},{12,13},{14,15},{16,17},{18,... | collective-permute-start | bytes 884744 | tf_op jit(solution)/shard_map/ppermute | solution.py:166
  5.2 14.0 %copy-start = (bf16[3,384,384]{2,1,0:T(8,128)(2,1)S(1)}, bf16[3,384,384]{2,1,0:T(8,128)(2,1)}, u32[]{:S(2)}) copy-start(bf16[3,384,384]{2,1,0:T(8,128)(2,1)} %refs_4_.1) | copy-start | bytes 2654212
  5.3 8.8 %copy-start.3 = (s32[3]{0:T(128)S(1)}, s32[3]{0:T(128)}, u32[]{:S(2)}) copy-start(s32[3]{0:T(128)} %offsets_ref.1) | copy-start | bytes 40
  5.3 8.8 %copy-start.4 = (f32[3]{0:T(128)S(1)}, f32[3]{0:T(128)}, u32[]{:S(2)}) copy-start(f32[3]{0:T(128)} %bose_ref.1) | copy-start | bytes 40
  5.3 7.2 %collective-permute-start.3 = (bf16[384,384]{1,0:T(8,128)(2,1)S(1)}, bf16[384,384]{1,0:T(8,128)(2,1)S(1)}, u32[]{:S(2)}, u32[]{:S(2)}) collective-permute-start(bf16[384,384]{1,0:T(8,128)(2,1)S(1)} %get-tuple-element.59.refs_0_), channel_id=1, source_target_pairs={{0,4},{1,3},{2,6},{3,1},{4,0},{5,7},{6,2},{7,5},{8,12},{9,11},{10,... | collective-permute-start | bytes 884744 | tf_op jit(solution)/shard_map/ppermute | solution.py:421
  6.9 9.2 %collective-permute-start.2 = (bf16[384,384]{1,0:T(8,128)(2,1)S(1)}, bf16[384,384]{1,0:T(8,128)(2,1)S(1)}, u32[]{:S(2)}, u32[]{:S(2)}) collective-permute-start(bf16[384,384]{1,0:T(8,128)(2,1)S(1)} %get-tuple-element.37.own_ref), channel_id=1, source_target_pairs={{0,8},{2,10},{4,12},{6,14},{8,0},{10,2},{12,4},{14,6},{16,24},{18,... | collective-permute-start | bytes 884744 | tf_op jit(solution)/shard_map/ppermute | solution.py:427
  7.4 11.8 %collective-permute-start.4 = (bf16[384,384]{1,0:T(8,128)(2,1)S(1)}, bf16[384,384]{1,0:T(8,128)(2,1)S(1)}, u32[]{:S(2)}, u32[]{:S(2)}) collective-permute-start(bf16[384,384]{1,0:T(8,128)(2,1)S(1)} %get-tuple-element.37.own_ref), channel_id=1, source_target_pairs={{8,16},{10,18},{12,20},{14,22},{16,8},{18,10},{20,12},{22,14},{9,1... | collective-permute-start | bytes 884744 | tf_op jit(solution)/shard_map/ppermute | solution.py:427
  12.0 7.2 %collective-permute-start.5 = (bf16[384,384]{1,0:T(8,128)(2,1)S(1)}, bf16[384,384]{1,0:T(8,128)(2,1)S(1)}, u32[]{:S(2)}, u32[]{:S(2)}) collective-permute-start(bf16[384,384]{1,0:T(8,128)(2,1)S(1)} %get-tuple-element.59.refs_0_), channel_id=1, source_target_pairs={{0,2},{1,5},{2,0},{3,7},{4,6},{5,1},{6,4},{7,3},{8,10},{9,13},{10,... | collective-permute-start | bytes 884744 | tf_op jit(solution)/shard_map/ppermute | solution.py:421
  12.6 9.3 %collective-permute-start.7 = (bf16[384,384]{1,0:T(8,128)(2,1)S(1)}, bf16[384,384]{1,0:T(8,128)(2,1)S(1)}, u32[]{:S(2)}, u32[]{:S(2)}) collective-permute-start(bf16[384,384]{1,0:T(8,128)(2,1)S(1)} %collective-permute-done.3.refs_0_.refs_1_), channel_id=1, source_target_pairs={{0,2},{1,5},{2,0},{3,7},{4,6},{5,1},{6,4},{7,3},{8,10},{9,13},{10,... | collective-permute-start | bytes 884744 | tf_op jit(solution)/shard_map/ppermute | solution.py:421
  16.2 4.8 %collective-permute-start.6 = (f32[1,384]{1,0:T(1,128)S(1)}, f32[1,384]{1,0:T(1,128)S(1)}, u32[]{:S(2)}, u32[]{:S(2)}) collective-permute-start(f32[1,384]{1,0:T(1,128)S(1)} %get-tuple-element.45), channel_id=1, source_target_pairs={{0,16},{2,18},{4,20},{6,22},{8,24},{10,26},{12,28},{14,30},{16,0},... | collective-permute-start | bytes 4616 | tf_op jit(solution)/shard_map/ppermute | solution.py:427
  22.1 8.2 %collective-permute-start.11 = (bf16[400,384]{1,0:T(8,128)(2,1)S(1)}, bf16[400,384]{1,0:T(8,128)(2,1)S(1)}, u32[]{:S(2)}, u32[]{:S(2)}) collective-permute-start(bf16[400,384]{1,0:T(8,128)(2,1)S(1)} %get-tuple-element.58), channel_id=1, source_target_pairs={{0,4},{1,3},{2,6},{3,1},{4,0},{5,7},{6,2},{7,5},{8,12},{9,11},{10,... | collective-permute-start | bytes 921608 | tf_op jit(solution)/shard_map/ppermute | solution.py:421
  22.7 14.0 %collective-permute-start.10 = (bf16[416,384]{1,0:T(8,128)(2,1)S(1)}, bf16[416,384]{1,0:T(8,128)(2,1)S(1)}, u32[]{:S(2)}, u32[]{:S(2)}) collective-permute-start(bf16[416,384]{1,0:T(8,128)(2,1)S(1)} %get-tuple-element.62), channel_id=1, source_target_pairs={{0,4},{1,3},{2,6},{3,1},{4,0},{5,7},{6,2},{7,5},{8,12},{9,11},{10,... | collective-permute-start | bytes 958472 | tf_op jit(solution)/shard_map/ppermute | solution.py:421
  26.3 7.8 %collective-permute-start.8 = (bf16[400,384]{1,0:T(8,128)(2,1)S(1)}, bf16[400,384]{1,0:T(8,128)(2,1)S(1)}, u32[]{:S(2)}, u32[]{:S(2)}) collective-permute-start(bf16[400,384]{1,0:T(8,128)(2,1)S(1)} %get-tuple-element.60), channel_id=1, source_target_pairs={{0,8},{2,10},{4,12},{6,14},{8,0},{10,2},{12,4},{14,6},{16,24},{18,... | collective-permute-start | bytes 921608 | tf_op jit(solution)/shard_map/ppermute | solution.py:427
  26.4 10.3 %collective-permute-start.9 = (bf16[400,384]{1,0:T(8,128)(2,1)S(1)}, bf16[400,384]{1,0:T(8,128)(2,1)S(1)}, u32[]{:S(2)}, u32[]{:S(2)}) collective-permute-start(bf16[400,384]{1,0:T(8,128)(2,1)S(1)} %get-tuple-element.61), channel_id=1, source_target_pairs={{8,16},{10,18},{12,20},{14,22},{16,8},{18,10},{20,12},{22,14},{9,1... | collective-permute-start | bytes 921608 | tf_op jit(solution)/shard_map/ppermute | solution.py:427
  30.4 6.9 %collective-permute-start.12 = (bf16[400,384]{1,0:T(8,128)(2,1)S(1)}, bf16[400,384]{1,0:T(8,128)(2,1)S(1)}, u32[]{:S(2)}, u32[]{:S(2)}) collective-permute-start(bf16[400,384]{1,0:T(8,128)(2,1)S(1)} %shard_map.79), channel_id=1, source_target_pairs={{0,2},{1,5},{2,0},{3,7},{4,6},{5,1},{6,4},{7,3},{8,10},{9,13},{10,... | collective-permute-start | bytes 921608 | tf_op jit(solution)/shard_map/ppermute | solution.py:421

commit v9 on v8

--- a/solution.py
+++ b/solution.py
@@ -185,7 +185,7 @@
 
 
 def hops():
-    bit = 2 - lax.rem(lax.axis_index("slab"), 2)
+    bit = 1 + lax.rem(lax.axis_index("slab"), 2)
     return bit, (GROUP - 1) - bit
 
 
@@ -410,7 +410,7 @@
 
 def hop(value, second):
     energies, slabs = lax.axis_size("energy"), lax.axis_size("slab")
-    bits = [2 - slab % 2 for slab in range(slabs)]
+    bits = [1 + slab % 2 for slab in range(slabs)]
     if second:
         bits = [GROUP - 1 - bit for bit in bits]
     pairs = [
@@ -504,7 +504,7 @@
     second_term = across_groups(second_out, second_pair)
     (real_total,) = call(group_terms, [wide], [*reals[1:], *modes], [bank(GROUP - 1)])
 
-    pieces = 4 if m % 64 == 0 else 1
+    pieces = 2 if m % 32 == 0 else 1
     sigma, cumulative = call(
         last_sum,
         [jax.ShapeDtypeStruct(g.shape, jnp.bfloat16), line],

time: 38.4 us -> 38.2 us (level)
  the two profiles are of different devices: /device:TPU:10 before, /device:TPU:8 now
where the time goes in v9:
time: 38.2 us; the launch traced here: 38 us
  starting transfers between devices  21.5 us (56%)
  Pallas kernels  8.81 us (23%)
  waiting for transfers between devices  6.93 us (18%)
  between operations  0.81 us (2%)
    ppermute x5, starting transfers between devices, across_groups(): lax.ppermute(value, 'energy', [(GROUP * a + i, GROUP * b + i) for a, b in...  12.1 us
    pallas_call x13, Pallas kernels, call(): pl.pallas_call(kernel, out_shape=outs, in_specs=[SCALARS if i.ndim == 1 e...  8.81 us
    ppermute x6, starting transfers between devices, hop(): return lax.ppermute(value, ('energy', 'slab'), pairs)  6.92 us
    ppermute x5, waiting for transfers between devices, across_groups(): lax.ppermute(value, 'energy', [(GROUP * a + i, GROUP * b + i) for a, b in...  5.25 us
    ppermute x1, starting transfers between devices, greens_halves(): below = lax.ppermute(coupling, 'slab', up)  2.41 us
    ppermute x6, waiting for transfers between devices, hop(): return lax.ppermute(value, ('energy', 'slab'), pairs)  1.67 us
  transfers between devices with their start and end apart: 13, of which 6 were waited for; matrix products, arithmetic and copies ran while one was open for 0% of the time, Pallas kernels for 20%

profile of v9, /device:TPU:8, one launch (start us, length us, event | category | flops | bytes accessed | tf_op | source)
XLA Modules:
  0.0 38.0 jit_solution(7065095826580727602)
XLA Ops:
  0.6 0.1 collective-permute-start
  0.7 2.4 %collective-permute-start.1 = (bf16[384,384]{1,0:T(8,128)(2,1)}, bf16[384,384]{1,0:T(8,128)(2,1)S(1)}, u32[]{:S(2)}, u32[]{:S(2)}) collective-permute-start(bf16[384,384]{1,0:T(8,128)(2,1)} %own_ref.1), channel_id=1, source_target_pairs={{0,1},{2,3},{4,5},{6,7},{8,9},{10,11},{12,13},{14,15},{16,17},{18,... | collective-permute-start | bytes 884744 | tf_op jit(solution)/shard_map/ppermute | solution.py:166
  3.2 2.0 %shard_map.69 = (bf16[384,384]{1,0:T(8,128)(2,1)S(1)}, bf16[384,384]{1,0:T(8,128)(2,1)S(1)}, f32[1,384]{1,0:T(1,128)S(1)}) custom-call(bf16[384,768]{1,0:T(8,128)(2,1)S(1)} %bitcast.3, bf16[384,768]{1,0:T(8,128)(2,1)S(1)} %collective-permute-done.other_ref, bf16[384,384]{1,0:T(8,128)(2,1)S(1)} %copy-done.2, f32[1,384]{1,0:T(1,128)S(1)} %shard_map.68.holes_ref), custom_call_target="tpu_custom_call" | custom-call | tf_op jit(solution)/shard_map/pallas_call | solution.py:44
  5.2 0.0 copy-start
  5.2 0.1 shard_map.70
  5.3 0.0 copy-start.3
  5.3 1.6 %collective-permute-start.3 = (bf16[384,384]{1,0:T(8,128)(2,1)S(1)}, bf16[384,384]{1,0:T(8,128)(2,1)S(1)}, u32[]{:S(2)}, u32[]{:S(2)}) collective-permute-start(bf16[384,384]{1,0:T(8,128)(2,1)S(1)} %get-tuple-element.59.refs_0_), channel_id=1, source_target_pairs={{0,2},{1,5},{2,0},{3,7},{4,6},{5,1},{6,4},{7,3},{8,10},{9,13},{10,... | collective-permute-start | bytes 884744 | tf_op jit(solution)/shard_map/ppermute | solution.py:421
  6.9 0.4 %collective-permute-start.2 = (bf16[384,384]{1,0:T(8,128)(2,1)S(1)}, bf16[384,384]{1,0:T(8,128)(2,1)S(1)}, u32[]{:S(2)}, u32[]{:S(2)}) collective-permute-start(bf16[384,384]{1,0:T(8,128)(2,1)S(1)} %get-tuple-element.37.own_ref), channel_id=1, source_target_pairs={{0,8},{2,10},{4,12},{6,14},{8,0},{10,2},{12,4},{14,6},{16,24},{18,... | collective-permute-start | bytes 884744 | tf_op jit(solution)/shard_map/ppermute | solution.py:427
  7.3 4.6 %collective-permute-start.4 = (bf16[384,384]{1,0:T(8,128)(2,1)S(1)}, bf16[384,384]{1,0:T(8,128)(2,1)S(1)}, u32[]{:S(2)}, u32[]{:S(2)}) collective-permute-start(bf16[384,384]{1,0:T(8,128)(2,1)S(1)} %get-tuple-element.37.own_ref), channel_id=1, source_target_pairs={{8,16},{10,18},{12,20},{14,22},{16,8},{18,10},{20,12},{22,14},{9,1... | collective-permute-start | bytes 884744 | tf_op jit(solution)/shard_map/ppermute | solution.py:427
  11.9 1.6 %collective-permute-start.5 = (bf16[384,384]{1,0:T(8,128)(2,1)S(1)}, bf16[384,384]{1,0:T(8,128)(2,1)S(1)}, u32[]{:S(2)}, u32[]{:S(2)}) collective-permute-start(bf16[384,384]{1,0:T(8,128)(2,1)S(1)} %get-tuple-element.59.refs_0_), channel_id=1, source_target_pairs={{0,4},{1,3},{2,6},{3,1},{4,0},{5,7},{6,2},{7,5},{8,12},{9,11},{10,... | collective-permute-start | bytes 884744 | tf_op jit(solution)/shard_map/ppermute | solution.py:421
  13.5 0.5 %collective-permute-start.7 = (bf16[384,384]{1,0:T(8,128)(2,1)S(1)}, bf16[384,384]{1,0:T(8,128)(2,1)S(1)}, u32[]{:S(2)}, u32[]{:S(2)}) collective-permute-start(bf16[384,384]{1,0:T(8,128)(2,1)S(1)} %collective-permute-done.3.refs_0_.refs_1_), channel_id=1, source_target_pairs={{0,4},{1,3},{2,6},{3,1},{4,0},{5,7},{6,2},{7,5},{8,12},{9,11},{10,... | collective-permute-start | bytes 884744 | tf_op jit(solution)/shard_map/ppermute | solution.py:421
  14.0 0.6 %shard_map.71 = (s32[8,128]{1,0:T(8,128)S(1)}, f32[8,128]{1,0:T(8,128)S(1)}) custom-call(s32[3]{0:T(128)S(1)} %copy-done.3, f32[3]{0:T(128)S(1)} %copy-done.4), custom_call_target="tpu_custom_call" | custom-call | tf_op jit(solution)/shard_map/pallas_call | solution.py:44
  14.6 1.9 %collective-permute-done.2.first_ref = bf16[384,384]{1,0:T(8,128)(2,1)S(1)} collective-permute-done((bf16[384,384]{1,0:T(8,128)(2,1)S(1)}, bf16[384,384]{1,0:T(8,128)(2,1)S(1)}, u32[]{:S(2)}, u32[]{:S(2)}) %collective-permute-start.2) | collective-permute-done | bytes 294944 | tf_op jit(solution)/shard_map/ppermute | solution.py:427
  16.5 2.7 %collective-permute-start.6 = (f32[1,384]{1,0:T(1,128)S(1)}, f32[1,384]{1,0:T(1,128)S(1)}, u32[]{:S(2)}, u32[]{:S(2)}) collective-permute-start(f32[1,384]{1,0:T(1,128)S(1)} %get-tuple-element.45), channel_id=1, source_target_pairs={{0,16},{2,18},{4,20},{6,22},{8,24},{10,26},{12,28},{14,30},{16,0},... | collective-permute-start | bytes 4616 | tf_op jit(solution)/shard_map/ppermute | solution.py:427
  19.2 0.3 collective-permute-done.4.second_ref
  19.5 1.5 %shard_map.73 = (bf16[400,384]{1,0:T(8,128)(2,1)S(1)}, bf16[416,384]{1,0:T(8,128)(2,1)S(1)}, bf16[400,384]{1,0:T(8,128)(2,1)S(1)}) custom-call(bf16[384,384]{1,0:T(8,128)(2,1)S(1)} %get-tuple-element.37.own_ref, bf16[384,384]{1,0:T(8,128)(2,1)S(1)} %collective-permute-done.2.first_ref, bf16[384,384]{1,0:T(8,128)(2,1)S(1)} %collective-permute-done.4.second_ref, ...), custom_call_target="tpu_custom_call" | custom-call | tf_op jit(solution)/shard_map/pallas_call | solution.py:44
  21.1 0.0 collective-permute-done.6.refs_1_
  21.1 0.8 %collective-permute-done.7.refs_2_.refs_3_ = bf16[384,384]{1,0:T(8,128)(2,1)S(1)} collective-permute-done((bf16[384,384]{1,0:T(8,128)(2,1)S(1)}, bf16[384,384]{1,0:T(8,128)(2,1)S(1)}, u32[]{:S(2)}, u32[]{:S(2)}) %collective-permute-start.7) | collective-permute-done | bytes 294944 | tf_op jit(solution)/shard_map/ppermute | solution.py:421
  21.9 0.2 shard_map.77
  22.1 0.6 %collective-permute-start.11 = (bf16[400,384]{1,0:T(8,128)(2,1)S(1)}, bf16[400,384]{1,0:T(8,128)(2,1)S(1)}, u32[]{:S(2)}, u32[]{:S(2)}) collective-permute-start(bf16[400,384]{1,0:T(8,128)(2,1)S(1)} %get-tuple-element.58), channel_id=1, source_target_pairs={{0,2},{1,5},{2,0},{3,7},{4,6},{5,1},{6,4},{7,3},{8,10},{9,13},{10,... | collective-permute-start | bytes 921608 | tf_op jit(solution)/shard_map/ppermute | solution.py:421
  22.7 1.5 %collective-permute-start.10 = (bf16[416,384]{1,0:T(8,128)(2,1)S(1)}, bf16[416,384]{1,0:T(8,128)(2,1)S(1)}, u32[]{:S(2)}, u32[]{:S(2)}) collective-permute-start(bf16[416,384]{1,0:T(8,128)(2,1)S(1)} %get-tuple-element.62), channel_id=1, source_target_pairs={{0,2},{1,5},{2,0},{3,7},{4,6},{5,1},{6,4},{7,3},{8,10},{9,13},{10,... | collective-permute-start | bytes 958472 | tf_op jit(solution)/shard_map/ppermute | solution.py:421
  24.2 1.5 %shard_map.78 = (bf16[400,384]{1,0:T(8,128)(2,1)S(1)}, bf16[400,384]{1,0:T(8,128)(2,1)S(1)}) custom-call(bf16[384,384]{1,0:T(8,128)(2,1)S(1)} %get-tuple-element.59.refs_0_, bf16[384,384]{1,0:T(8,128)(2,1)S(1)} %collective-permute-done.3.refs_0_.refs_1_, bf16[384,384]{1,0:T(8,128)(2,1)S(1)} %collective-permute-done.5.refs_1_.refs_2_, ...), custom_call_target="tpu_custom_call" | custom-call | tf_op jit(solution)/shard_map/pallas_call | solution.py:44
  25.7 0.1 collective-permute-start.8
  25.8 4.3 %collective-permute-start.9 = (bf16[400,384]{1,0:T(8,128)(2,1)S(1)}, bf16[400,384]{1,0:T(8,128)(2,1)S(1)}, u32[]{:S(2)}, u32[]{:S(2)}) collective-permute-start(bf16[400,384]{1,0:T(8,128)(2,1)S(1)} %get-tuple-element.61), channel_id=1, source_target_pairs={{8,16},{10,18},{12,20},{14,22},{16,8},{18,10},{20,12},{22,14},{9,1... | collective-permute-start | bytes 921608 | tf_op jit(solution)/shard_map/ppermute | solution.py:427
  30.1 0.1 shard_map.79
  30.2 1.2 %collective-permute-start.12 = (bf16[400,384]{1,0:T(8,128)(2,1)S(1)}, bf16[400,384]{1,0:T(8,128)(2,1)S(1)}, u32[]{:S(2)}, u32[]{:S(2)}) collective-permute-start(bf16[400,384]{1,0:T(8,128)(2,1)S(1)} %shard_map.79), channel_id=1, source_target_pairs={{0,4},{1,3},{2,6},{3,1},{4,0},{5,7},{6,2},{7,5},{8,12},{9,11},{10,... | collective-permute-start | bytes 921608 | tf_op jit(solution)/shard_map/ppermute | solution.py:421
  31.3 0.7 %shard_map.75.refs_1_ = f32[384,384]{1,0:T(8,128)S(1)} custom-call(bf16[384,384]{1,0:T(8,128)(2,1)S(1)} %collective-permute-done.2.first_ref, bf16[384,384]{1,0:T(8,128)(2,1)S(1)} %collective-permute-done.4.second_ref, bf16[3,384,384]{2,1,0:T(8,128)(2,1)S(1)} %copy-done, s32[8,128]{1,0:T(8,128)S(1)} %get-tuple-element.47.places_ref.refs_4_.refs_5_, ...), custom_call_target="tpu_custom_call" | custom-call | tf_op jit(solution)/shard_map/pallas_call | solution.py:44
  32.0 1.1 %shard_map.74.refs_0_ = f32[384,384]{1,0:T(8,128)S(1)} custom-call(bf16[384,384]{1,0:T(8,128)(2,1)S(1)} %collective-permute-done.3.refs_0_.refs_1_, bf16[384,384]{1,0:T(8,128)(2,1)S(1)} %collective-permute-done.5.refs_1_.refs_2_, bf16[384,384]{1,0:T(8,128)(2,1)S(1)} %collective-permute-done.7.refs_2_.refs_3_, bf16[3,384,384]{2,1,0:T(8,128)(2,1)S(1)} %copy-done, ...), custom_call_target="tpu_custom_call" | custom-call | tf_op jit(solution)/shard_map/pallas_call | solution.py:44
  33.2 1.1 %collective-permute-done.8.refs_2_ = bf16[400,384]{1,0:T(8,128)(2,1)S(1)} collective-permute-done((bf16[400,384]{1,0:T(8,128)(2,1)S(1)}, bf16[400,384]{1,0:T(8,128)(2,1)S(1)}, u32[]{:S(2)}, u32[]{:S(2)}) %collective-permute-start.8) | collective-permute-done | bytes 307232 | tf_op jit(solution)/shard_map/ppermute | solution.py:427
  34.3 1.9 %collective-permute-done.9.refs_3_ = bf16[400,384]{1,0:T(8,128)(2,1)S(1)} collective-permute-done((bf16[400,384]{1,0:T(8,128)(2,1)S(1)}, bf16[400,384]{1,0:T(8,128)(2,1)S(1)}, u32[]{:S(2)}, u32[]{:S(2)}) %collective-permute-start.9) | collective-permute-done | bytes 307232 | tf_op jit(solution)/shard_map/ppermute | solution.py:427
  36.2 0.9 %collective-permute-done.12.refs_7_ = bf16[400,384]{1,0:T(8,128)(2,1)S(1)} collective-permute-done((bf16[400,384]{1,0:T(8,128)(2,1)S(1)}, bf16[400,384]{1,0:T(8,128)(2,1)S(1)}, u32[]{:S(2)}, u32[]{:S(2)}) %collective-permute-start.12) | collective-permute-done | bytes 307232 | tf_op jit(solution)/shard_map/ppermute | solution.py:421
  37.1 0.9 %shard_map.80 = (bf16[384,768]{1,0:T(8,128)(2,1)}, f32[1,384]{1,0:T(1,128)}) custom-call(f32[384,384]{1,0:T(8,128)S(1)} %shard_map.74.refs_0_, f32[384,384]{1,0:T(8,128)S(1)} %shard_map.75.refs_1_, bf16[400,384]{1,0:T(8,128)(2,1)S(1)} %collective-permute-done.8.refs_2_, bf16[400,384]{1,0:T(8,128)(2,1)S(1)} %collective-permute-done.9.refs_3_, ...), custom_call_target="tpu_custom_call" | custom-call | tf_op jit(solution)/shard_map/pallas_call | solution.py:44
  (17 shorter events, 0.1 us)
Async XLA Ops:
  0.6 2.6 %copy-start.1 = (bf16[1,384,768]{2,1,0:T(8,128)(2,1)S(1)}, bf16[1,384,768]{2,1,0:T(8,128)(2,1)}, u32[]{:S(2)}) copy-start(bf16[1,384,768]{2,1,0:T(8,128)(2,1)} %param.5) | copy-start | bytes 1769476
  0.6 2.6 %copy-start.2 = (bf16[384,384]{1,0:T(8,128)(2,1)S(1)}, bf16[384,384]{1,0:T(8,128)(2,1)}, u32[]{:S(2)}) copy-start(bf16[384,384]{1,0:T(8,128)(2,1)} %own_ref.1) | copy-start | bytes 884740
  0.6 2.5 %collective-permute-start = (bf16[384,768]{1,0:T(8,128)(2,1)}, bf16[384,768]{1,0:T(8,128)(2,1)S(1)}, u32[]{:S(2)}, u32[]{:S(2)}) collective-permute-start(bf16[384,768]{1,0:T(8,128)(2,1)} %bitcast.2), channel_id=1, source_target_pairs={{0,1},{1,0},{2,3},{3,2},{4,5},{5,4},{6,7},{7,6},{8,9},{9,8},{10,11... | collective-permute-start | bytes 1769480 | tf_op jit(solution)/shard_map/ppermute | solution.py:170
  0.7 4.4 %collective-permute-start.1 = (bf16[384,384]{1,0:T(8,128)(2,1)}, bf16[384,384]{1,0:T(8,128)(2,1)S(1)}, u32[]{:S(2)}, u32[]{:S(2)}) collective-permute-start(bf16[384,384]{1,0:T(8,128)(2,1)} %own_ref.1), channel_id=1, source_target_pairs={{0,1},{2,3},{4,5},{6,7},{8,9},{10,11},{12,13},{14,15},{16,17},{18,... | collective-permute-start | bytes 884744 | tf_op jit(solution)/shard_map/ppermute | solution.py:166
  5.2 14.3 %copy-start = (bf16[3,384,384]{2,1,0:T(8,128)(2,1)S(1)}, bf16[3,384,384]{2,1,0:T(8,128)(2,1)}, u32[]{:S(2)}) copy-start(bf16[3,384,384]{2,1,0:T(8,128)(2,1)} %refs_4_.1) | copy-start | bytes 2654212
  5.3 8.7 %copy-start.3 = (s32[3]{0:T(128)S(1)}, s32[3]{0:T(128)}, u32[]{:S(2)}) copy-start(s32[3]{0:T(128)} %offsets_ref.1) | copy-start | bytes 40
  5.3 8.7 %copy-start.4 = (f32[3]{0:T(128)S(1)}, f32[3]{0:T(128)}, u32[]{:S(2)}) copy-start(f32[3]{0:T(128)} %bose_ref.1) | copy-start | bytes 40
  5.3 8.2 %collective-permute-start.3 = (bf16[384,384]{1,0:T(8,128)(2,1)S(1)}, bf16[384,384]{1,0:T(8,128)(2,1)S(1)}, u32[]{:S(2)}, u32[]{:S(2)}) collective-permute-start(bf16[384,384]{1,0:T(8,128)(2,1)S(1)} %get-tuple-element.59.refs_0_), channel_id=1, source_target_pairs={{0,2},{1,5},{2,0},{3,7},{4,6},{5,1},{6,4},{7,3},{8,10},{9,13},{10,... | collective-permute-start | bytes 884744 | tf_op jit(solution)/shard_map/ppermute | solution.py:421
  6.9 9.6 %collective-permute-start.2 = (bf16[384,384]{1,0:T(8,128)(2,1)S(1)}, bf16[384,384]{1,0:T(8,128)(2,1)S(1)}, u32[]{:S(2)}, u32[]{:S(2)}) collective-permute-start(bf16[384,384]{1,0:T(8,128)(2,1)S(1)} %get-tuple-element.37.own_ref), channel_id=1, source_target_pairs={{0,8},{2,10},{4,12},{6,14},{8,0},{10,2},{12,4},{14,6},{16,24},{18,... | collective-permute-start | bytes 884744 | tf_op jit(solution)/shard_map/ppermute | solution.py:427
  7.3 12.2 %collective-permute-start.4 = (bf16[384,384]{1,0:T(8,128)(2,1)S(1)}, bf16[384,384]{1,0:T(8,128)(2,1)S(1)}, u32[]{:S(2)}, u32[]{:S(2)}) collective-permute-start(bf16[384,384]{1,0:T(8,128)(2,1)S(1)} %get-tuple-element.37.own_ref), channel_id=1, source_target_pairs={{8,16},{10,18},{12,20},{14,22},{16,8},{18,10},{20,12},{22,14},{9,1... | collective-permute-start | bytes 884744 | tf_op jit(solution)/shard_map/ppermute | solution.py:427
  11.9 7.6 %collective-permute-start.5 = (bf16[384,384]{1,0:T(8,128)(2,1)S(1)}, bf16[384,384]{1,0:T(8,128)(2,1)S(1)}, u32[]{:S(2)}, u32[]{:S(2)}) collective-permute-start(bf16[384,384]{1,0:T(8,128)(2,1)S(1)} %get-tuple-element.59.refs_0_), channel_id=1, source_target_pairs={{0,4},{1,3},{2,6},{3,1},{4,0},{5,7},{6,2},{7,5},{8,12},{9,11},{10,... | collective-permute-start | bytes 884744 | tf_op jit(solution)/shard_map/ppermute | solution.py:421
  13.5 8.4 %collective-permute-start.7 = (bf16[384,384]{1,0:T(8,128)(2,1)S(1)}, bf16[384,384]{1,0:T(8,128)(2,1)S(1)}, u32[]{:S(2)}, u32[]{:S(2)}) collective-permute-start(bf16[384,384]{1,0:T(8,128)(2,1)S(1)} %collective-permute-done.3.refs_0_.refs_1_), channel_id=1, source_target_pairs={{0,4},{1,3},{2,6},{3,1},{4,0},{5,7},{6,2},{7,5},{8,12},{9,11},{10,... | collective-permute-start | bytes 884744 | tf_op jit(solution)/shard_map/ppermute | solution.py:421
  16.5 4.6 %collective-permute-start.6 = (f32[1,384]{1,0:T(1,128)S(1)}, f32[1,384]{1,0:T(1,128)S(1)}, u32[]{:S(2)}, u32[]{:S(2)}) collective-permute-start(f32[1,384]{1,0:T(1,128)S(1)} %get-tuple-element.45), channel_id=1, source_target_pairs={{0,16},{2,18},{4,20},{6,22},{8,24},{10,26},{12,28},{14,30},{16,0},... | collective-permute-start | bytes 4616 | tf_op jit(solution)/shard_map/ppermute | solution.py:427
  22.1 8.0 %collective-permute-start.11 = (bf16[400,384]{1,0:T(8,128)(2,1)S(1)}, bf16[400,384]{1,0:T(8,128)(2,1)S(1)}, u32[]{:S(2)}, u32[]{:S(2)}) collective-permute-start(bf16[400,384]{1,0:T(8,128)(2,1)S(1)} %get-tuple-element.58), channel_id=1, source_target_pairs={{0,2},{1,5},{2,0},{3,7},{4,6},{5,1},{6,4},{7,3},{8,10},{9,13},{10,... | collective-permute-start | bytes 921608 | tf_op jit(solution)/shard_map/ppermute | solution.py:421
  22.7 13.5 %collective-permute-start.10 = (bf16[416,384]{1,0:T(8,128)(2,1)S(1)}, bf16[416,384]{1,0:T(8,128)(2,1)S(1)}, u32[]{:S(2)}, u32[]{:S(2)}) collective-permute-start(bf16[416,384]{1,0:T(8,128)(2,1)S(1)} %get-tuple-element.62), channel_id=1, source_target_pairs={{0,2},{1,5},{2,0},{3,7},{4,6},{5,1},{6,4},{7,3},{8,10},{9,13},{10,... | collective-permute-start | bytes 958472 | tf_op jit(solution)/shard_map/ppermute | solution.py:421
  25.7 8.6 %collective-permute-start.8 = (bf16[400,384]{1,0:T(8,128)(2,1)S(1)}, bf16[400,384]{1,0:T(8,128)(2,1)S(1)}, u32[]{:S(2)}, u32[]{:S(2)}) collective-permute-start(bf16[400,384]{1,0:T(8,128)(2,1)S(1)} %get-tuple-element.60), channel_id=1, source_target_pairs={{0,8},{2,10},{4,12},{6,14},{8,0},{10,2},{12,4},{14,6},{16,24},{18,... | collective-permute-start | bytes 921608 | tf_op jit(solution)/shard_map/ppermute | solution.py:427
  25.8 10.4 %collective-permute-start.9 = (bf16[400,384]{1,0:T(8,128)(2,1)S(1)}, bf16[400,384]{1,0:T(8,128)(2,1)S(1)}, u32[]{:S(2)}, u32[]{:S(2)}) collective-permute-start(bf16[400,384]{1,0:T(8,128)(2,1)S(1)} %get-tuple-element.61), channel_id=1, source_target_pairs={{8,16},{10,18},{12,20},{14,22},{16,8},{18,10},{20,12},{22,14},{9,1... | collective-permute-start | bytes 921608 | tf_op jit(solution)/shard_map/ppermute | solution.py:427
  30.2 6.9 %collective-permute-start.12 = (bf16[400,384]{1,0:T(8,128)(2,1)S(1)}, bf16[400,384]{1,0:T(8,128)(2,1)S(1)}, u32[]{:S(2)}, u32[]{:S(2)}) collective-permute-start(bf16[400,384]{1,0:T(8,128)(2,1)S(1)} %shard_map.79), channel_id=1, source_target_pairs={{0,4},{1,3},{2,6},{3,1},{4,0},{5,7},{6,2},{7,5},{8,12},{9,11},{10,... | collective-permute-start | bytes 921608 | tf_op jit(solution)/shard_map/ppermute | solution.py:421

commit v10 on v8

--- a/solution.py
+++ b/solution.py
@@ -504,7 +504,7 @@
     second_term = across_groups(second_out, second_pair)
     (real_total,) = call(group_terms, [wide], [*reals[1:], *modes], [bank(GROUP - 1)])
 
-    pieces = 4 if m % 64 == 0 else 1
+    pieces = 2 if m % 32 == 0 else 1
     sigma, cumulative = call(
         last_sum,
         [jax.ShapeDtypeStruct(g.shape, jnp.bfloat16), line],

time: 38.4 us -> 38.2 us (level)
  Pallas kernels: 9.65 us -> 8.8 us
  starting transfers between devices: 20.2 us -> 20.8 us
    pallas_call x13, Pallas kernels: 9.65 us -> 8.8 us  [call(): pl.pallas_call(kernel, out_shape=outs, in_specs=[SCALARS if i.ndim == 1 e...]
    ppermute x5, waiting for transfers between devices: 5.97 us -> 5.35 us  [across_groups(): lax.ppermute(value, 'energy', [(GROUP * a + i, GROUP * b + i) for a, b in...]
    ppermute x6, starting transfers between devices: 6.1 us -> 6.71 us  [hop(): return lax.ppermute(value, ('energy', 'slab'), pairs)]
  transfers between devices with their start and end apart: 13 -> 13, of which waited for: 6 -> 6; matrix products, arithmetic and copies ran while one was open for 0% -> 0% of each run, Pallas kernels for 22% -> 20%
where the time goes in v10:
time: 38.2 us; the launch traced here: 37.6 us
  starting transfers between devices  20.8 us (54%)
  Pallas kernels  8.8 us (23%)
  waiting for transfers between devices  7.17 us (19%)
  between operations  0.82 us (2%)
    ppermute x5, starting transfers between devices, across_groups(): lax.ppermute(value, 'energy', [(GROUP * a + i, GROUP * b + i) for a, b in...  11.6 us
    pallas_call x13, Pallas kernels, call(): pl.pallas_call(kernel, out_shape=outs, in_specs=[SCALARS if i.ndim == 1 e...  8.8 us
    ppermute x6, starting transfers between devices, hop(): return lax.ppermute(value, ('energy', 'slab'), pairs)  6.71 us
    ppermute x5, waiting for transfers between devices, across_groups(): lax.ppermute(value, 'energy', [(GROUP * a + i, GROUP * b + i) for a, b in...  5.35 us
    ppermute x1, starting transfers between devices, greens_halves(): below = lax.ppermute(coupling, 'slab', up)  2.41 us
    ppermute x6, waiting for transfers between devices, hop(): return lax.ppermute(value, ('energy', 'slab'), pairs)  1.82 us
  transfers between devices with their start and end apart: 13, of which 6 were waited for; matrix products, arithmetic and copies ran while one was open for 0% of the time, Pallas kernels for 20%

profile of v10, /device:TPU:10, one launch (start us, length us, event | category | flops | bytes accessed | tf_op | source)
XLA Modules:
  0.0 37.6 jit_solution(14540026756614589291)
XLA Ops:
  0.6 0.1 collective-permute-start
  0.7 2.4 %collective-permute-start.1 = (bf16[384,384]{1,0:T(8,128)(2,1)}, bf16[384,384]{1,0:T(8,128)(2,1)S(1)}, u32[]{:S(2)}, u32[]{:S(2)}) collective-permute-start(bf16[384,384]{1,0:T(8,128)(2,1)} %own_ref.1), channel_id=1, source_target_pairs={{0,1},{2,3},{4,5},{6,7},{8,9},{10,11},{12,13},{14,15},{16,17},{18,... | collective-permute-start | bytes 884744 | tf_op jit(solution)/shard_map/ppermute | solution.py:166
  3.2 2.0 %shard_map.69 = (bf16[384,384]{1,0:T(8,128)(2,1)S(1)}, bf16[384,384]{1,0:T(8,128)(2,1)S(1)}, f32[1,384]{1,0:T(1,128)S(1)}) custom-call(bf16[384,768]{1,0:T(8,128)(2,1)S(1)} %bitcast.3, bf16[384,768]{1,0:T(8,128)(2,1)S(1)} %collective-permute-done.other_ref, bf16[384,384]{1,0:T(8,128)(2,1)S(1)} %copy-done.2, f32[1,384]{1,0:T(1,128)S(1)} %shard_map.68.holes_ref), custom_call_target="tpu_custom_call" | custom-call | tf_op jit(solution)/shard_map/pallas_call | solution.py:44
  5.2 0.0 copy-start
  5.2 0.1 shard_map.70
  5.3 0.0 copy-start.3
  5.3 0.0 copy-start.4
  5.3 1.6 %collective-permute-start.3 = (bf16[384,384]{1,0:T(8,128)(2,1)S(1)}, bf16[384,384]{1,0:T(8,128)(2,1)S(1)}, u32[]{:S(2)}, u32[]{:S(2)}) collective-permute-start(bf16[384,384]{1,0:T(8,128)(2,1)S(1)} %get-tuple-element.59.refs_0_), channel_id=1, source_target_pairs={{0,4},{1,3},{2,6},{3,1},{4,0},{5,7},{6,2},{7,5},{8,12},{9,11},{10,... | collective-permute-start | bytes 884744 | tf_op jit(solution)/shard_map/ppermute | solution.py:421
  6.9 0.4 %collective-permute-start.2 = (bf16[384,384]{1,0:T(8,128)(2,1)S(1)}, bf16[384,384]{1,0:T(8,128)(2,1)S(1)}, u32[]{:S(2)}, u32[]{:S(2)}) collective-permute-start(bf16[384,384]{1,0:T(8,128)(2,1)S(1)} %get-tuple-element.37.own_ref), channel_id=1, source_target_pairs={{0,8},{2,10},{4,12},{6,14},{8,0},{10,2},{12,4},{14,6},{16,24},{18,... | collective-permute-start | bytes 884744 | tf_op jit(solution)/shard_map/ppermute | solution.py:427
  7.4 4.6 %collective-permute-start.4 = (bf16[384,384]{1,0:T(8,128)(2,1)S(1)}, bf16[384,384]{1,0:T(8,128)(2,1)S(1)}, u32[]{:S(2)}, u32[]{:S(2)}) collective-permute-start(bf16[384,384]{1,0:T(8,128)(2,1)S(1)} %get-tuple-element.37.own_ref), channel_id=1, source_target_pairs={{8,16},{10,18},{12,20},{14,22},{16,8},{18,10},{20,12},{22,14},{9,1... | collective-permute-start | bytes 884744 | tf_op jit(solution)/shard_map/ppermute | solution.py:427
  12.0 0.6 %collective-permute-start.5 = (bf16[384,384]{1,0:T(8,128)(2,1)S(1)}, bf16[384,384]{1,0:T(8,128)(2,1)S(1)}, u32[]{:S(2)}, u32[]{:S(2)}) collective-permute-start(bf16[384,384]{1,0:T(8,128)(2,1)S(1)} %get-tuple-element.59.refs_0_), channel_id=1, source_target_pairs={{0,2},{1,5},{2,0},{3,7},{4,6},{5,1},{6,4},{7,3},{8,10},{9,13},{10,... | collective-permute-start | bytes 884744 | tf_op jit(solution)/shard_map/ppermute | solution.py:421
  12.6 1.5 %collective-permute-start.7 = (bf16[384,384]{1,0:T(8,128)(2,1)S(1)}, bf16[384,384]{1,0:T(8,128)(2,1)S(1)}, u32[]{:S(2)}, u32[]{:S(2)}) collective-permute-start(bf16[384,384]{1,0:T(8,128)(2,1)S(1)} %collective-permute-done.3.refs_0_.refs_1_), channel_id=1, source_target_pairs={{0,2},{1,5},{2,0},{3,7},{4,6},{5,1},{6,4},{7,3},{8,10},{9,13},{10,... | collective-permute-start | bytes 884744 | tf_op jit(solution)/shard_map/ppermute | solution.py:421
  14.1 0.6 %shard_map.71 = (s32[8,128]{1,0:T(8,128)S(1)}, f32[8,128]{1,0:T(8,128)S(1)}) custom-call(s32[3]{0:T(128)S(1)} %copy-done.3, f32[3]{0:T(128)S(1)} %copy-done.4), custom_call_target="tpu_custom_call" | custom-call | tf_op jit(solution)/shard_map/pallas_call | solution.py:44
  14.6 1.5 %collective-permute-done.2.first_ref = bf16[384,384]{1,0:T(8,128)(2,1)S(1)} collective-permute-done((bf16[384,384]{1,0:T(8,128)(2,1)S(1)}, bf16[384,384]{1,0:T(8,128)(2,1)S(1)}, u32[]{:S(2)}, u32[]{:S(2)}) %collective-permute-start.2) | collective-permute-done | bytes 294944 | tf_op jit(solution)/shard_map/ppermute | solution.py:427
  16.2 2.7 %collective-permute-start.6 = (f32[1,384]{1,0:T(1,128)S(1)}, f32[1,384]{1,0:T(1,128)S(1)}, u32[]{:S(2)}, u32[]{:S(2)}) collective-permute-start(f32[1,384]{1,0:T(1,128)S(1)} %get-tuple-element.45), channel_id=1, source_target_pairs={{0,16},{2,18},{4,20},{6,22},{8,24},{10,26},{12,28},{14,30},{16,0},... | collective-permute-start | bytes 4616 | tf_op jit(solution)/shard_map/ppermute | solution.py:427
  18.8 0.3 collective-permute-done.4.second_ref
  19.2 1.5 %shard_map.73 = (bf16[400,384]{1,0:T(8,128)(2,1)S(1)}, bf16[416,384]{1,0:T(8,128)(2,1)S(1)}, bf16[400,384]{1,0:T(8,128)(2,1)S(1)}) custom-call(bf16[384,384]{1,0:T(8,128)(2,1)S(1)} %get-tuple-element.37.own_ref, bf16[384,384]{1,0:T(8,128)(2,1)S(1)} %collective-permute-done.2.first_ref, bf16[384,384]{1,0:T(8,128)(2,1)S(1)} %collective-permute-done.4.second_ref, ...), custom_call_target="tpu_custom_call" | custom-call | tf_op jit(solution)/shard_map/pallas_call | solution.py:44
  20.7 1.2 %collective-permute-done.7.refs_2_.refs_3_ = bf16[384,384]{1,0:T(8,128)(2,1)S(1)} collective-permute-done((bf16[384,384]{1,0:T(8,128)(2,1)S(1)}, bf16[384,384]{1,0:T(8,128)(2,1)S(1)}, u32[]{:S(2)}, u32[]{:S(2)}) %collective-permute-start.7) | collective-permute-done | bytes 294944 | tf_op jit(solution)/shard_map/ppermute | solution.py:421
  21.9 0.2 shard_map.77
  22.1 0.6 %collective-permute-start.11 = (bf16[400,384]{1,0:T(8,128)(2,1)S(1)}, bf16[400,384]{1,0:T(8,128)(2,1)S(1)}, u32[]{:S(2)}, u32[]{:S(2)}) collective-permute-start(bf16[400,384]{1,0:T(8,128)(2,1)S(1)} %get-tuple-element.58), channel_id=1, source_target_pairs={{0,4},{1,3},{2,6},{3,1},{4,0},{5,7},{6,2},{7,5},{8,12},{9,11},{10,... | collective-permute-start | bytes 921608 | tf_op jit(solution)/shard_map/ppermute | solution.py:421
  22.7 1.5 %collective-permute-start.10 = (bf16[416,384]{1,0:T(8,128)(2,1)S(1)}, bf16[416,384]{1,0:T(8,128)(2,1)S(1)}, u32[]{:S(2)}, u32[]{:S(2)}) collective-permute-start(bf16[416,384]{1,0:T(8,128)(2,1)S(1)} %get-tuple-element.62), channel_id=1, source_target_pairs={{0,4},{1,3},{2,6},{3,1},{4,0},{5,7},{6,2},{7,5},{8,12},{9,11},{10,... | collective-permute-start | bytes 958472 | tf_op jit(solution)/shard_map/ppermute | solution.py:421
  24.2 1.5 %shard_map.78 = (bf16[400,384]{1,0:T(8,128)(2,1)S(1)}, bf16[400,384]{1,0:T(8,128)(2,1)S(1)}) custom-call(bf16[384,384]{1,0:T(8,128)(2,1)S(1)} %get-tuple-element.59.refs_0_, bf16[384,384]{1,0:T(8,128)(2,1)S(1)} %collective-permute-done.3.refs_0_.refs_1_, bf16[384,384]{1,0:T(8,128)(2,1)S(1)} %collective-permute-done.5.refs_1_.refs_2_, ...), custom_call_target="tpu_custom_call" | custom-call | tf_op jit(solution)/shard_map/pallas_call | solution.py:44
  25.7 0.1 collective-permute-start.8
  25.8 3.9 %collective-permute-start.9 = (bf16[400,384]{1,0:T(8,128)(2,1)S(1)}, bf16[400,384]{1,0:T(8,128)(2,1)S(1)}, u32[]{:S(2)}, u32[]{:S(2)}) collective-permute-start(bf16[400,384]{1,0:T(8,128)(2,1)S(1)} %get-tuple-element.61), channel_id=1, source_target_pairs={{8,16},{10,18},{12,20},{14,22},{16,8},{18,10},{20,12},{22,14},{9,1... | collective-permute-start | bytes 921608 | tf_op jit(solution)/shard_map/ppermute | solution.py:427
  29.7 0.1 shard_map.79
  29.8 0.9 %collective-permute-start.12 = (bf16[400,384]{1,0:T(8,128)(2,1)S(1)}, bf16[400,384]{1,0:T(8,128)(2,1)S(1)}, u32[]{:S(2)}, u32[]{:S(2)}) collective-permute-start(bf16[400,384]{1,0:T(8,128)(2,1)S(1)} %shard_map.79), channel_id=1, source_target_pairs={{0,2},{1,5},{2,0},{3,7},{4,6},{5,1},{6,4},{7,3},{8,10},{9,13},{10,... | collective-permute-start | bytes 921608 | tf_op jit(solution)/shard_map/ppermute | solution.py:421
  30.7 0.7 %shard_map.75.refs_1_ = f32[384,384]{1,0:T(8,128)S(1)} custom-call(bf16[384,384]{1,0:T(8,128)(2,1)S(1)} %collective-permute-done.2.first_ref, bf16[384,384]{1,0:T(8,128)(2,1)S(1)} %collective-permute-done.4.second_ref, bf16[3,384,384]{2,1,0:T(8,128)(2,1)S(1)} %copy-done, s32[8,128]{1,0:T(8,128)S(1)} %get-tuple-element.47.places_ref.refs_4_.refs_5_, ...), custom_call_target="tpu_custom_call" | custom-call | tf_op jit(solution)/shard_map/pallas_call | solution.py:44
  31.4 1.1 %shard_map.74.refs_0_ = f32[384,384]{1,0:T(8,128)S(1)} custom-call(bf16[384,384]{1,0:T(8,128)(2,1)S(1)} %collective-permute-done.3.refs_0_.refs_1_, bf16[384,384]{1,0:T(8,128)(2,1)S(1)} %collective-permute-done.5.refs_1_.refs_2_, bf16[384,384]{1,0:T(8,128)(2,1)S(1)} %collective-permute-done.7.refs_2_.refs_3_, bf16[3,384,384]{2,1,0:T(8,128)(2,1)S(1)} %copy-done, ...), custom_call_target="tpu_custom_call" | custom-call | tf_op jit(solution)/shard_map/pallas_call | solution.py:44
  32.5 0.8 %collective-permute-done.8.refs_2_ = bf16[400,384]{1,0:T(8,128)(2,1)S(1)} collective-permute-done((bf16[400,384]{1,0:T(8,128)(2,1)S(1)}, bf16[400,384]{1,0:T(8,128)(2,1)S(1)}, u32[]{:S(2)}, u32[]{:S(2)}) %collective-permute-start.8) | collective-permute-done | bytes 307232 | tf_op jit(solution)/shard_map/ppermute | solution.py:427
  33.3 2.7 %collective-permute-done.9.refs_3_ = bf16[400,384]{1,0:T(8,128)(2,1)S(1)} collective-permute-done((bf16[400,384]{1,0:T(8,128)(2,1)S(1)}, bf16[400,384]{1,0:T(8,128)(2,1)S(1)}, u32[]{:S(2)}, u32[]{:S(2)}) %collective-permute-start.9) | collective-permute-done | bytes 307232 | tf_op jit(solution)/shard_map/ppermute | solution.py:427
  36.1 0.6 %collective-permute-done.12.refs_7_ = bf16[400,384]{1,0:T(8,128)(2,1)S(1)} collective-permute-done((bf16[400,384]{1,0:T(8,128)(2,1)S(1)}, bf16[400,384]{1,0:T(8,128)(2,1)S(1)}, u32[]{:S(2)}, u32[]{:S(2)}) %collective-permute-start.12) | collective-permute-done | bytes 307232 | tf_op jit(solution)/shard_map/ppermute | solution.py:421
  36.7 0.9 %shard_map.80 = (bf16[384,768]{1,0:T(8,128)(2,1)}, f32[1,384]{1,0:T(1,128)}) custom-call(f32[384,384]{1,0:T(8,128)S(1)} %shard_map.74.refs_0_, f32[384,384]{1,0:T(8,128)S(1)} %shard_map.75.refs_1_, bf16[400,384]{1,0:T(8,128)(2,1)S(1)} %collective-permute-done.8.refs_2_, bf16[400,384]{1,0:T(8,128)(2,1)S(1)} %collective-permute-done.9.refs_3_, ...), custom_call_target="tpu_custom_call" | custom-call | tf_op jit(solution)/shard_map/pallas_call | solution.py:44
  (17 shorter events, 0.1 us)
Async XLA Ops:
  0.6 2.6 %copy-start.1 = (bf16[1,384,768]{2,1,0:T(8,128)(2,1)S(1)}, bf16[1,384,768]{2,1,0:T(8,128)(2,1)}, u32[]{:S(2)}) copy-start(bf16[1,384,768]{2,1,0:T(8,128)(2,1)} %param.5) | copy-start | bytes 1769476
  0.6 2.6 %copy-start.2 = (bf16[384,384]{1,0:T(8,128)(2,1)S(1)}, bf16[384,384]{1,0:T(8,128)(2,1)}, u32[]{:S(2)}) copy-start(bf16[384,384]{1,0:T(8,128)(2,1)} %own_ref.1) | copy-start | bytes 884740
  0.6 2.5 %collective-permute-start = (bf16[384,768]{1,0:T(8,128)(2,1)}, bf16[384,768]{1,0:T(8,128)(2,1)S(1)}, u32[]{:S(2)}, u32[]{:S(2)}) collective-permute-start(bf16[384,768]{1,0:T(8,128)(2,1)} %bitcast.2), channel_id=1, source_target_pairs={{0,1},{1,0},{2,3},{3,2},{4,5},{5,4},{6,7},{7,6},{8,9},{9,8},{10,11... | collective-permute-start | bytes 1769480 | tf_op jit(solution)/shard_map/ppermute | solution.py:170
  0.7 4.4 %collective-permute-start.1 = (bf16[384,384]{1,0:T(8,128)(2,1)}, bf16[384,384]{1,0:T(8,128)(2,1)S(1)}, u32[]{:S(2)}, u32[]{:S(2)}) collective-permute-start(bf16[384,384]{1,0:T(8,128)(2,1)} %own_ref.1), channel_id=1, source_target_pairs={{0,1},{2,3},{4,5},{6,7},{8,9},{10,11},{12,13},{14,15},{16,17},{18,... | collective-permute-start | bytes 884744 | tf_op jit(solution)/shard_map/ppermute | solution.py:166
  5.2 14.0 %copy-start = (bf16[3,384,384]{2,1,0:T(8,128)(2,1)S(1)}, bf16[3,384,384]{2,1,0:T(8,128)(2,1)}, u32[]{:S(2)}) copy-start(bf16[3,384,384]{2,1,0:T(8,128)(2,1)} %refs_4_.1) | copy-start | bytes 2654212
  5.3 8.8 %copy-start.3 = (s32[3]{0:T(128)S(1)}, s32[3]{0:T(128)}, u32[]{:S(2)}) copy-start(s32[3]{0:T(128)} %offsets_ref.1) | copy-start | bytes 40
  5.3 8.8 %copy-start.4 = (f32[3]{0:T(128)S(1)}, f32[3]{0:T(128)}, u32[]{:S(2)}) copy-start(f32[3]{0:T(128)} %bose_ref.1) | copy-start | bytes 40
  5.3 7.2 %collective-permute-start.3 = (bf16[384,384]{1,0:T(8,128)(2,1)S(1)}, bf16[384,384]{1,0:T(8,128)(2,1)S(1)}, u32[]{:S(2)}, u32[]{:S(2)}) collective-permute-start(bf16[384,384]{1,0:T(8,128)(2,1)S(1)} %get-tuple-element.59.refs_0_), channel_id=1, source_target_pairs={{0,4},{1,3},{2,6},{3,1},{4,0},{5,7},{6,2},{7,5},{8,12},{9,11},{10,... | collective-permute-start | bytes 884744 | tf_op jit(solution)/shard_map/ppermute | solution.py:421
  6.9 9.2 %collective-permute-start.2 = (bf16[384,384]{1,0:T(8,128)(2,1)S(1)}, bf16[384,384]{1,0:T(8,128)(2,1)S(1)}, u32[]{:S(2)}, u32[]{:S(2)}) collective-permute-start(bf16[384,384]{1,0:T(8,128)(2,1)S(1)} %get-tuple-element.37.own_ref), channel_id=1, source_target_pairs={{0,8},{2,10},{4,12},{6,14},{8,0},{10,2},{12,4},{14,6},{16,24},{18,... | collective-permute-start | bytes 884744 | tf_op jit(solution)/shard_map/ppermute | solution.py:427
  7.4 11.8 %collective-permute-start.4 = (bf16[384,384]{1,0:T(8,128)(2,1)S(1)}, bf16[384,384]{1,0:T(8,128)(2,1)S(1)}, u32[]{:S(2)}, u32[]{:S(2)}) collective-permute-start(bf16[384,384]{1,0:T(8,128)(2,1)S(1)} %get-tuple-element.37.own_ref), channel_id=1, source_target_pairs={{8,16},{10,18},{12,20},{14,22},{16,8},{18,10},{20,12},{22,14},{9,1... | collective-permute-start | bytes 884744 | tf_op jit(solution)/shard_map/ppermute | solution.py:427
  12.0 7.2 %collective-permute-start.5 = (bf16[384,384]{1,0:T(8,128)(2,1)S(1)}, bf16[384,384]{1,0:T(8,128)(2,1)S(1)}, u32[]{:S(2)}, u32[]{:S(2)}) collective-permute-start(bf16[384,384]{1,0:T(8,128)(2,1)S(1)} %get-tuple-element.59.refs_0_), channel_id=1, source_target_pairs={{0,2},{1,5},{2,0},{3,7},{4,6},{5,1},{6,4},{7,3},{8,10},{9,13},{10,... | collective-permute-start | bytes 884744 | tf_op jit(solution)/shard_map/ppermute | solution.py:421
  12.6 9.3 %collective-permute-start.7 = (bf16[384,384]{1,0:T(8,128)(2,1)S(1)}, bf16[384,384]{1,0:T(8,128)(2,1)S(1)}, u32[]{:S(2)}, u32[]{:S(2)}) collective-permute-start(bf16[384,384]{1,0:T(8,128)(2,1)S(1)} %collective-permute-done.3.refs_0_.refs_1_), channel_id=1, source_target_pairs={{0,2},{1,5},{2,0},{3,7},{4,6},{5,1},{6,4},{7,3},{8,10},{9,13},{10,... | collective-permute-start | bytes 884744 | tf_op jit(solution)/shard_map/ppermute | solution.py:421
  16.2 4.6 %collective-permute-start.6 = (f32[1,384]{1,0:T(1,128)S(1)}, f32[1,384]{1,0:T(1,128)S(1)}, u32[]{:S(2)}, u32[]{:S(2)}) collective-permute-start(f32[1,384]{1,0:T(1,128)S(1)} %get-tuple-element.45), channel_id=1, source_target_pairs={{0,16},{2,18},{4,20},{6,22},{8,24},{10,26},{12,28},{14,30},{16,0},... | collective-permute-start | bytes 4616 | tf_op jit(solution)/shard_map/ppermute | solution.py:427
  22.1 7.6 %collective-permute-start.11 = (bf16[400,384]{1,0:T(8,128)(2,1)S(1)}, bf16[400,384]{1,0:T(8,128)(2,1)S(1)}, u32[]{:S(2)}, u32[]{:S(2)}) collective-permute-start(bf16[400,384]{1,0:T(8,128)(2,1)S(1)} %get-tuple-element.58), channel_id=1, source_target_pairs={{0,4},{1,3},{2,6},{3,1},{4,0},{5,7},{6,2},{7,5},{8,12},{9,11},{10,... | collective-permute-start | bytes 921608 | tf_op jit(solution)/shard_map/ppermute | solution.py:421
  22.7 13.4 %collective-permute-start.10 = (bf16[416,384]{1,0:T(8,128)(2,1)S(1)}, bf16[416,384]{1,0:T(8,128)(2,1)S(1)}, u32[]{:S(2)}, u32[]{:S(2)}) collective-permute-start(bf16[416,384]{1,0:T(8,128)(2,1)S(1)} %get-tuple-element.62), channel_id=1, source_target_pairs={{0,4},{1,3},{2,6},{3,1},{4,0},{5,7},{6,2},{7,5},{8,12},{9,11},{10,... | collective-permute-start | bytes 958472 | tf_op jit(solution)/shard_map/ppermute | solution.py:421
  25.7 7.6 %collective-permute-start.8 = (bf16[400,384]{1,0:T(8,128)(2,1)S(1)}, bf16[400,384]{1,0:T(8,128)(2,1)S(1)}, u32[]{:S(2)}, u32[]{:S(2)}) collective-permute-start(bf16[400,384]{1,0:T(8,128)(2,1)S(1)} %get-tuple-element.60), channel_id=1, source_target_pairs={{0,8},{2,10},{4,12},{6,14},{8,0},{10,2},{12,4},{14,6},{16,24},{18,... | collective-permute-start | bytes 921608 | tf_op jit(solution)/shard_map/ppermute | solution.py:427
  25.8 10.3 %collective-permute-start.9 = (bf16[400,384]{1,0:T(8,128)(2,1)S(1)}, bf16[400,384]{1,0:T(8,128)(2,1)S(1)}, u32[]{:S(2)}, u32[]{:S(2)}) collective-permute-start(bf16[400,384]{1,0:T(8,128)(2,1)S(1)} %get-tuple-element.61), channel_id=1, source_target_pairs={{8,16},{10,18},{12,20},{14,22},{16,8},{18,10},{20,12},{22,14},{9,1... | collective-permute-start | bytes 921608 | tf_op jit(solution)/shard_map/ppermute | solution.py:427
  29.8 6.9 %collective-permute-start.12 = (bf16[400,384]{1,0:T(8,128)(2,1)S(1)}, bf16[400,384]{1,0:T(8,128)(2,1)S(1)}, u32[]{:S(2)}, u32[]{:S(2)}) collective-permute-start(bf16[400,384]{1,0:T(8,128)(2,1)S(1)} %shard_map.79), channel_id=1, source_target_pairs={{0,2},{1,5},{2,0},{3,7},{4,6},{5,1},{6,4},{7,3},{8,10},{9,13},{10,... | collective-permute-start | bytes 921608 | tf_op jit(solution)/shard_map/ppermute | solution.py:421
